TPU v7x, 512 devices: a whole 4x4x16 slice. The times are simulated.
512 devices in a mesh: group: 64 (over z, y_lo, core), mp: 8 (over x, y_hi).
Axes of the slice: x: 4, y: 4 (y_hi: 2, y_lo: 2; y = y_hi * 2 + y_lo), z: 16, core: 2. Of those that a mesh axis runs over, the one named last changes fastest.
Arguments:
- tokens: bfloat16 [3, 4096, 4096], P(None, 'group'), may hold values from -600 to 600
- neighbour_ids: int32 [64, 3, 128], P('group'), may hold values from 0 to 65535, as said below
- group_document: int32 [3, 64], replicated, may hold values from 0 to 15, never falling along the last dimension, each value on 1 to 8 neighbouring positions
- embed_table: bfloat16 [65536, 4096], P('group', 'mp'), may hold values from -6 to 6
- w_query: bfloat16 [4096, 2048], P('group', 'mp'), may hold values from -0.09375 to 0.09375
- w_key: bfloat16 [4096, 2048], P('group', 'mp'), may hold values from -0.09375 to 0.09375
- w_value: bfloat16 [4096, 2048], P('group', 'mp'), may hold values from -0.375 to 0.375
- attended_grad: bfloat16 [3, 4096, 2048], P(None, 'group', 'mp'), may hold values from -6 to 6
Outputs:
- attended: bfloat16 [3, 4096, 2048], P(None, 'group', 'mp')
- token_grad: bfloat16 [3, 4096, 4096], P(None, 'group')
Inputs may be any that keep to these rules, and one draw needn't show every extreme that they name: `neighbour_ids`: among the ids of one group, all sequences together, at most 9 fall in any one block of 1024 consecutive ids starting at a multiple of 1024; in every draw one block holds exactly 9 ids of every group. `group_document`: never falls along a sequence; a document covers 1 to 8 groups.
All inputs are finite; a program needn't handle non-finite values.
Results may differ from a plain program's by a relative error of at most 0.0065.
The roundings to bfloat16 on the way count: a program that leaves them out, or rounds other values in their place, can miss the bound.
Values may be sent and summed in bfloat16 or wider, within the bound.
No kernel may reach another device: no remote copies, remote signals or barrier semaphores. Data moves between devices by JAX's collectives and lax.ppermute only.
A program may use at most 128 MiB of HBM per device.

v0:
```python
import jax
import jax.numpy as jnp
from jax import lax
from jax.sharding import PartitionSpec as P

HEAD_DIM = 128


def shifted(value, axis, steps):
    count = lax.axis_size(axis)
    leading, last = (max(0, -steps), min(count, count - steps))
    return lax.ppermute(value, axis, [(source, source + steps) for source in range(leading, last)])


def local(
    tokens, neighbour_ids, group_document, embed_table, w_query, w_key, w_value, attended_grad
):
    nchunk = lax.axis_size("group")
    group_here = lax.axis_index("group")
    seq_count, group_len, model_width = tokens.shape
    head_cols = w_query.shape[1]
    local_heads = head_cols // HEAD_DIM
    score_scale = HEAD_DIM ** (-0.5)
    query_w, key_w, value_w = (
        lax.all_gather(w_query, "group", axis=0, tiled=True),
        lax.all_gather(w_key, "group", axis=0, tiled=True),
        lax.all_gather(w_value, "group", axis=0, tiled=True),
    )
    flat_ids = neighbour_ids.reshape(-1)
    id_count = flat_ids.shape[0]
    key_count = id_count // seq_count
    rows_dev = embed_table.shape[0]
    capacity = max(2, 3 * id_count // (2 * nchunk))
    owner_group = flat_ids // rows_dev
    onehot = (owner_group[:, None] == jnp.arange(nchunk, dtype=jnp.int32)[None, :]).astype(
        jnp.int32
    )
    before = jnp.cumsum(onehot, axis=0) - onehot
    bucket_rank = jnp.sum(before * onehot, axis=1)
    slot_index = owner_group * capacity + bucket_rank
    requests = (
        jnp.zeros((nchunk * capacity,), jnp.int32)
        .at[slot_index]
        .set(flat_ids - owner_group * rows_dev)
    )
    requests = requests.reshape(nchunk, capacity)
    found_rows = embed_table[
        lax.all_to_all(requests, "group", split_axis=0, concat_axis=0, tiled=True)
    ]
    returned = lax.all_to_all(found_rows, "group", split_axis=0, concat_axis=0, tiled=True)
    encoded = returned.reshape(nchunk * capacity, returned.shape[2])[slot_index]
    block_cols = lax.all_gather(encoded, "mp", axis=1, tiled=True)
    key_acc = jnp.dot(block_cols, key_w, preferred_element_type=jnp.float32)
    value_acc = jnp.dot(block_cols, value_w, preferred_element_type=jnp.float32)
    key_own = key_acc.astype(jnp.bfloat16).reshape(seq_count, key_count, local_heads, HEAD_DIM)
    value_own = value_acc.astype(jnp.bfloat16).reshape(seq_count, key_count, local_heads, HEAD_DIM)
    key_prev, value_prev = shifted((key_own, value_own), "group", 1)
    query_act = jnp.dot(
        tokens.reshape(-1, model_width), query_w, preferred_element_type=jnp.float32
    )
    query_act = query_act.astype(jnp.bfloat16).reshape(seq_count, group_len, local_heads, HEAD_DIM)
    last_flat = jnp.arange(group_len) == group_len - 1
    earlier = jnp.maximum(group_here - 1, 0)
    doc_here = lax.dynamic_slice_in_dim(group_document, group_here, 1, 1)[:, 0]
    doc_before = lax.dynamic_slice_in_dim(group_document, earlier, 1, 1)[:, 0]
    same_doc = (group_here >= 1) & (doc_here == doc_before)
    valid_tok = (last_flat[None, :] | same_doc[:, None])[:, :, None, None]
    last_token = last_flat[:, None]
    score_prev = (
        jnp.einsum("slhd,skhd->shlk", query_act, key_prev, preferred_element_type=jnp.float32)
        * score_scale
    )
    score_own = (
        jnp.einsum("slhd,skhd->shlk", query_act, key_own, preferred_element_type=jnp.float32)
        * score_scale
    )
    scores = jnp.where(last_token, score_own, score_prev)
    row_max = jnp.max(scores, axis=-1, keepdims=True)
    exp_scores = jnp.exp(scores - row_max)
    attn_prob = exp_scores / jnp.sum(exp_scores, axis=-1, keepdims=True)
    prob_bf = attn_prob.astype(jnp.bfloat16)
    zero_bf = jnp.zeros_like(prob_bf)
    prob_prev = jnp.where(last_token, zero_bf, prob_bf)
    prob_own = jnp.where(last_token, prob_bf, zero_bf)
    mixed_sum = jnp.einsum(
        "shlk,skhd->slhd", prob_prev, value_prev, preferred_element_type=jnp.float32
    )
    mixed_sum = mixed_sum + jnp.einsum(
        "shlk,skhd->slhd", prob_own, value_own, preferred_element_type=jnp.float32
    )
    attended = (
        jnp.where(valid_tok, mixed_sum, 0.0)
        .astype(jnp.bfloat16)
        .reshape(seq_count, group_len, head_cols)
    )
    grad_in = attended_grad.reshape(seq_count, group_len, local_heads, HEAD_DIM)
    grad_kept = jnp.where(valid_tok, grad_in, jnp.zeros_like(grad_in))
    grad_prev = jnp.einsum(
        "slhd,skhd->shlk", grad_kept, value_prev, preferred_element_type=jnp.float32
    )
    grad_own = jnp.einsum(
        "slhd,skhd->shlk", grad_kept, value_own, preferred_element_type=jnp.float32
    )
    prob_grad = jnp.where(last_token, grad_own, grad_prev)
    dscore = (
        attn_prob
        * (prob_grad - jnp.sum(attn_prob * prob_grad, axis=-1, keepdims=True))
        * score_scale
    )
    dscore = dscore.astype(jnp.bfloat16)
    zero_ds = jnp.zeros_like(dscore)
    dscore_prev = jnp.where(last_token, zero_ds, dscore)
    dscore_own = jnp.where(last_token, dscore, zero_ds)
    dquery = jnp.einsum(
        "shlk,skhd->slhd", dscore_prev, key_prev, preferred_element_type=jnp.float32
    )
    dquery = dquery + jnp.einsum(
        "shlk,skhd->slhd", dscore_own, key_own, preferred_element_type=jnp.float32
    )
    dquery = dquery.astype(jnp.bfloat16).reshape(-1, head_cols)
    partial_value = lax.dot_general(
        dquery, query_w, (((1,), (1,)), ((), ())), preferred_element_type=jnp.float32
    )
    token_grad = lax.psum(partial_value, "mp").astype(jnp.bfloat16)
    return (attended, token_grad.reshape(seq_count, group_len, model_width))


def solution(mesh):
    in_specs = (
        P(None, "group", None),
        P("group", None, None),
        P(),
        P("group", "mp"),
        P("group", "mp"),
        P("group", "mp"),
        P("group", "mp"),
        P(None, "group", "mp"),
    )
    out_specs = (P(None, "group", "mp"), P(None, "group", None))
    return jax.shard_map(local, mesh=mesh, in_specs=in_specs, out_specs=out_specs, check_vma=False)
```

profile of v0, /device:TPU:24, one launch (start us, length us, event | category | flops | bytes accessed | tf_op | source)
XLA Modules:
  0.0 635.2 jit_solution(15965642953757153576)
XLA Ops:
  10.1 0.9 reduce-window.6
  12.1 2.9 scatter_custom_fusion
  15.1 29.4 %all_to_all.17 = s32[64,1,9]{2,1,0:T(1,128)S(1)} all-to-all(s32[64,1,9]{2,1,0:T(1,128)S(1)} %bitcast.112), channel_id=1, replica_groups=mesh['group'=64,'mp'=8] {'group'}, dimensions={0} | all-to-all | bytes 4608 | tf_op jit(solution)/shard_map/all_to_all | solution.py:48
  44.7 4.1 gather_fusion
  48.9 1.2 reshape.238
  50.1 5.4 all-to-all-start.1
  55.6 59.7 %all-to-all-done.1 = bf16[64,9,512]{2,1,0:T(8,128)(2,1)S(1)} async-done(((bf16[64,9,512]{2,1,0:T(8,128)(2,1)}), bf16[64,9,512]{2,1,0:T(8,128)(2,1)S(1)}, u32[]{:S(2)}, u32[]{:S(2)}) %all-to-all-start.1) | async-done | bytes 589856 | tf_op jit(solution)/shard_map/all_to_all | solution.py:50
  115.5 2.6 gather_fusion.1
  119.0 32.4 %all-gather.8.cloned.1.call-done = bf16[4096,256]{1,0:T(8,128)(2,1)} async-done(((bf16[64,256]{1,0:T(8,128)(2,1)}), bf16[4096,256]{1,0:T(8,128)(2,1)}) %all-gather.8.cloned.1.call-update) | async-done | bytes 2097168 | tf_op jit(solution)/shard_map/all_gather | solution.py:25
  151.4 2.2 convolution_convert_fusion.2
  153.6 117.8 %all-gather.6.cloned.1.call-done = bf16[4096,256]{1,0:T(8,128)(2,1)} async-done(((bf16[64,256]{1,0:T(8,128)(2,1)}), bf16[4096,256]{1,0:T(8,128)(2,1)}) %all-gather.6.cloned.1.call-update) | async-done | bytes 2097168 | tf_op jit(solution)/shard_map/all_gather | solution.py:27
  271.4 81.7 %all-gather.12.cloned.1.call-done = bf16[384,4096]{1,0:T(8,128)(2,1)} async-done(((bf16[384,512]{1,0:T(8,128)(2,1)}), bf16[384,4096]{1,0:T(8,128)(2,1)}) %all-gather.12.cloned.1.call-update) | async-done | bytes 3145744 | tf_op jit(solution)/shard_map/all_gather | solution.py:52
  353.1 3.5 convolution_convert_fusion.1
  356.8 2.1 collective-permute-start
  358.8 118.7 %all-gather.10.cloned.1.call-done = bf16[4096,256]{1,0:T(8,128)(2,1)} async-done(((bf16[64,256]{1,0:T(8,128)(2,1)}), bf16[4096,256]{1,0:T(8,128)(2,1)}) %all-gather.10.cloned.1.call-update) | async-done | bytes 2097168 | tf_op jit(solution)/shard_map/all_gather | solution.py:26
  477.5 3.5 convolution_convert_fusion
  481.1 2.1 collective-permute-start.1
  483.8 4.3 collective-permute-done.1
  488.3 1.1 fusion.76
  490.4 1.8 fusion.21
  492.2 1.7 fusion.13
  494.0 4.1 fusion.15
  498.1 129.1 %all-reduce.1 = bf16[192,4096]{1,0:T(8,128)(2,1)} all-reduce(f32[192,4096]{1,0:T(8,128)} %fusion.15), channel_id=1, replica_groups=mesh['group'=64,'mp'=8] {'mp'}, use_global_device_ids=true, to_apply=%region_7.8 | all-reduce | flops 786432 | bytes 4718592 | tf_op jit(solution)/shard_map/psum | solution.py:124
  627.2 0.8 fusion.12
  (44 shorter events, 8.0 us)
Async XLA Ops:
  7.2 144.3 %copy-start = (bf16[3,64,4096]{2,1,0:T(8,128)(2,1)S(1)}, bf16[3,64,4096]{2,1,0:T(8,128)(2,1)}, u32[]{:S(2)}) copy-start(bf16[3,64,4096]{2,1,0:T(8,128)(2,1)} %param.8) | copy-start | bytes 4718596
  7.2 144.2 %all-gather.8.cloned.1.call-start = ((), (), s32[]{:S(2)}) async-start(), calls=%async_computation.3 | async-start | bytes 2129920 | tf_op jit(solution)/shard_map/all_gather | solution.py:25
  7.9 263.5 %all-gather.6.cloned.1.call-start = ((), (), s32[]{:S(2)}) async-start(), calls=%async_computation.2 | async-start | bytes 2129920 | tf_op jit(solution)/shard_map/all_gather | solution.py:27
  50.1 65.2 %all-to-all-start.1 = ((bf16[64,9,512]{2,1,0:T(8,128)(2,1)}), bf16[64,9,512]{2,1,0:T(8,128)(2,1)S(1)}, u32[]{:S(2)}, u32[]{:S(2)}) async-start(bf16[64,9,512]{2,1,0:T(8,128)(2,1)} %reshape.238), calls=%async_computation.1 | async-start | bytes 2097152 | tf_op jit(solution)/shard_map/all_to_all | solution.py:50
  55.5 297.6 %all-gather.12.cloned.1.call-start = ((), (), s32[]{:S(2)}) async-start(), calls=%async_computation.5 | async-start | bytes 3538944 | tf_op jit(solution)/shard_map/all_gather | solution.py:52
  115.5 3.2 copy-start.2
  118.1 359.4 %all-gather.10.cloned.1.call-start = ((), (), s32[]{:S(2)}) async-start(), calls=%async_computation.4 | async-start | bytes 2129920 | tf_op jit(solution)/shard_map/all_gather | solution.py:26
  356.7 126.5 %copy-start.1 = (bf16[3,64,256]{2,1,0:T(8,128)(2,1)S(1)}, bf16[3,64,256]{2,1,0:T(8,128)(2,1)}, u32[]{:S(2)}) copy-start(bf16[3,64,256]{2,1,0:T(8,128)(2,1)} %param.15) | copy-start | bytes 294916
  356.8 133.4 %collective-permute-start = (bf16[3,128,2,128]{3,1,2,0:T(8,128)(2,1)S(1)}, bf16[3,128,2,128]{3,1,2,0:T(8,128)(2,1)S(1)}, u32[]{:S(2)}, u32[]{:S(2)}) collective-permute-start(bf16[3,128,2,128]{3,1,2,0:T(8,128)(2,1)S(1)} %copy.33), channel_id=1, source_target_pairs={{0,8},{8,16},{16,24},{24,32},{32,40},{40,48},{48,56},{56,64},{64,7... | collective-permute-start | bytes 589832 | tf_op jit(solution)/shard_map/ppermute | solution.py:12
  481.1 7.0 %collective-permute-start.1 = (bf16[3,128,2,128]{3,1,2,0:T(8,128)(2,1)S(1)}, bf16[3,128,2,128]{3,1,2,0:T(8,128)(2,1)S(1)}, u32[]{:S(2)}, u32[]{:S(2)}) collective-permute-start(bf16[3,128,2,128]{3,1,2,0:T(8,128)(2,1)S(1)} %copy.35), channel_id=1, source_target_pairs={{0,8},{8,16},{16,24},{24,32},{32,40},{40,48},{48,56},{56,64},{64,7... | collective-permute-start | bytes 589832 | tf_op jit(solution)/shard_map/ppermute | solution.py:12
Sparse Core Ops, SparseCore 0:
  10.2 141.2 all-gather.7
  153.6 117.7 all-gather.5
  275.0 78.0 all-gather.11
  355.1 122.3 all-gather.9
where the time goes:
time: 637 us; the launch traced here: 635 us
  waiting for transfers between devices  417 us (65%)
  blocking collectives  159 us (25%)
  matrix products  19.3 us (3%)
  between operations  14 us (2%)
  local copies, waits for them, and re-layouts  12.6 us (2%)
  starting transfers between devices  9.76 us (2%)
    psum x1, blocking collectives, local(): token_grad = lax.psum(partial_value, 'mp').astype(jnp.bfloat16)  129 us
    all_gather x1, waiting for transfers between devices, local(): lax.all_gather(w_key, 'group', axis=0, tiled=True)  119 us
    all_gather x1, waiting for transfers between devices, local(): lax.all_gather(w_value, 'group', axis=0, tiled=True)  118 us
    all_gather x1, waiting for transfers between devices, local(): block_cols = lax.all_gather(encoded, 'mp', axis=1, tiled=True)  81.7 us
    all_to_all x1, waiting for transfers between devices, local(): lax.all_to_all(found_rows, 'group', split_axis=0, concat_axis=0, tiled=True)  59.7 us
    all_gather x1, waiting for transfers between devices, local(): lax.all_gather(w_query, 'group', axis=0, tiled=True)  32.4 us
    all_to_all x1, blocking collectives, local(): lax.all_to_all(requests, 'group', split_axis=0, concat_axis=0, tiled=True)  29.4 us
  transfers between devices with their start and end apart: 7, of which 6 were waited for; matrix products, arithmetic and copies ran while one was open for 4% of the time, Pallas kernels for 0%

commit v1 on v0

v1 whole, which is shorter than its diff:
```python
import jax
import jax.numpy as jnp
from jax import lax
from jax.sharding import PartitionSpec as P

HEAD_DIM = 128


def gather_mp(value):
    count = lax.axis_size("mp")
    copies = jnp.broadcast_to(value[None], (count,) + value.shape)
    return lax.all_to_all(copies, "mp", split_axis=0, concat_axis=0, tiled=True)


def local(
    tokens, neighbour_ids, group_document, embed_table, w_query, w_key, w_value, attended_grad
):
    nchunk = lax.axis_size("group")
    mp_size = lax.axis_size("mp")
    group_here = lax.axis_index("group")
    seq_count, group_len, model_width = tokens.shape
    depth_rows, head_cols = w_query.shape
    local_heads = head_cols // HEAD_DIM
    score_scale = HEAD_DIM ** (-0.5)
    onward = [(g, (g + 1) % nchunk) for g in range(nchunk)]
    backward = [(g, (g - 1) % nchunk) for g in range(nchunk)]

    per = nchunk // mp_size
    spread = [
        (r * mp_size + c, (c * per + r % per) * mp_size + r // per)
        for r in range(nchunk)
        for c in range(mp_size)
    ]
    row_piece = lax.ppermute(w_query, ("group", "mp"), spread)
    weights = lax.all_gather(
        jnp.concatenate([w_key, w_value, w_query, row_piece], axis=1), "group", axis=0, tiled=True
    )
    kv_w = weights[:, : 2 * head_cols]
    query_w = weights[:, 2 * head_cols : 3 * head_cols]
    row_w = weights[:, 3 * head_cols :].reshape(mp_size, per * depth_rows, head_cols)

    last_tok, last_grad = lax.ppermute(
        (tokens[:, -1:], attended_grad[:, -1:]), "group", onward
    )
    moved_tok = jnp.concatenate([last_tok, tokens[:, :-1]], axis=1)
    moved_grad = jnp.concatenate([last_grad, attended_grad[:, :-1]], axis=1)

    flat_ids = neighbour_ids.reshape(-1)
    id_count = flat_ids.shape[0]
    key_count = id_count // seq_count
    rows_dev = embed_table.shape[0]
    capacity = max(2, 3 * id_count // (2 * nchunk))
    owner_group = flat_ids // rows_dev
    onehot = (owner_group[:, None] == jnp.arange(nchunk, dtype=jnp.int32)[None, :]).astype(
        jnp.int32
    )
    before = jnp.cumsum(onehot, axis=0) - onehot
    bucket_rank = jnp.sum(before * onehot, axis=1)
    requests = (
        jnp.zeros((nchunk, 128), jnp.int32)
        .at[owner_group, bucket_rank]
        .set(flat_ids - owner_group * rows_dev)
    )
    slot_index = lax.ppermute(owner_group * capacity + bucket_rank, "group", onward)
    asked = lax.all_to_all(requests, "group", split_axis=0, concat_axis=0, tiled=True)
    asked = jnp.roll(asked[:, :capacity], 1, axis=0)
    found_rows = embed_table[asked].reshape(nchunk, -1)
    returned = lax.all_to_all(found_rows, "group", split_axis=0, concat_axis=0, tiled=True)
    encoded = returned.reshape(nchunk * capacity, -1)[slot_index]
    blocks = gather_mp(encoded)
    block_cols = jnp.swapaxes(blocks, 0, 1).reshape(id_count, model_width)

    kv = jnp.dot(block_cols, kv_w, preferred_element_type=jnp.float32).astype(jnp.bfloat16)
    keys = kv[:, :head_cols].reshape(seq_count, key_count, local_heads, HEAD_DIM)
    values = kv[:, head_cols:].reshape(seq_count, key_count, local_heads, HEAD_DIM)
    query_act = jnp.dot(
        moved_tok.reshape(-1, model_width), query_w, preferred_element_type=jnp.float32
    )
    query_act = query_act.astype(jnp.bfloat16).reshape(seq_count, group_len, local_heads, HEAD_DIM)

    earlier = jnp.maximum(group_here - 1, 0)
    doc_here = lax.dynamic_slice_in_dim(group_document, group_here, 1, 1)[:, 0]
    doc_before = lax.dynamic_slice_in_dim(group_document, earlier, 1, 1)[:, 0]
    same_doc = (group_here >= 1) & (doc_here == doc_before)
    first = jnp.arange(group_len) == 0
    valid_tok = (first[None, :] | same_doc[:, None])[:, :, None, None]

    scores = (
        jnp.einsum("slhd,skhd->shlk", query_act, keys, preferred_element_type=jnp.float32)
        * score_scale
    )
    row_max = jnp.max(scores, axis=-1, keepdims=True)
    exp_scores = jnp.exp(scores - row_max)
    attn_prob = exp_scores / jnp.sum(exp_scores, axis=-1, keepdims=True)
    prob_bf = attn_prob.astype(jnp.bfloat16)
    mixed_sum = jnp.einsum(
        "shlk,skhd->slhd", prob_bf, values, preferred_element_type=jnp.float32
    )
    attended = (
        jnp.where(valid_tok, mixed_sum, 0.0)
        .astype(jnp.bfloat16)
        .reshape(seq_count, group_len, head_cols)
    )
    grad_in = moved_grad.reshape(seq_count, group_len, local_heads, HEAD_DIM)
    grad_kept = jnp.where(valid_tok, grad_in, jnp.zeros_like(grad_in))
    prob_grad = jnp.einsum(
        "slhd,skhd->shlk", grad_kept, values, preferred_element_type=jnp.float32
    )
    dscore = (
        attn_prob
        * (prob_grad - jnp.sum(attn_prob * prob_grad, axis=-1, keepdims=True))
        * score_scale
    ).astype(jnp.bfloat16)
    dquery = jnp.einsum("shlk,skhd->slhd", dscore, keys, preferred_element_type=jnp.float32)
    dquery = dquery.astype(jnp.bfloat16).reshape(seq_count, group_len, head_cols)

    last = lax.ppermute(
        jnp.concatenate([attended[:, :1], dquery[:, :1]], axis=-1), "group", backward
    )
    attended = jnp.concatenate([attended[:, 1:], last[:, :, :head_cols]], axis=1)
    dquery = jnp.concatenate([dquery[:, 1:], last[:, :, head_cols:]], axis=1)
    all_dquery = gather_mp(dquery.reshape(-1, head_cols))
    part = jnp.einsum(
        "ctj,cnj->tn", all_dquery, row_w, preferred_element_type=jnp.float32
    ).astype(jnp.bfloat16)
    token_grad = jnp.swapaxes(gather_mp(part), 0, 1)
    return (attended, token_grad.reshape(seq_count, group_len, model_width))


def solution(mesh):
    in_specs = (
        P(None, "group", None),
        P("group", None, None),
        P(),
        P("group", "mp"),
        P("group", "mp"),
        P("group", "mp"),
        P("group", "mp"),
        P(None, "group", "mp"),
    )
    out_specs = (P(None, "group", "mp"), P(None, "group", None))
    return jax.shard_map(local, mesh=mesh, in_specs=in_specs, out_specs=out_specs, check_vma=False)
```

time: 637 us -> 280 us (0.44)
  waiting for transfers between devices: 417 us -> 120 us
  blocking collectives: 159 us -> 38.3 us
  starting transfers between devices: 9.76 us -> 39.9 us
  local copies, waits for them, and re-layouts: 12.6 us -> 38.7 us
  other arithmetic: 4.54 us -> 16 us
  matrix products: 19.3 us -> 12.2 us
    all_gather x4 -> x1, waiting for transfers between devices: 351 us -> 0.44 us  [local(): lax.all_gather(jnp.concatenate([w_key, w_value, w_query, row_piece], axis...]
    psum x1 -> x0, blocking collectives: 129 us -> none  [local(): token_grad = lax.psum(partial_value, 'mp').astype(jnp.bfloat16)]
    all_to_all x0 -> x3, waiting for transfers between devices: none -> 39.8 us  [gather_mp(): return lax.all_to_all(copies, 'mp', split_axis=0, concat_axis=0, tiled=True)]
    ppermute x2 -> x5, waiting for transfers between devices: 4.34 us -> 42 us  [the longest x2 34.2 us: local(): lax.ppermute((tokens[:, -1:], attended_grad[:, -1:]), 'group', onward)]
    all_to_all x1, waiting for transfers between devices: 59.7 us -> 37.9 us  [local(): lax.all_to_all(found_rows, 'group', split_axis=0, concat_axis=0, tiled=True)]
    all_to_all x0 -> x3, starting transfers between devices: none -> 18.2 us  [gather_mp(): return lax.all_to_all(copies, 'mp', split_axis=0, concat_axis=0, tiled=True)]
    scatter x1, local copies, waits for them, and re-layouts: 2.92 us -> 19.7 us  [local(): requests = jnp.zeros((nchunk, 128), jnp.int32).at[owner_group, bucket_ran...]
    ppermute x2 -> x5, starting transfers between devices: 4.19 us -> 16.2 us  [the longest x1 5.98 us: local(): row_piece = lax.ppermute(w_query, ('group', 'mp'), spread)]
  transfers between devices with their start and end apart: 7 -> 10, of which waited for: 6 -> 9; matrix products, arithmetic and copies ran while one was open for 4% -> 19% of each run, Pallas kernels for 0% -> 0%
where the time goes in v1:
time: 280 us
  waiting for transfers between devices  120 us (43%)
  starting transfers between devices  39.9 us (14%)
  local copies, waits for them, and re-layouts  38.7 us (14%)
  blocking collectives  38.3 us (14%)
  other arithmetic  16 us (6%)
  between operations  14.4 us (5%)
  matrix products  12.2 us (4%)
    all_to_all x3, waiting for transfers between devices, gather_mp(): return lax.all_to_all(copies, 'mp', split_axis=0, concat_axis=0, tiled=True)  39.8 us
    all_to_all x1, blocking collectives, local(): lax.all_to_all(requests, 'group', split_axis=0, concat_axis=0, tiled=True)  38.3 us
    all_to_all x1, waiting for transfers between devices, local(): lax.all_to_all(found_rows, 'group', split_axis=0, concat_axis=0, tiled=True)  37.9 us
    ppermute x2, waiting for transfers between devices, local(): lax.ppermute((tokens[:, -1:], attended_grad[:, -1:]), 'group', onward)  34.2 us
    scatter x1, local copies, waits for them, and re-layouts, local(): requests = jnp.zeros((nchunk, 128), jnp.int32).at[owner_group, bucket_ran...  19.7 us
    all_to_all x3, starting transfers between devices, gather_mp(): return lax.all_to_all(copies, 'mp', split_axis=0, concat_axis=0, tiled=True)  18.2 us
    all_to_all x2, other arithmetic, local(): lax.all_to_all(found_rows, 'group', split_axis=0, concat_axis=0, tiled=True)  7.72 us
    ppermute x1, starting transfers between devices, local(): row_piece = lax.ppermute(w_query, ('group', 'mp'), spread)  5.98 us
  transfers between devices with their start and end apart: 10, of which 9 were waited for; matrix products, arithmetic and copies ran while one was open for 19% of the time, Pallas kernels for 0%

profile of v1, /device:TPU:24, one launch (start us, length us, event | category | flops | bytes accessed | tf_op | source)
XLA Modules:
  0.0 279.6 jit_solution(6060550063477982929)
XLA Ops:
  7.2 6.0 %collective-permute-start.1 = (bf16[64,256]{1,0:T(8,128)(2,1)}, bf16[64,256]{1,0:T(8,128)(2,1)S(1)}, u32[]{:S(2)}, u32[]{:S(2)}) collective-permute-start(bf16[64,256]{1,0:T(8,128)(2,1)} %param.12), channel_id=1, source_target_pairs={{0,0},{1,64},{2,128},{3,192},{4,256},{5,320},{6,384},{7,448},{8,8}... | collective-permute-start | bytes 98312 | tf_op jit(solution)/shard_map/ppermute | solution.py:34
  13.2 3.8 %collective-permute-done.1 = bf16[64,256]{1,0:T(8,128)(2,1)S(1)} collective-permute-done((bf16[64,256]{1,0:T(8,128)(2,1)}, bf16[64,256]{1,0:T(8,128)(2,1)S(1)}, u32[]{:S(2)}, u32[]{:S(2)}) %collective-permute-start.1) | collective-permute-done | bytes 32800 | tf_op jit(solution)/shard_map/ppermute | solution.py:34
  21.9 19.7 %scatter_fusion = s32[64,128]{1,0:T(8,128)S(1)} fusion(s32[64,128]{1,0:T(8,128)S(1)} %broadcast_in_dim.35, s32[384]{0:T(512)S(1)} %fusion.48, s32[384]{0:T(512)S(1)} %get-tuple-element.2), kind=kCustom, calls=%fused_computation.2 | custom fusion | bytes 7680 | tf_op jit(solution)/shard_map/scatter | solution.py:62
  41.6 38.3 %all_to_all.37 = s32[64,1,128]{2,1,0:T(1,128)S(1)} all-to-all(s32[64,1,128]{2,1,0:T(1,128)S(1)} %bitcast.114), channel_id=1, replica_groups=mesh['group'=64,'mp'=8] {'group'}, dimensions={0} | all-to-all | bytes 65536 | tf_op jit(solution)/shard_map/all_to_all | solution.py:65
  80.5 2.7 gather_fusion
  84.1 4.2 %reduce.8 = bf16[64,4608]{1,0:T(8,128)(2,1)S(1)} reduce(bf16[64,1,4608]{2,1,0:T(2,128)(2,1)S(1)} %all_to_all.31, bf16[]{:T(256)} %broadcast.236), dimensions={1}, to_apply=%all_to_all.31.reduce_sub_computation | reduce | bytes 1179650 | tf_op jit(solution)/shard_map/all_to_all | solution.py:68
  89.2 5.4 %all-to-all-start.1 = ((bf16[64,2,2304]{2,1,0:T(2,128)(2,1)}), bf16[64,2,2304]{2,1,0:T(2,128)(2,1)S(1)}, u32[]{:S(2)}, u32[]{:S(2)}) async-start(bf16[64,2,2304]{2,1,0:T(2,128)(2,1)} %reshape.340), calls=%async_computation.1 | async-start | bytes 1179648 | tf_op jit(solution)/shard_map/all_to_all | solution.py:68
  94.7 2.2 collective-permute-start
  96.9 2.7 collective-permute-done
  99.6 37.9 %all-to-all-done.1 = bf16[64,2,2304]{2,1,0:T(2,128)(2,1)S(1)} async-done(((bf16[64,2,2304]{2,1,0:T(2,128)(2,1)}), bf16[64,2,2304]{2,1,0:T(2,128)(2,1)S(1)}, u32[]{:S(2)}, u32[]{:S(2)}) %all-to-all-start.1) | async-done | bytes 589856 | tf_op jit(solution)/shard_map/all_to_all | solution.py:68
  138.0 3.5 %reduce.4 = bf16[64,4608]{1,0:T(8,128)(2,1)S(1)} reduce(bf16[64,1,4608]{2,1,0:T(2,128)(2,1)S(1)} %reshape.341, bf16[]{:T(256)} %constant.75), dimensions={1}, to_apply=%all_to_all.27.reduce_sub_computation | reduce | bytes 1179650 | tf_op jit(solution)/shard_map/all_to_all | solution.py:68
  142.2 2.1 gather_fusion.1
  146.5 4.9 %all-to-all-start.2 = ((bf16[8,384,512]{1,2,0:T(8,128)(2,1)}), bf16[8,384,512]{1,2,0:T(8,128)(2,1)}, u32[]{:S(2)}, u32[]{:S(2)}) async-start(bf16[8,384,512]{1,2,0:T(8,128)(2,1)} %broadcast_in_dim.37), calls=%async_computation.2 | async-start | bytes 6291456 | tf_op jit(solution)/shard_map/all_to_all | solution.py:12
  153.5 2.4 collective-permute-start.2
  156.2 34.2 %collective-permute-done.2 = bf16[3,1,4096]{2,1,0:T(2,128)(2,1)S(1)} collective-permute-done((bf16[3,1,4096]{2,1,0:T(2,128)(2,1)S(1)}, bf16[3,1,4096]{2,1,0:T(2,128)(2,1)S(1)}, u32[]{:S(2)}, u32[]{:S(2)}) %collective-permute-start.2) | collective-permute-done | bytes 24608 | tf_op jit(solution)/shard_map/ppermute | solution.py:42
  191.9 4.7 %all-to-all-done.2 = bf16[8,384,512]{1,2,0:T(8,128)(2,1)} async-done(((bf16[8,384,512]{1,2,0:T(8,128)(2,1)}), bf16[8,384,512]{1,2,0:T(8,128)(2,1)}, u32[]{:S(2)}, u32[]{:S(2)}) %all-to-all-start.2) | async-done | bytes 3145760 | tf_op jit(solution)/shard_map/all_to_all | solution.py:12
  197.0 5.1 %fusion.6 = bf16[384,512]{1,0:T(8,128)(2,1)S(1)} fusion(bf16[384,4096]{0,1:T(8,128)(2,1)} %bitcast.8, bf16[4096,1024]{1,0:T(8,128)(2,1)} %all-gather.2.cloned.1.call-done), kind=kOutput, calls=%fused_computation.10 | convolution fusion | flops 1610809344 | bytes 7733248 | tf_op jit(solution)/shard_map/dot_general | solution.py:73
  202.3 2.2 fusion.19
  208.6 3.7 %collective-permute-start.4 = (bf16[3,1,512]{2,1,0:T(2,128)(2,1)S(1)}, bf16[3,1,512]{2,1,0:T(2,128)(2,1)S(1)}, u32[]{:S(2)}, u32[]{:S(2)}) collective-permute-start(bf16[3,1,512]{2,1,0:T(2,128)(2,1)S(1)} %pad_maximum_fusion.4), channel_id=1, source_target_pairs={{0,504},{8,0},{16,8},{24,16},{32,24},{40,32},{48,40},{56,48},{64,5... | collective-permute-start | bytes 9224 | tf_op jit(solution)/shard_map/ppermute | solution.py:117
  214.7 7.0 %all-to-all-start.3 = ((bf16[8,192,256]{2,1,0:T(8,128)(2,1)}), bf16[8,192,256]{2,1,0:T(8,128)(2,1)}, u32[]{:S(2)}, u32[]{:S(2)}) async-start(bf16[8,192,256]{2,1,0:T(8,128)(2,1)} %broadcast_in_dim.67), calls=%async_computation.3 | async-start | bytes 1572864 | tf_op jit(solution)/shard_map/all_to_all | solution.py:12
  221.7 11.7 %all-to-all-done.3 = bf16[8,192,256]{2,1,0:T(8,128)(2,1)} async-done(((bf16[8,192,256]{2,1,0:T(8,128)(2,1)}), bf16[8,192,256]{2,1,0:T(8,128)(2,1)}, u32[]{:S(2)}, u32[]{:S(2)}) %all-to-all-start.3) | async-done | bytes 786464 | tf_op jit(solution)/shard_map/all_to_all | solution.py:12
  236.6 6.3 %all-to-all-start.4 = ((bf16[8,192,512]{2,1,0:T(8,128)(2,1)}), bf16[8,192,512]{2,1,0:T(8,128)(2,1)S(1)}, u32[]{:S(2)}, u32[]{:S(2)}) async-start(bf16[8,192,512]{2,1,0:T(8,128)(2,1)} %broadcast_in_dim.68), calls=%async_computation.4 | async-start | bytes 3145728 | tf_op jit(solution)/shard_map/all_to_all | solution.py:12
  243.6 23.4 %all-to-all-done.4 = bf16[8,192,512]{2,1,0:T(8,128)(2,1)S(1)} async-done(((bf16[8,192,512]{2,1,0:T(8,128)(2,1)}), bf16[8,192,512]{2,1,0:T(8,128)(2,1)S(1)}, u32[]{:S(2)}, u32[]{:S(2)}) %all-to-all-start.4) | async-done | bytes 1572896 | tf_op jit(solution)/shard_map/all_to_all | solution.py:12
  269.0 3.7 %reshape.308 = bf16[3,64,4096]{2,1,0:T(8,128)(2,1)} reshape(bf16[192,8,512]{2,1,0:T(8,128)(2,1)} %copy.58) | data formatting | bytes 3145728 | tf_op jit(solution)/shard_map/reshape | solution.py:127
  (76 shorter events, 27.4 us)
Async XLA Ops:
  7.2 73.3 %copy-start = (bf16[1024,512]{1,0:T(8,128)(2,1)S(1)}, bf16[1024,512]{1,0:T(8,128)(2,1)}, u32[]{:S(2)}) copy-start(bf16[1024,512]{1,0:T(8,128)(2,1)} %param.11) | copy-start | bytes 3145732
  7.2 189.8 %all-gather.2.cloned.1.call-start = ((), (), s32[]{:S(2)}) async-start(), calls=%async_computation.5 | async-start | bytes 8519680 | tf_op jit(solution)/shard_map/all_gather | solution.py:35
  7.2 9.8 %collective-permute-start.1 = (bf16[64,256]{1,0:T(8,128)(2,1)}, bf16[64,256]{1,0:T(8,128)(2,1)S(1)}, u32[]{:S(2)}, u32[]{:S(2)}) collective-permute-start(bf16[64,256]{1,0:T(8,128)(2,1)} %param.12), channel_id=1, source_target_pairs={{0,0},{1,64},{2,128},{3,192},{4,256},{5,320},{6,384},{7,448},{8,8}... | collective-permute-start | bytes 98312 | tf_op jit(solution)/shard_map/ppermute | solution.py:34
  89.2 48.3 %all-to-all-start.1 = ((bf16[64,2,2304]{2,1,0:T(2,128)(2,1)}), bf16[64,2,2304]{2,1,0:T(2,128)(2,1)S(1)}, u32[]{:S(2)}, u32[]{:S(2)}) async-start(bf16[64,2,2304]{2,1,0:T(2,128)(2,1)} %reshape.340), calls=%async_computation.1 | async-start | bytes 1179648 | tf_op jit(solution)/shard_map/all_to_all | solution.py:68
  94.7 4.9 %collective-permute-start = (s32[384]{0:T(512)S(1)}, s32[384]{0:T(512)S(1)}, u32[]{:S(2)}, u32[]{:S(2)}) collective-permute-start(s32[384]{0:T(512)S(1)} %multiply_add_fusion), channel_id=1, source_target_pairs={{0,8},{8,16},{16,24},{24,32},{32,40},{40,48},{48,56},{56,64},{64,7... | collective-permute-start | bytes 4616 | tf_op jit(solution)/shard_map/ppermute | solution.py:64
  146.5 4.9 %copy-start.4 = (bf16[3,64,256]{2,1,0:T(8,128)(2,1)S(1)}, bf16[3,64,256]{2,1,0:T(8,128)(2,1)}, u32[]{:S(2)}) copy-start(bf16[3,64,256]{2,1,0:T(8,128)(2,1)} %param.15) | copy-start | bytes 294916
  146.5 6.9 %copy-start.1 = (bf16[3,64,4096]{2,1,0:T(8,128)(2,1)S(1)}, bf16[3,64,4096]{2,1,0:T(8,128)(2,1)}, u32[]{:S(2)}) copy-start(bf16[3,64,4096]{2,1,0:T(8,128)(2,1)} %param.8) | copy-start | bytes 4718596
  146.5 9.3 %copy-start.3 = (s32[3,64]{1,0:T(4,128)S(1)}, s32[3,64]{1,0:T(4,128)}, u32[]{:S(2)}) copy-start(s32[3,64]{1,0:T(4,128)} %param.10) | copy-start | bytes 2308
  146.5 50.1 %all-to-all-start.2 = ((bf16[8,384,512]{1,2,0:T(8,128)(2,1)}), bf16[8,384,512]{1,2,0:T(8,128)(2,1)}, u32[]{:S(2)}, u32[]{:S(2)}) async-start(bf16[8,384,512]{1,2,0:T(8,128)(2,1)} %broadcast_in_dim.37), calls=%async_computation.2 | async-start | bytes 6291456 | tf_op jit(solution)/shard_map/all_to_all | solution.py:12
  151.5 55.0 %collective-permute-start.3 = (bf16[3,1,256]{2,1,0:T(2,128)(2,1)S(1)}, bf16[3,1,256]{2,1,0:T(2,128)(2,1)S(1)}, u32[]{:S(2)}, u32[]{:S(2)}) collective-permute-start(bf16[3,1,256]{2,1,0:T(2,128)(2,1)S(1)} %slice.74), channel_id=1, source_target_pairs={{0,8},{8,16},{16,24},{24,32},{32,40},{40,48},{48,56},{56,64},{64,7... | collective-permute-start | bytes 4616 | tf_op jit(solution)/shard_map/ppermute | solution.py:42
  153.5 36.9 %collective-permute-start.2 = (bf16[3,1,4096]{2,1,0:T(2,128)(2,1)S(1)}, bf16[3,1,4096]{2,1,0:T(2,128)(2,1)S(1)}, u32[]{:S(2)}, u32[]{:S(2)}) collective-permute-start(bf16[3,1,4096]{2,1,0:T(2,128)(2,1)S(1)} %slice.68), channel_id=1, source_target_pairs={{0,8},{8,16},{16,24},{24,32},{32,40},{40,48},{48,56},{56,64},{64,7... | collective-permute-start | bytes 73736 | tf_op jit(solution)/shard_map/ppermute | solution.py:42
  197.0 5.2 %copy-start.2 = (bf16[3,64,4096]{2,1,0:T(8,128)(2,1)S(1)}, bf16[3,64,4096]{2,1,0:T(8,128)(2,1)}, u32[]{:S(2)}) copy-start(bf16[3,64,4096]{2,1,0:T(8,128)(2,1)} %pad_maximum_fusion) | copy-start | bytes 4718596
  208.6 5.1 %collective-permute-start.4 = (bf16[3,1,512]{2,1,0:T(2,128)(2,1)S(1)}, bf16[3,1,512]{2,1,0:T(2,128)(2,1)S(1)}, u32[]{:S(2)}, u32[]{:S(2)}) collective-permute-start(bf16[3,1,512]{2,1,0:T(2,128)(2,1)S(1)} %pad_maximum_fusion.4), channel_id=1, source_target_pairs={{0,504},{8,0},{16,8},{24,16},{32,24},{40,32},{48,40},{56,48},{64,5... | collective-permute-start | bytes 9224 | tf_op jit(solution)/shard_map/ppermute | solution.py:117
  214.7 18.7 %all-to-all-start.3 = ((bf16[8,192,256]{2,1,0:T(8,128)(2,1)}), bf16[8,192,256]{2,1,0:T(8,128)(2,1)}, u32[]{:S(2)}, u32[]{:S(2)}) async-start(bf16[8,192,256]{2,1,0:T(8,128)(2,1)} %broadcast_in_dim.67), calls=%async_computation.3 | async-start | bytes 1572864 | tf_op jit(solution)/shard_map/all_to_all | solution.py:12
  221.7 11.7 %slice-start = ((bf16[4096,1024]{1,0:T(8,128)(2,1)}), bf16[4096,256]{1,0:T(8,128)(2,1)S(1)}, s32[]{:S(2)}) async-start(bf16[4096,1024]{1,0:T(8,128)(2,1)} %all-gather.2.cloned.1.call-done), calls=%async_computation.6 | async-start | bytes 4194304 | tf_op jit(solution)/shard_map/slice | solution.py:40
  236.6 30.4 %all-to-all-start.4 = ((bf16[8,192,512]{2,1,0:T(8,128)(2,1)}), bf16[8,192,512]{2,1,0:T(8,128)(2,1)S(1)}, u32[]{:S(2)}, u32[]{:S(2)}) async-start(bf16[8,192,512]{2,1,0:T(8,128)(2,1)} %broadcast_in_dim.68), calls=%async_computation.4 | async-start | bytes 3145728 | tf_op jit(solution)/shard_map/all_to_all | solution.py:12
Sparse Core Ops, SparseCore 0:
  18.6 178.3 all-gather.1

commit v2 on v1

v2 whole, which is shorter than its diff:
```python
import functools

import jax
import jax.numpy as jnp
from jax import lax
from jax.experimental import pallas as pl
from jax.experimental.pallas import tpu as pltpu
from jax.sharding import PartitionSpec as P

HEAD_DIM = 128
BF, F32, I32 = jnp.bfloat16, jnp.float32, jnp.int32
PARAMS = pltpu.CompilerParams(vmem_limit_bytes=48 * 1024 * 1024)
NT = (((1,), (1,)), ((), ()))


def iota(shape, dim):
    return lax.broadcasted_iota(I32, shape, dim)


def dot(a, b, dims=(((1,), (0,)), ((), ()))):
    return lax.dot_general(a, b, dims, preferred_element_type=F32)


def bucket_kernel(nchunk, rows_dev, ids_ref, requests_ref, slot_ref):
    seqs, keys = ids_ref.shape
    ids = jnp.concatenate([ids_ref[s : s + 1, :] for s in range(seqs)], axis=1)
    total = seqs * keys
    owner = ids // rows_dev
    lid = ids - owner * rows_dev
    owned = (iota((nchunk, total), 0) == owner).astype(F32)
    owned_bf = owned.astype(BF)
    earlier = (iota((total, total), 0) < iota((total, total), 1)).astype(F32).astype(BF)
    rank = jnp.sum(dot(owned_bf, earlier) * owned, axis=0, keepdims=True).astype(I32)
    placed = iota((128, total), 0) == rank
    high = jnp.where(placed, lid // 32, 0).astype(F32).astype(BF)
    low = jnp.where(placed, lid % 32, 0).astype(F32).astype(BF)
    requests_ref[...] = (dot(owned_bf, high, NT) * 32.0 + dot(owned_bf, low, NT)).astype(I32)
    slot = rank * nchunk + owner
    for s in range(seqs):
        slot_ref[s : s + 1, :] = slot[:, s * keys : (s + 1) * keys]


def fetch_kernel(capacity, asked_ref, table_ref, out_ref):
    nchunk = asked_ref.shape[0]
    rows_dev, feats = table_ref.shape
    asked = pltpu.roll(asked_ref[...], 1, 0)
    lanes = iota((nchunk, rows_dev), 1)
    chosen = jnp.concatenate(
        [(asked[:, s : s + 1] == lanes).astype(F32).astype(BF) for s in range(capacity)], axis=0
    )
    found = dot(chosen, table_ref[...]).astype(BF)
    for s in range(capacity):
        out_ref[:, s * feats : (s + 1) * feats] = found[s * nchunk : (s + 1) * nchunk]


def order_kernel(capacity, slot_ref, rows_ref, out_ref):
    seqs, keys = slot_ref.shape
    nchunk = rows_ref.shape[0]
    copies, _, feats = out_ref.shape
    rows = jnp.concatenate(
        [rows_ref[:, s * feats : (s + 1) * feats] for s in range(capacity)], axis=0
    )
    slots = jnp.concatenate([slot_ref[...], jnp.zeros((8 - seqs, keys), I32)], axis=0)
    slots = slots.astype(F32).T.astype(I32)
    lanes = iota((keys, capacity * nchunk), 1)
    for s in range(seqs):
        chosen = (slots[:, s : s + 1] == lanes).astype(F32).astype(BF)
        found = dot(chosen, rows).astype(BF)
        for c in range(copies):
            out_ref[c, s * keys : (s + 1) * keys, :] = found


def interleave(core0, core1, run):
    parts = []
    for start in range(0, core0.shape[0], run):
        parts += [core0[start : start + run], core1[start : start + run]]
    return jnp.concatenate(parts, axis=0)


def attend_kernel(
    run, scal_ref, enc_ref, mine_ref, other_ref, tok_ref, last_tok_ref, grad_ref, last_grad_ref,
    att_ref, dq_ref, kv_acc, q_acc,
):
    step, steps = pl.program_id(0), pl.num_programs(0)
    seqs, length, cols = grad_ref.shape
    keys = kv_acc.shape[0] // seqs

    @pl.when(step == 0)
    def _():
        kv_acc[...] = jnp.zeros_like(kv_acc)
        q_acc[...] = jnp.zeros_like(q_acc)

    is_last = iota((length, tok_ref.shape[2]), 0) == length - 1
    tok = jnp.concatenate(
        [jnp.where(is_last, last_tok_ref[s : s + 1, :], tok_ref[s]) for s in range(seqs)], axis=0
    )

    def add(core0, core1):
        weights = interleave(core0, core1, run)
        kv_acc[...] += dot(enc_ref[0], weights[:, : 2 * cols])
        q_acc[...] += dot(tok, weights[:, 2 * cols :])

    @pl.when(scal_ref[0] == 0)
    def _():
        add(mine_ref[...], other_ref[...])

    @pl.when(scal_ref[0] != 0)
    def _():
        add(other_ref[...], mine_ref[...])

    @pl.when(step == steps - 1)
    def _():
        scale = HEAD_DIM ** (-0.5)
        last_row = iota((length, HEAD_DIM), 0) == length - 1
        for s in range(seqs):
            valid = last_row | (scal_ref[1 + s] != 0)
            for h in range(cols // HEAD_DIM):
                head = slice(h * HEAD_DIM, (h + 1) * HEAD_DIM)
                value_head = slice(cols + h * HEAD_DIM, cols + (h + 1) * HEAD_DIM)
                query = q_acc[s * length : (s + 1) * length, head].astype(BF)
                key = kv_acc[s * keys : (s + 1) * keys, head].astype(BF)
                value = kv_acc[s * keys : (s + 1) * keys, value_head].astype(BF)
                grad = jnp.where(last_row, last_grad_ref[s : s + 1, head], grad_ref[s, :, head])
                grad = jnp.where(valid, grad, jnp.zeros_like(grad))
                scores = dot(query, key, NT) * scale
                exps = jnp.exp(scores - jnp.max(scores, axis=-1, keepdims=True))
                prob = exps / jnp.sum(exps, axis=-1, keepdims=True)
                mixed = dot(prob.astype(BF), value)
                att_ref[s, :, head] = jnp.where(valid, mixed, 0.0).astype(BF)
                prob_grad = dot(grad, value, NT)
                mean = jnp.sum(prob * prob_grad, axis=-1, keepdims=True)
                dscore = (prob * (prob_grad - mean) * scale).astype(BF)
                dq_ref[s, :, head] = dot(dscore, key).astype(BF)


def return_kernel(att_ref, dq_ref, last_ref, att_out, dq_out):
    seqs, length, cols = att_ref.shape
    is_last = iota((length, cols), 0) == length - 1
    for s in range(seqs):
        att_out[s] = jnp.where(is_last, last_ref[s : s + 1, :cols], att_ref[s])
        rows = jnp.where(is_last, last_ref[s : s + 1, cols:], dq_ref[s])
        for c in range(dq_out.shape[0]):
            dq_out[c, s * length : (s + 1) * length, :] = rows


def token_kernel(run, scal_ref, dq_ref, mine_ref, other_ref, out_ref, acc):
    step, steps = pl.program_id(0), pl.num_programs(0)

    @pl.when(step == 0)
    def _():
        acc[...] = jnp.zeros_like(acc)

    @pl.when(scal_ref[0] == 0)
    def _():
        acc[...] += dot(dq_ref[0], interleave(mine_ref[...], other_ref[...], run), NT)

    @pl.when(scal_ref[0] != 0)
    def _():
        acc[...] += dot(dq_ref[0], interleave(other_ref[...], mine_ref[...], run), NT)

    @pl.when(step == steps - 1)
    def _():
        rounded = acc[...].astype(BF)
        for c in range(out_ref.shape[0]):
            out_ref[c] = rounded


def join_kernel(in_ref, out_ref):
    out_ref[...] = in_ref[0]


def local(
    tokens, neighbour_ids, group_document, embed_table, w_query, w_key, w_value, attended_grad
):
    nchunk = lax.axis_size("group")
    mp_size = lax.axis_size("mp")
    group_here = lax.axis_index("group")
    core = group_here % 2
    seqs, length, width = tokens.shape
    run, cols = w_query.shape
    keys = neighbour_ids.shape[2]
    id_count = seqs * keys
    rows_dev, feats = embed_table.shape
    capacity = max(2, 3 * id_count // (2 * nchunk))
    per = nchunk // mp_size
    onward = [(g, (g + 1) % nchunk) for g in range(nchunk)]
    backward = [(g, (g - 1) % nchunk) for g in range(nchunk)]

    def across(g):
        return g ^ 2

    def spread(turn):
        return [
            (r * mp_size + c, turn(c * per + r % per) * mp_size + r // per)
            for r in range(nchunk)
            for c in range(mp_size)
        ]

    own = jnp.concatenate([w_key, w_value, w_query], axis=1)
    near = lax.ppermute(own, "group", [(g, across(g)) for g in range(nchunk)])
    piece = lax.ppermute(w_query, ("group", "mp"), spread(lambda g: g))
    near_piece = lax.ppermute(w_query, ("group", "mp"), spread(across))
    own = jnp.concatenate([own, piece], axis=1)
    near = jnp.concatenate([near, near_piece], axis=1)
    lower = (group_here // 2) % 2 == 0
    pair = jnp.concatenate([jnp.where(lower, own, near), jnp.where(lower, near, own)], axis=0)
    mine = lax.all_gather(
        pair, "group", axis=0, tiled=True,
        axis_index_groups=[[z * 4 + r for z in range(nchunk // 4)] for r in range(4)],
    )
    other = lax.ppermute(mine, "group", [(g, g ^ 1) for g in range(nchunk)])

    last_tok, last_grad = lax.ppermute((tokens[:, -1], attended_grad[:, -1]), "group", onward)

    requests, slot = pl.pallas_call(
        functools.partial(bucket_kernel, nchunk, rows_dev),
        out_shape=[
            jax.ShapeDtypeStruct((nchunk, 128), I32),
            jax.ShapeDtypeStruct((seqs, keys), I32),
        ],
        compiler_params=PARAMS,
    )(neighbour_ids.reshape(seqs, keys))
    slot = lax.ppermute(slot, "group", onward)
    asked = lax.all_to_all(requests, "group", split_axis=0, concat_axis=0, tiled=True)
    found = pl.pallas_call(
        functools.partial(fetch_kernel, capacity),
        out_shape=jax.ShapeDtypeStruct((nchunk, capacity * feats), BF),
        compiler_params=PARAMS,
    )(asked, embed_table)
    returned = lax.all_to_all(found, "group", split_axis=0, concat_axis=0, tiled=True)
    encoded = pl.pallas_call(
        functools.partial(order_kernel, capacity),
        out_shape=jax.ShapeDtypeStruct((mp_size, id_count, feats), BF),
        compiler_params=PARAMS,
    )(slot, returned)
    encoded = lax.all_to_all(encoded, "mp", split_axis=0, concat_axis=0, tiled=True)

    earlier = jnp.maximum(group_here - 1, 0)
    doc_here = lax.dynamic_slice_in_dim(group_document, group_here, 1, 1)[:, 0]
    doc_before = lax.dynamic_slice_in_dim(group_document, earlier, 1, 1)[:, 0]
    same_doc = (group_here >= 1) & (doc_here == doc_before)
    scalars = jnp.concatenate([core[None].astype(I32), same_doc.astype(I32)])

    half = width // mp_size // 2
    whole = lambda *shape: pl.BlockSpec(shape, lambda i, s: (0,) * len(shape))
    att, dquery = pl.pallas_call(
        functools.partial(attend_kernel, run),
        grid_spec=pltpu.PrefetchScalarGridSpec(
            num_scalar_prefetch=1,
            grid=(mp_size,),
            in_specs=[
                pl.BlockSpec((1, id_count, feats), lambda i, s: (i, 0, 0)),
                pl.BlockSpec((half, 3 * cols), lambda i, s: (i, 0)),
                pl.BlockSpec((half, 3 * cols), lambda i, s: (i, 0)),
                pl.BlockSpec((seqs, length, feats), lambda i, s: (0, 0, i)),
                pl.BlockSpec((seqs, feats), lambda i, s: (0, i)),
                whole(seqs, length, cols),
                whole(seqs, cols),
            ],
            out_specs=[whole(seqs, length, cols), whole(seqs, length, cols)],
            scratch_shapes=[
                pltpu.VMEM((id_count, 2 * cols), F32),
                pltpu.VMEM((seqs * length, cols), F32),
            ],
        ),
        out_shape=[jax.ShapeDtypeStruct((seqs, length, cols), BF)] * 2,
        compiler_params=PARAMS,
    )(scalars, encoded, mine, other, tokens, last_tok, attended_grad, last_grad)

    last = lax.ppermute(
        jnp.concatenate([att[:, -1], dquery[:, -1]], axis=-1), "group", backward
    )
    attended, dquery = pl.pallas_call(
        return_kernel,
        out_shape=[
            jax.ShapeDtypeStruct((seqs, length, cols), BF),
            jax.ShapeDtypeStruct((mp_size, seqs * length, cols), BF),
        ],
        compiler_params=PARAMS,
    )(att, dquery, last)
    dquery = lax.all_to_all(dquery, "mp", split_axis=0, concat_axis=0, tiled=True)
    part = pl.pallas_call(
        functools.partial(token_kernel, run),
        grid_spec=pltpu.PrefetchScalarGridSpec(
            num_scalar_prefetch=1,
            grid=(mp_size,),
            in_specs=[
                pl.BlockSpec((1, seqs * length, cols), lambda i, s: (i, 0, 0)),
                pl.BlockSpec((half, cols), lambda i, s: (i, 3)),
                pl.BlockSpec((half, cols), lambda i, s: (i, 3)),
            ],
            out_specs=whole(mp_size, seqs * length, feats),
            scratch_shapes=[pltpu.VMEM((seqs * length, feats), F32)],
        ),
        out_shape=jax.ShapeDtypeStruct((mp_size, seqs * length, feats), BF),
        compiler_params=PARAMS,
    )(scalars, dquery, mine, other)
    part = lax.all_to_all(part, "mp", split_axis=0, concat_axis=0, tiled=True)
    token_grad = pl.pallas_call(
        join_kernel,
        grid=(mp_size,),
        in_specs=[pl.BlockSpec((1, seqs * length, feats), lambda i: (i, 0, 0))],
        out_specs=pl.BlockSpec((seqs * length, feats), lambda i: (0, i)),
        out_shape=jax.ShapeDtypeStruct((seqs * length, width), BF),
        compiler_params=PARAMS,
    )(part)
    return (attended, token_grad.reshape(seqs, length, width))


def solution(mesh):
    in_specs = (
        P(None, "group", None),
        P("group", None, None),
        P(),
        P("group", "mp"),
        P("group", "mp"),
        P("group", "mp"),
        P("group", "mp"),
        P(None, "group", "mp"),
    )
    out_specs = (P(None, "group", "mp"), P(None, "group", None))
    return jax.shard_map(local, mesh=mesh, in_specs=in_specs, out_specs=out_specs, check_vma=False)
```

time: 280 us -> 281 us (level)
  blocking collectives: 38.3 us -> 82 us
  local copies, waits for them, and re-layouts: 38.7 us -> 6.98 us
  Pallas kernels: 0 us -> 24.2 us
  other arithmetic: 16 us -> 2.88 us
  matrix products: 12.2 us -> 0 us
  waiting for transfers between devices: 120 us -> 113 us
  starting transfers between devices: 39.9 us -> 35.3 us
    all_gather x1, waiting for transfers between devices: 0.44 us -> 67.2 us  [local(): lax.all_gather(pair, 'group', axis=0, tiled=True, axis_index_groups=[[z *...]
    all_to_all x4 -> x2, waiting for transfers between devices: 77.7 us -> 26.9 us  [the longest x1 26.9 us: local(): lax.all_to_all(encoded, 'mp', split_axis=0, concat_axis=0, tiled=True)]
    all_to_all x0 -> x2, blocking collectives: none -> 44.1 us  [the longest x1 25.8 us: local(): part = lax.all_to_all(part, 'mp', split_axis=0, concat_axis=0, tiled=True)]
    pallas_call x0 -> x7, Pallas kernels: none -> 24.2 us  [the longest x1 11 us: local(): pl.pallas_call(functools.partial(attend_kernel, run), grid_spec=pltpu.Pre...]
    ppermute x5 -> x8, waiting for transfers between devices: 42 us -> 18.6 us  [the longest x2 11.3 us: local(): lax.ppermute((tokens[:, -1], attended_grad[:, -1]), 'group', onward)]
    scatter x1 -> x0, local copies, waits for them, and re-layouts: 19.7 us -> none  [local(): requests = jnp.zeros((nchunk, 128), jnp.int32).at[owner_group, bucket_ran...]
    dot_general x7 -> x0, matrix products: 12.2 us -> none  [the longest x1 5.06 us: local(): jnp.dot(block_cols, kv_w, preferred_element_type=jnp.float32)]
    all_to_all x4 -> x2, starting transfers between devices: 23.6 us -> 12.5 us  [the longest x1 6.99 us: local(): lax.all_to_all(encoded, 'mp', split_axis=0, concat_axis=0, tiled=True)]
  transfers between devices with their start and end apart: 10 -> 11, of which waited for: 9 -> 7; matrix products, arithmetic and copies ran while one was open for 19% -> 3% of each run, Pallas kernels for 0% -> 1%
where the time goes in v2:
time: 281 us; the launch traced here: 278 us
  waiting for transfers between devices  113 us (40%)
  blocking collectives  82 us (29%)
  starting transfers between devices  35.3 us (13%)
  Pallas kernels  24.2 us (9%)
  between operations  14.3 us (5%)
  local copies, waits for them, and re-layouts  6.98 us (2%)
  other arithmetic  2.88 us (1%)
    all_gather x1, waiting for transfers between devices, local(): lax.all_gather(pair, 'group', axis=0, tiled=True, axis_index_groups=[[z *...  67.2 us
    all_to_all x1, blocking collectives, local(): lax.all_to_all(requests, 'group', split_axis=0, concat_axis=0, tiled=True)  37.8 us
    all_to_all x1, waiting for transfers between devices, local(): lax.all_to_all(encoded, 'mp', split_axis=0, concat_axis=0, tiled=True)  26.9 us
    all_to_all x1, blocking collectives, local(): part = lax.all_to_all(part, 'mp', split_axis=0, concat_axis=0, tiled=True)  25.8 us
    all_to_all x1, blocking collectives, local(): lax.all_to_all(dquery, 'mp', split_axis=0, concat_axis=0, tiled=True)  18.4 us
    ppermute x2, waiting for transfers between devices, local(): lax.ppermute((tokens[:, -1], attended_grad[:, -1]), 'group', onward)  11.3 us
    pallas_call x1, Pallas kernels, local(): pl.pallas_call(functools.partial(attend_kernel, run), grid_spec=pltpu.Pre...  11 us
    all_to_all x1, starting transfers between devices, local(): lax.all_to_all(encoded, 'mp', split_axis=0, concat_axis=0, tiled=True)  6.99 us
  transfers between devices with their start and end apart: 11, of which 7 were waited for; matrix products, arithmetic and copies ran while one was open for 3% of the time, Pallas kernels for 1%

profile of v2, /device:TPU:24, one launch (start us, length us, event | category | flops | bytes accessed | tf_op | source)
XLA Modules:
  0.0 278.3 jit_solution(7443001074633342027)
XLA Ops:
  7.2 6.0 %collective-permute-start.1 = (bf16[64,256]{1,0:T(8,128)(2,1)}, bf16[64,256]{1,0:T(8,128)(2,1)S(1)}, u32[]{:S(2)}, u32[]{:S(2)}) collective-permute-start(bf16[64,256]{1,0:T(8,128)(2,1)} %param.12), channel_id=1, source_target_pairs={{0,0},{1,64},{2,128},{3,192},{4,256},{5,320},{6,384},{7,448},{8,8}... | collective-permute-start | bytes 98312 | tf_op jit(solution)/shard_map/ppermute | solution.py:201
  13.2 3.2 %collective-permute-start.3 = (bf16[64,256]{1,0:T(8,128)(2,1)}, bf16[64,256]{1,0:T(8,128)(2,1)S(1)}, u32[]{:S(2)}, u32[]{:S(2)}) collective-permute-start(bf16[64,256]{1,0:T(8,128)(2,1)} %param.12), channel_id=1, source_target_pairs={{0,16},{1,80},{2,144},{3,208},{4,272},{5,336},{6,400},{7,464},{8,2... | collective-permute-start | bytes 98312 | tf_op jit(solution)/shard_map/ppermute | solution.py:202
  17.2 2.0 collective-permute-start.2
  21.5 2.2 collective-permute-done.2
  25.0 37.8 %all_to_all.37 = s32[64,1,128]{2,1,0:T(1,128)S(1)} all-to-all(s32[64,1,128]{2,1,0:T(1,128)S(1)} %bitcast.26), channel_id=1, replica_groups=mesh['group'=64,'mp'=8] {'group'}, dimensions={0} | all-to-all | bytes 65536 | tf_op jit(solution)/shard_map/all_to_all | solution.py:224
  66.1 5.5 %all-to-all-start.1 = ((bf16[64,2,2304]{2,1,0:T(2,128)(2,1)}), bf16[64,2,2304]{2,1,0:T(2,128)(2,1)S(1)}, u32[]{:S(2)}, u32[]{:S(2)}) async-start(bf16[64,2,2304]{2,1,0:T(2,128)(2,1)} %reshape.23), calls=%async_computation.1 | async-start | bytes 1179648 | tf_op jit(solution)/shard_map/all_to_all | solution.py:230
  71.6 67.2 %all-gather.2.cloned.1.call-done.mine_ref = bf16[2048,1024]{1,0:T(8,128)(2,1)} async-done(((bf16[128,1024]{1,0:T(8,128)(2,1)}), bf16[2048,1024]{1,0:T(8,128)(2,1)}) %all-gather.2.cloned.1.call-update) | async-done | bytes 4194320 | tf_op jit(solution)/shard_map/all_gather | solution.py:207
  138.8 1.9 collective-permute-start.4
  140.7 2.4 collective-permute-start
  143.7 3.7 %collective-permute-done.slot_ref = s32[3,128]{1,0:T(4,128)S(1)} collective-permute-done((s32[3,128]{1,0:T(4,128)S(1)}, s32[3,128]{1,0:T(4,128)S(1)}, u32[]{:S(2)}, u32[]{:S(2)}) %collective-permute-start) | collective-permute-done | bytes 1568 | tf_op jit(solution)/shard_map/ppermute | solution.py:223
  147.5 2.4 shard_map.97
  149.9 7.0 %all-to-all-start.2 = ((bf16[8,384,512]{2,1,0:T(8,128)(2,1)}), bf16[8,384,512]{2,1,0:T(8,128)(2,1)S(1)}, u32[]{:S(2)}, u32[]{:S(2)}) async-start(bf16[8,384,512]{2,1,0:T(8,128)(2,1)} %shard_map.97), calls=%async_computation.2 | async-start | bytes 6291456 | tf_op jit(solution)/shard_map/all_to_all | solution.py:236
  156.9 1.9 collective-permute-start.6
  159.9 3.5 %collective-permute-start.5 = (bf16[3,4096]{1,0:T(4,128)(2,1)S(1)}, bf16[3,4096]{1,0:T(4,128)(2,1)S(1)}, u32[]{:S(2)}, u32[]{:S(2)}) collective-permute-start(bf16[3,4096]{1,0:T(4,128)(2,1)S(1)} %bitcast.29), channel_id=1, source_target_pairs={{0,8},{8,16},{16,24},{24,32},{32,40},{40,48},{48,56},{56,64},{64,7... | collective-permute-start | bytes 73736 | tf_op jit(solution)/shard_map/ppermute | solution.py:213
  163.7 10.6 %collective-permute-done.6.last_grad_ref = bf16[3,256]{1,0:T(4,128)(2,1)S(1)} collective-permute-done((bf16[3,256]{1,0:T(4,128)(2,1)S(1)}, bf16[3,256]{1,0:T(4,128)(2,1)S(1)}, u32[]{:S(2)}, u32[]{:S(2)}) %collective-permute-start.6) | collective-permute-done | bytes 1568 | tf_op jit(solution)/shard_map/ppermute | solution.py:213
  175.0 26.9 %all-to-all-done.2.enc_ref = bf16[8,384,512]{2,1,0:T(8,128)(2,1)S(1)} async-done(((bf16[8,384,512]{2,1,0:T(8,128)(2,1)}), bf16[8,384,512]{2,1,0:T(8,128)(2,1)S(1)}, u32[]{:S(2)}, u32[]{:S(2)}) %all-to-all-start.2) | async-done | bytes 3145760 | tf_op jit(solution)/shard_map/all_to_all | solution.py:236
  201.9 1.4 copy-done
  203.3 11.0 %shard_map.98 = (bf16[3,64,256]{2,1,0:T(8,128)(2,1)S(1)}, bf16[3,64,256]{2,1,0:T(8,128)(2,1)S(1)}) custom-call(s32[4]{0:T(128)S(1)} %pad_add_fusion.scal_ref, bf16[8,384,512]{2,1,0:T(8,128)(2,1)S(1)} %all-to-all-done.2.enc_ref, bf16[2048,1024]{1,0:T(8,128)(2,1)} %all-gather.2.cloned.1.call-done.mine_ref, ...), custom_call_target="tpu_custom_call" | custom-call | tf_op jit(solution)/shard_map/pallas_call | solution.py:246
  214.6 1.9 collective-permute-start.7
  216.5 1.3 collective-permute-done.7.last_ref
  218.5 18.4 %all_to_all.38.dq_ref = bf16[8,192,256]{2,1,0:T(8,128)(2,1)S(1)} all-to-all(bf16[8,192,256]{2,1,0:T(8,128)(2,1)S(1)} %get-tuple-element.13), channel_id=1, replica_groups=mesh['group'=64,'mp'=8] {'mp'}, dimensions={0} | all-to-all | bytes 1572864 | tf_op jit(solution)/shard_map/all_to_all | solution.py:281
  236.9 6.0 %shard_map.100 = bf16[8,192,512]{2,1,0:T(8,128)(2,1)S(1)} custom-call(s32[4]{0:T(128)S(1)} %pad_add_fusion.scal_ref, bf16[8,192,256]{2,1,0:T(8,128)(2,1)S(1)} %all_to_all.38.dq_ref, bf16[2048,1024]{1,0:T(8,128)(2,1)} %all-gather.2.cloned.1.call-done.mine_ref, bf16[2048,1024]{1,0:T(8,128)(2,1)} %collective-permute-done.4.other_ref), custom_call_target="tpu_custom_call" | custom-call | tf_op jit(solution)/shard_map/pallas_call | solution.py:282
  242.9 25.8 %all_to_all.39.in_ref = bf16[8,192,512]{2,1,0:T(8,128)(2,1)S(1)} all-to-all(bf16[8,192,512]{2,1,0:T(8,128)(2,1)S(1)} %shard_map.100), channel_id=1, replica_groups=mesh['group'=64,'mp'=8] {'mp'}, dimensions={0} | all-to-all | bytes 3145728 | tf_op jit(solution)/shard_map/all_to_all | solution.py:298
  268.7 2.8 %shard_map.101 = bf16[192,4096]{1,0:T(8,128)(2,1)} custom-call(bf16[8,192,512]{2,1,0:T(8,128)(2,1)S(1)} %all_to_all.39.in_ref), custom_call_target="tpu_custom_call" | custom-call | tf_op jit(solution)/shard_map/pallas_call | solution.py:299
  (44 shorter events, 11.1 us)
Async XLA Ops:
  7.2 17.4 %copy-start.4 = (s32[1,3,128]{2,0,1:T(1,128)S(1)}, s32[1,3,128]{2,0,1:T(1,128)}, u32[]{:S(2)}) copy-start(s32[1,3,128]{2,0,1:T(1,128)} %param.9) | copy-start | bytes 4612
  7.2 55.6 %copy-start.1 = (bf16[1024,512]{1,0:T(8,128)(2,1)S(1)}, bf16[1024,512]{1,0:T(8,128)(2,1)}, u32[]{:S(2)}) copy-start(bf16[1024,512]{1,0:T(8,128)(2,1)} %table_ref.1) | copy-start | bytes 3145732
  7.2 131.6 %all-gather.2.cloned.1.call-start = ((), (), s32[]{:S(2)}) async-start(), calls=%async_computation.5 | async-start | bytes 4456448 | tf_op jit(solution)/shard_map/all_gather | solution.py:207
  7.2 14.2 %collective-permute-start.1 = (bf16[64,256]{1,0:T(8,128)(2,1)}, bf16[64,256]{1,0:T(8,128)(2,1)S(1)}, u32[]{:S(2)}, u32[]{:S(2)}) collective-permute-start(bf16[64,256]{1,0:T(8,128)(2,1)} %param.12), channel_id=1, source_target_pairs={{0,0},{1,64},{2,128},{3,192},{4,256},{5,320},{6,384},{7,448},{8,8}... | collective-permute-start | bytes 98312 | tf_op jit(solution)/shard_map/ppermute | solution.py:201
  13.2 10.5 %collective-permute-start.3 = (bf16[64,256]{1,0:T(8,128)(2,1)}, bf16[64,256]{1,0:T(8,128)(2,1)S(1)}, u32[]{:S(2)}, u32[]{:S(2)}) collective-permute-start(bf16[64,256]{1,0:T(8,128)(2,1)} %param.12), channel_id=1, source_target_pairs={{0,16},{1,80},{2,144},{3,208},{4,272},{5,336},{6,400},{7,464},{8,2... | collective-permute-start | bytes 98312 | tf_op jit(solution)/shard_map/ppermute | solution.py:202
  17.2 6.5 %collective-permute-start.2 = (bf16[64,768]{1,0:T(8,128)(2,1)S(1)}, bf16[64,768]{1,0:T(8,128)(2,1)S(1)}, u32[]{:S(2)}, u32[]{:S(2)}) collective-permute-start(bf16[64,768]{1,0:T(8,128)(2,1)S(1)} %pad_maximum_fusion.1), channel_id=1, source_target_pairs={{0,16},{8,24},{16,0},{24,8},{32,48},{40,56},{48,32},{56,40},{64,80... | collective-permute-start | bytes 294920 | tf_op jit(solution)/shard_map/ppermute | solution.py:200
  66.1 77.0 %all-to-all-start.1 = ((bf16[64,2,2304]{2,1,0:T(2,128)(2,1)}), bf16[64,2,2304]{2,1,0:T(2,128)(2,1)S(1)}, u32[]{:S(2)}, u32[]{:S(2)}) async-start(bf16[64,2,2304]{2,1,0:T(2,128)(2,1)} %reshape.23), calls=%async_computation.1 | async-start | bytes 1179648 | tf_op jit(solution)/shard_map/all_to_all | solution.py:230
  138.8 63.1 %collective-permute-start.4 = (bf16[2048,1024]{1,0:T(8,128)(2,1)}, bf16[2048,1024]{1,0:T(8,128)(2,1)}, u32[]{:S(2)}, u32[]{:S(2)}) collective-permute-start(bf16[2048,1024]{1,0:T(8,128)(2,1)} %all-gather.2.cloned.1.call-done.mine_ref), channel_id=1, source_target_pairs={{0,8},{8,0},{16,24},{24,16},{32,40},{40,32},{48,56},{56,48},{64,72... | collective-permute-start | bytes 12582920 | tf_op jit(solution)/shard_map/ppermute | solution.py:211
  140.7 6.8 %collective-permute-start = (s32[3,128]{1,0:T(4,128)S(1)}, s32[3,128]{1,0:T(4,128)S(1)}, u32[]{:S(2)}, u32[]{:S(2)}) collective-permute-start(s32[3,128]{1,0:T(4,128)S(1)} %get-tuple-element.8), channel_id=1, source_target_pairs={{0,8},{8,16},{16,24},{24,32},{32,40},{40,48},{48,56},{56,64},{64,7... | collective-permute-start | bytes 4616 | tf_op jit(solution)/shard_map/ppermute | solution.py:223
  149.9 7.0 %copy-start.2 = (bf16[3,64,256]{2,1,0:T(8,128)(2,1)S(1)}, bf16[3,64,256]{2,1,0:T(8,128)(2,1)}, u32[]{:S(2)}) copy-start(bf16[3,64,256]{2,1,0:T(8,128)(2,1)} %grad_ref.1) | copy-start | bytes 294916
  149.9 13.5 %copy-start.3 = (s32[3,64]{1,0:T(4,128)S(1)}, s32[3,64]{1,0:T(4,128)}, u32[]{:S(2)}) copy-start(s32[3,64]{1,0:T(4,128)} %param.10) | copy-start | bytes 2308
  149.9 52.0 %all-to-all-start.2 = ((bf16[8,384,512]{2,1,0:T(8,128)(2,1)}), bf16[8,384,512]{2,1,0:T(8,128)(2,1)S(1)}, u32[]{:S(2)}, u32[]{:S(2)}) async-start(bf16[8,384,512]{2,1,0:T(8,128)(2,1)} %shard_map.97), calls=%async_computation.2 | async-start | bytes 6291456 | tf_op jit(solution)/shard_map/all_to_all | solution.py:236
  156.9 17.3 %collective-permute-start.6 = (bf16[3,256]{1,0:T(4,128)(2,1)S(1)}, bf16[3,256]{1,0:T(4,128)(2,1)S(1)}, u32[]{:S(2)}, u32[]{:S(2)}) collective-permute-start(bf16[3,256]{1,0:T(4,128)(2,1)S(1)} %bitcast.30), channel_id=1, source_target_pairs={{0,8},{8,16},{16,24},{24,32},{32,40},{40,48},{48,56},{56,64},{64,7... | collective-permute-start | bytes 4616 | tf_op jit(solution)/shard_map/ppermute | solution.py:213
  159.9 15.1 %collective-permute-start.5 = (bf16[3,4096]{1,0:T(4,128)(2,1)S(1)}, bf16[3,4096]{1,0:T(4,128)(2,1)S(1)}, u32[]{:S(2)}, u32[]{:S(2)}) collective-permute-start(bf16[3,4096]{1,0:T(4,128)(2,1)S(1)} %bitcast.29), channel_id=1, source_target_pairs={{0,8},{8,16},{16,24},{24,32},{32,40},{40,48},{48,56},{56,64},{64,7... | collective-permute-start | bytes 73736 | tf_op jit(solution)/shard_map/ppermute | solution.py:213
  201.9 1.4 copy-start
  214.6 3.2 %collective-permute-start.7 = (bf16[3,512]{1,0:T(4,128)(2,1)S(1)}, bf16[3,512]{1,0:T(4,128)(2,1)S(1)}, u32[]{:S(2)}, u32[]{:S(2)}) collective-permute-start(bf16[3,512]{1,0:T(4,128)(2,1)S(1)} %pad_maximum_fusion.2), channel_id=1, source_target_pairs={{0,504},{8,0},{16,8},{24,16},{32,24},{40,32},{48,40},{56,48},{64,5... | collective-permute-start | bytes 9224 | tf_op jit(solution)/shard_map/ppermute | solution.py:270
Sparse Core Ops, SparseCore 0:
  24.7 114.1 all-gather.1

commit v3 on v2

v3 whole, which is shorter than its diff:
```python
import functools

import jax
import jax.numpy as jnp
from jax import lax
from jax.experimental import pallas as pl
from jax.experimental.pallas import tpu as pltpu
from jax.sharding import PartitionSpec as P

HEAD_DIM = 128
BF, F32, I32 = jnp.bfloat16, jnp.float32, jnp.int32
PARAMS = pltpu.CompilerParams(vmem_limit_bytes=48 * 1024 * 1024)
NT = (((1,), (1,)), ((), ()))


def iota(shape, dim):
    return lax.broadcasted_iota(I32, shape, dim)


def dot(a, b, dims=(((1,), (0,)), ((), ()))):
    return lax.dot_general(a, b, dims, preferred_element_type=F32)


def bucket_kernel(nchunk, rows_dev, ids_ref, requests_ref, slot_ref):
    seqs, keys = ids_ref.shape
    ids = jnp.concatenate([ids_ref[s : s + 1, :] for s in range(seqs)], axis=1)
    total = seqs * keys
    owner = ids // rows_dev
    lid = ids - owner * rows_dev
    owned = (iota((nchunk, total), 0) == owner).astype(F32)
    owned_bf = owned.astype(BF)
    earlier = (iota((total, total), 0) < iota((total, total), 1)).astype(F32).astype(BF)
    rank = jnp.sum(dot(owned_bf, earlier) * owned, axis=0, keepdims=True).astype(I32)
    placed = iota((128, total), 0) == rank
    high = jnp.where(placed, lid // 32, 0).astype(F32).astype(BF)
    low = jnp.where(placed, lid % 32, 0).astype(F32).astype(BF)
    requests_ref[...] = (dot(owned_bf, high, NT) * 32.0 + dot(owned_bf, low, NT)).astype(I32)
    slot = rank * nchunk + owner
    for s in range(seqs):
        slot_ref[s : s + 1, :] = slot[:, s * keys : (s + 1) * keys]


def fetch_kernel(capacity, asked_ref, table_ref, out_ref):
    nchunk = asked_ref.shape[0]
    rows_dev, feats = table_ref.shape
    asked = pltpu.roll(asked_ref[...], 1, 0)
    lanes = iota((nchunk, rows_dev), 1)
    chosen = jnp.concatenate(
        [(asked[:, s : s + 1] == lanes).astype(F32).astype(BF) for s in range(capacity)], axis=0
    )
    found = dot(chosen, table_ref[...]).astype(BF)
    for s in range(capacity):
        out_ref[:, s * feats : (s + 1) * feats] = found[s * nchunk : (s + 1) * nchunk]


def order_kernel(capacity, slot_ref, rows_ref, one_ref, out_ref):
    seqs, keys = slot_ref.shape
    nchunk = rows_ref.shape[0]
    copies, _, feats = out_ref.shape
    rows = jnp.concatenate(
        [rows_ref[:, s * feats : (s + 1) * feats] for s in range(capacity)], axis=0
    )
    slots = jnp.concatenate([slot_ref[...], jnp.zeros((8 - seqs, keys), I32)], axis=0)
    slots = slots.astype(F32).T.astype(I32)
    lanes = iota((keys, capacity * nchunk), 1)
    for s in range(seqs):
        chosen = (slots[:, s : s + 1] == lanes).astype(F32).astype(BF)
        found = dot(chosen, rows).astype(BF)
        one_ref[s * keys : (s + 1) * keys, :] = found
        for c in range(copies):
            out_ref[c, s * keys : (s + 1) * keys, :] = found


def in_order(weights, run):
    starts = [quad + turn * run for quad in range(0, weights.shape[0], 4 * run) for turn in (0, 2, 1, 3)]
    return jnp.concatenate([weights[start : start + run] for start in starts], axis=0)


def copies_kernel(in_ref, out_ref):
    for c in range(out_ref.shape[0]):
        out_ref[c] = in_ref[...]


def project_kernel(
    run, scal_ref, enc_ref, w_ref, tok_ref, last_tok_ref, q_w_ref, kv_ref, q_ref, kv_acc, q_acc
):
    step, steps = pl.program_id(0), pl.num_programs(0)
    seqs, length, deep = tok_ref.shape

    @pl.when(step == 0)
    def _():
        kv_acc[...] = jnp.zeros_like(kv_acc)
        q_acc[...] = jnp.zeros_like(q_acc)

    is_last = iota((length, deep), 0) == length - 1
    tok = jnp.concatenate(
        [jnp.where(is_last, last_tok_ref[s : s + 1, :], tok_ref[s]) for s in range(seqs)], axis=0
    )
    kv_acc[...] += dot(enc_ref[0], in_order(w_ref[...], run))
    q_acc[...] += dot(tok, in_order(q_w_ref[...], run))

    @pl.when(step == steps - 1)
    def _():
        kv_ref[...] = kv_acc[...]
        q_ref[...] = q_acc[...].astype(BF)


def attend_kernel(
    run, scal_ref, kv_ref, q_ref, enc_ref, w_ref, grad_ref, last_grad_ref, att_ref, dq_ref, kv_acc
):
    step, steps = pl.program_id(0), pl.num_programs(0)
    seqs, length, cols = grad_ref.shape
    keys = kv_acc.shape[0] // seqs

    @pl.when(step == 0)
    def _():
        kv_acc[...] = kv_ref[...]

    kv_acc[...] += dot(enc_ref[0], in_order(w_ref[...], run))

    @pl.when(step == steps - 1)
    def _():
        scale = HEAD_DIM ** (-0.5)
        kv, q = kv_acc[...].astype(BF), q_ref[...]
        last_row = iota((length, HEAD_DIM), 0) == length - 1
        units = [(s, h * HEAD_DIM) for s in range(seqs) for h in range(cols // HEAD_DIM)]
        valid = [last_row | (scal_ref[1 + s] != 0) for s in range(seqs)]
        query = [q[s * length : (s + 1) * length, h : h + HEAD_DIM] for s, h in units]
        key = [kv[s * keys : (s + 1) * keys, h : h + HEAD_DIM] for s, h in units]
        value = [kv[s * keys : (s + 1) * keys, cols + h : cols + h + HEAD_DIM] for s, h in units]
        grad = []
        for s, h in units:
            own = grad_ref[s, :, h : h + HEAD_DIM]
            own = jnp.where(last_row, last_grad_ref[s : s + 1, h : h + HEAD_DIM], own)
            grad.append(jnp.where(valid[s], own, jnp.zeros_like(own)))
        scores = jnp.concatenate([dot(a, b, NT) for a, b in zip(query, key)], axis=0) * scale
        prob_grad = jnp.concatenate([dot(a, b, NT) for a, b in zip(grad, value)], axis=0)
        exps = jnp.exp(scores - jnp.max(scores, axis=-1, keepdims=True))
        prob = exps / jnp.sum(exps, axis=-1, keepdims=True)
        prob_bf = prob.astype(BF)
        mean = jnp.sum(prob * prob_grad, axis=-1, keepdims=True)
        dscore = (prob * (prob_grad - mean) * scale).astype(BF)
        for i, (s, h) in enumerate(units):
            rows = slice(i * length, (i + 1) * length)
            mixed = dot(prob_bf[rows], value[i])
            att_ref[s, :, h : h + HEAD_DIM] = jnp.where(valid[s], mixed, 0.0).astype(BF)
            dq_ref[s, :, h : h + HEAD_DIM] = dot(dscore[rows], key[i]).astype(BF)


def token_kernel(run, att_ref, dq_ref, last_ref, w_ref, att_out, part_ref):
    seqs, length, cols = att_ref.shape
    blocks, _, feats = part_ref.shape
    is_last = iota((length, cols), 0) == length - 1
    rows = jnp.concatenate(
        [jnp.where(is_last, last_ref[s : s + 1, cols:], dq_ref[s]) for s in range(seqs)], axis=0
    )
    for c in range(blocks):
        weights = in_order(w_ref[c * feats : (c + 1) * feats], run)
        part_ref[c] = dot(rows, weights, NT).astype(BF)
    for s in range(seqs):
        att_out[s] = jnp.where(is_last, last_ref[s : s + 1, :cols], att_ref[s])


def sum_kernel(in_ref, out_ref):
    total = in_ref[0].astype(F32)
    for c in range(1, in_ref.shape[0]):
        total = total + in_ref[c].astype(F32)
    rounded = total.astype(BF)
    for c in range(out_ref.shape[0]):
        out_ref[c] = rounded


def join_kernel(in_ref, out_ref):
    feats = in_ref.shape[2]
    for c in range(in_ref.shape[0]):
        out_ref[:, c * feats : (c + 1) * feats] = in_ref[c]


def after(value, *earlier):
    return lax.optimization_barrier((value, earlier))[0]


def local(
    tokens, neighbour_ids, group_document, embed_table, w_query, w_key, w_value, attended_grad
):
    nchunk = lax.axis_size("group")
    mp_size = lax.axis_size("mp")
    group_here = lax.axis_index("group")
    seqs, length, width = tokens.shape
    run, cols = w_query.shape
    keys = neighbour_ids.shape[2]
    id_count = seqs * keys
    rows_dev, feats = embed_table.shape
    capacity = max(2, 3 * id_count // (2 * nchunk))
    onward = [(g, (g + 1) % nchunk) for g in range(nchunk)]
    backward = [(g, (g - 1) % nchunk) for g in range(nchunk)]

    def paired(own, near):
        lower = (group_here // 2) % 2 == 0
        return jnp.concatenate([jnp.where(lower, own, near), jnp.where(lower, near, own)], axis=0)

    def round_z(value):
        groups = [
            [z * 4 + y * 2 + c for z in range(nchunk // 4) for c in range(2)] for y in range(2)
        ]
        return lax.all_gather(value, "group", axis=0, tiled=True, axis_index_groups=groups)

    own = jnp.concatenate([w_key, w_value, w_query], axis=1)
    pair = paired(own, lax.ppermute(own, "group", [(g, g ^ 2) for g in range(nchunk)]))

    last_row = lax.ppermute(
        jnp.concatenate([tokens[:, -1], attended_grad[:, -1]], axis=1), "group", onward
    )

    requests, slot = pl.pallas_call(
        functools.partial(bucket_kernel, nchunk, rows_dev),
        out_shape=[
            jax.ShapeDtypeStruct((nchunk, 128), I32),
            jax.ShapeDtypeStruct((seqs, keys), I32),
        ],
        compiler_params=PARAMS,
    )(neighbour_ids.reshape(seqs, keys))
    slot = lax.ppermute(slot, "group", onward)
    asked = lax.all_to_all(requests, "group", split_axis=0, concat_axis=0, tiled=True)
    weights = round_z(after(pair, asked))
    found = pl.pallas_call(
        functools.partial(fetch_kernel, capacity),
        out_shape=jax.ShapeDtypeStruct((nchunk, capacity * feats), BF),
        compiler_params=PARAMS,
    )(asked, embed_table)
    found = found.reshape(nchunk, 2, -1)
    returned = lax.all_to_all(found, "group", split_axis=0, concat_axis=0, tiled=True)
    returned = after(returned.reshape(nchunk, -1), last_row)
    across_x = mp_size // 2
    along_x = [[2 * x + y for x in range(across_x)] for y in range(2)]
    copies = jax.ShapeDtypeStruct((across_x, id_count, feats), BF)

    def round_x(value):
        return lax.all_to_all(
            value, "mp", split_axis=0, concat_axis=0, tiled=True, axis_index_groups=along_x
        )

    single, encoded = pl.pallas_call(
        functools.partial(order_kernel, capacity),
        out_shape=[jax.ShapeDtypeStruct((id_count, feats), BF), copies],
        compiler_params=PARAMS,
    )(slot, returned)
    single = lax.ppermute(single, "mp", [(m, m ^ 1) for m in range(mp_size)])
    encoded = round_x(encoded)
    encoded_other = round_x(
        pl.pallas_call(copies_kernel, out_shape=copies, compiler_params=PARAMS)(single)
    )

    earlier = jnp.maximum(group_here - 1, 0)
    doc_here = lax.dynamic_slice_in_dim(group_document, group_here, 1, 1)[:, 0]
    doc_before = lax.dynamic_slice_in_dim(group_document, earlier, 1, 1)[:, 0]
    same_doc = (group_here >= 1) & (doc_here == doc_before)
    y_hi = lax.axis_index("mp") % 2
    scalars = jnp.concatenate([y_hi[None].astype(I32), same_doc.astype(I32)])
    whole = lambda *shape: pl.BlockSpec(shape, lambda i, s: (0,) * len(shape))
    kv_part, query = pl.pallas_call(
        functools.partial(project_kernel, run),
        grid_spec=pltpu.PrefetchScalarGridSpec(
            num_scalar_prefetch=1,
            grid=(across_x,),
            in_specs=[
                pl.BlockSpec((1, id_count, feats), lambda i, s: (i, 0, 0)),
                pl.BlockSpec((feats, 2 * cols), lambda i, s: (2 * i + s[0], 0)),
                pl.BlockSpec((seqs, length, 2 * feats), lambda i, s: (0, 0, i)),
                pl.BlockSpec((seqs, 2 * feats), lambda i, s: (0, i)),
                pl.BlockSpec((2 * feats, cols), lambda i, s: (i, 2)),
            ],
            out_specs=[whole(id_count, 2 * cols), whole(seqs * length, cols)],
            scratch_shapes=[
                pltpu.VMEM((id_count, 2 * cols), F32),
                pltpu.VMEM((seqs * length, cols), F32),
            ],
        ),
        out_shape=[
            jax.ShapeDtypeStruct((id_count, 2 * cols), F32),
            jax.ShapeDtypeStruct((seqs * length, cols), BF),
        ],
        compiler_params=PARAMS,
    )(scalars, encoded, weights, tokens, last_row, weights)
    att, dquery = pl.pallas_call(
        functools.partial(attend_kernel, run),
        grid_spec=pltpu.PrefetchScalarGridSpec(
            num_scalar_prefetch=1,
            grid=(across_x,),
            in_specs=[
                whole(id_count, 2 * cols),
                whole(seqs * length, cols),
                pl.BlockSpec((1, id_count, feats), lambda i, s: (i, 0, 0)),
                pl.BlockSpec((feats, 2 * cols), lambda i, s: (2 * i + 1 - s[0], 0)),
                whole(seqs, length, cols),
                pl.BlockSpec((seqs, cols), lambda i, s: (0, width // cols)),
            ],
            out_specs=[whole(seqs, length, cols), whole(seqs, length, cols)],
            scratch_shapes=[pltpu.VMEM((id_count, 2 * cols), F32)],
        ),
        out_shape=[jax.ShapeDtypeStruct((seqs, length, cols), BF)] * 2,
        compiler_params=PARAMS,
    )(scalars, kv_part, query, encoded_other, weights, attended_grad, last_row)

    last = lax.ppermute(
        jnp.concatenate([att[:, -1], dquery[:, -1]], axis=-1), "group", backward
    )
    fixed = lambda *shape: pl.BlockSpec(shape, lambda i: (0,) * len(shape))
    attended, part = pl.pallas_call(
        functools.partial(token_kernel, run),
        grid=(1,),
        in_specs=[
            fixed(seqs, length, cols),
            fixed(seqs, length, cols),
            fixed(seqs, 2 * cols),
            pl.BlockSpec((width, cols), lambda i: (0, 2)),
        ],
        out_specs=[fixed(seqs, length, cols), fixed(mp_size, seqs * length, feats)],
        out_shape=[
            jax.ShapeDtypeStruct((seqs, length, cols), BF),
            jax.ShapeDtypeStruct((mp_size, seqs * length, feats), BF),
        ],
        compiler_params=PARAMS,
    )(att, dquery, last, weights)
    part = lax.all_to_all(part, "mp", split_axis=0, concat_axis=0, tiled=True)
    part = pl.pallas_call(
        sum_kernel,
        out_shape=jax.ShapeDtypeStruct((mp_size, seqs * length, feats), BF),
        compiler_params=PARAMS,
    )(part)
    part = lax.all_to_all(part, "mp", split_axis=0, concat_axis=0, tiled=True)
    token_grad = pl.pallas_call(
        join_kernel,
        grid=(mp_size // 2,),
        in_specs=[pl.BlockSpec((2, seqs * length, feats), lambda i: (i, 0, 0))],
        out_specs=pl.BlockSpec((seqs * length, 2 * feats), lambda i: (0, i)),
        out_shape=jax.ShapeDtypeStruct((seqs * length, width), BF),
        compiler_params=PARAMS,
    )(part)
    return (attended, token_grad.reshape(seqs, length, width))


def solution(mesh):
    in_specs = (
        P(None, "group", None),
        P("group", None, None),
        P(),
        P("group", "mp"),
        P("group", "mp"),
        P("group", "mp"),
        P("group", "mp"),
        P(None, "group", "mp"),
    )
    out_specs = (P(None, "group", "mp"), P(None, "group", None))
    return jax.shard_map(local, mesh=mesh, in_specs=in_specs, out_specs=out_specs, check_vma=False)
```

time: 281 us -> 216 us (0.77)
  waiting for transfers between devices: 113 us -> 75.7 us
  blocking collectives: 82 us -> 52.9 us
  starting transfers between devices: 35.3 us -> 43.3 us
  Pallas kernels: 24.2 us -> 17.3 us
  local copies, waits for them, and re-layouts: 6.98 us -> 9.84 us
    all_gather x1, waiting for transfers between devices: 67.2 us -> 9.9 us  [round_z(): lax.all_gather(value, 'group', axis=0, tiled=True, axis_index_groups=groups)]
    all_to_all x2 -> x0, blocking collectives: 56.2 us -> none  [the longest x1 37.8 us: local(): lax.all_to_all(requests, 'group', split_axis=0, concat_axis=0, tiled=True)]
    all_to_all x1, waiting for transfers between devices: 0.01 us -> 36.3 us  [local(): lax.all_to_all(found, 'group', split_axis=0, concat_axis=0, tiled=True)]
    all_to_all x1 -> x2, blocking collectives: 25.8 us -> 52.9 us  [local(): part = lax.all_to_all(part, 'mp', split_axis=0, concat_axis=0, tiled=True)]
    all_to_all x1 -> x3, starting transfers between devices: 6.99 us -> 25 us  [the longest x1 17.1 us: local(): lax.all_to_all(requests, 'group', split_axis=0, concat_axis=0, tiled=True)]
    ppermute x6 -> x3, starting transfers between devices: 18.5 us -> 7.59 us  [the longest x1 2.89 us: local(): single = lax.ppermute(single, 'mp', [(m, m ^ 1) for m in range(mp_size)])]
    all_to_all x1 -> x3, waiting for transfers between devices: 26.9 us -> 18.4 us  [the longest x1 11.6 us: local(): lax.all_to_all(requests, 'group', split_axis=0, concat_axis=0, tiled=True)]
    pallas_call x1, Pallas kernels: 11 us -> 4.55 us  [local(): pl.pallas_call(functools.partial(attend_kernel, run), grid_spec=pltpu.Pre...]
  transfers between devices with their start and end apart: 11 -> 10, of which waited for: 7 -> 7; matrix products, arithmetic and copies ran while one was open for 3% -> 2% of each run, Pallas kernels for 1% -> 4%
where the time goes in v3:
time: 216 us; the launch traced here: 214 us
  waiting for transfers between devices  75.7 us (35%)
  blocking collectives  52.9 us (24%)
  starting transfers between devices  43.3 us (20%)
  Pallas kernels  17.3 us (8%)
  between operations  14.3 us (7%)
  local copies, waits for them, and re-layouts  9.84 us (5%)
    all_to_all x2, blocking collectives, local(): part = lax.all_to_all(part, 'mp', split_axis=0, concat_axis=0, tiled=True)  52.9 us
    all_to_all x1, waiting for transfers between devices, local(): lax.all_to_all(found, 'group', split_axis=0, concat_axis=0, tiled=True)  36.3 us
    all_to_all x1, starting transfers between devices, local(): lax.all_to_all(requests, 'group', split_axis=0, concat_axis=0, tiled=True)  17.1 us
    all_to_all x1, waiting for transfers between devices, local(): lax.all_to_all(requests, 'group', split_axis=0, concat_axis=0, tiled=True)  11.6 us
    all_gather x1, waiting for transfers between devices, round_z(): lax.all_gather(value, 'group', axis=0, tiled=True, axis_index_groups=groups)  9.9 us
    ppermute x1, waiting for transfers between devices, local(): single = lax.ppermute(single, 'mp', [(m, m ^ 1) for m in range(mp_size)])  9.79 us
    all_to_all x2, starting transfers between devices, round_x(): lax.all_to_all(value, 'mp', split_axis=0, concat_axis=0, tiled=True, axis...  7.87 us
    unnamed x20, local copies, waits for them, and re-layouts  6.96 us
  transfers between devices with their start and end apart: 10, of which 7 were waited for; matrix products, arithmetic and copies ran while one was open for 2% of the time, Pallas kernels for 4%

profile of v3, /device:TPU:24, one launch (start us, length us, event | category | flops | bytes accessed | tf_op | source)
XLA Modules:
  0.0 214.3 jit_solution(11786852483054321779)
XLA Ops:
  9.5 2.6 %collective-permute-start.2 = (bf16[64,768]{1,0:T(8,128)(2,1)S(1)}, bf16[64,768]{1,0:T(8,128)(2,1)S(1)}, u32[]{:S(2)}, u32[]{:S(2)}) collective-permute-start(bf16[64,768]{1,0:T(8,128)(2,1)S(1)} %constant_dynamic-update-slice_fusion), channel_id=1, source_target_pairs={{0,16},{8,24},{16,0},{24,8},{32,48},{40,56},{48,32},{56,40},{64,80... | collective-permute-start | bytes 294920 | tf_op jit(solution)/shard_map/ppermute | solution.py:209
  13.9 17.1 %all-to-all-start = ((s32[64,1,128]{2,1,0:T(1,128)}), s32[64,1,128]{2,1,0:T(1,128)S(1)}, u32[]{:S(2)}, u32[]{:S(2)}) async-start(s32[64,1,128]{2,1,0:T(1,128)} %bitcast.2), calls=%async_computation | async-start | bytes 65536 | tf_op jit(solution)/shard_map/all_to_all | solution.py:224
  31.8 11.6 %all-to-all-done = s32[64,1,128]{2,1,0:T(1,128)S(1)} async-done(((s32[64,1,128]{2,1,0:T(1,128)}), s32[64,1,128]{2,1,0:T(1,128)S(1)}, u32[]{:S(2)}, u32[]{:S(2)}) %all-to-all-start) | async-done | bytes 32800 | tf_op jit(solution)/shard_map/all_to_all | solution.py:224
  45.2 5.5 %all-to-all-start.1 = ((bf16[64,2,2304]{2,1,0:T(2,128)(2,1)}), bf16[64,2,2304]{2,1,0:T(2,128)(2,1)S(1)}, u32[]{:S(2)}, u32[]{:S(2)}) async-start(bf16[64,2,2304]{2,1,0:T(2,128)(2,1)} %reshape.24), calls=%async_computation.1 | async-start | bytes 1179648 | tf_op jit(solution)/shard_map/all_to_all | solution.py:232
  51.8 2.1 collective-permute-start.1
  53.8 3.4 %collective-permute-start = (s32[3,128]{1,0:T(4,128)S(1)}, s32[3,128]{1,0:T(4,128)S(1)}, u32[]{:S(2)}, u32[]{:S(2)}) collective-permute-start(s32[3,128]{1,0:T(4,128)S(1)} %get-tuple-element.14), channel_id=1, source_target_pairs={{0,8},{8,16},{16,24},{24,32},{32,40},{40,48},{48,56},{56,64},{64,7... | collective-permute-start | bytes 4616 | tf_op jit(solution)/shard_map/ppermute | solution.py:223
  57.2 36.3 %all-to-all-done.1 = bf16[64,2,2304]{2,1,0:T(2,128)(2,1)S(1)} async-done(((bf16[64,2,2304]{2,1,0:T(2,128)(2,1)}), bf16[64,2,2304]{2,1,0:T(2,128)(2,1)S(1)}, u32[]{:S(2)}, u32[]{:S(2)}) %all-to-all-start.1) | async-done | bytes 589856 | tf_op jit(solution)/shard_map/all_to_all | solution.py:232
  93.6 1.8 shard_map.97
  95.3 4.3 %all-to-all-start.2 = ((bf16[4,384,512]{2,1,0:T(8,128)(2,1)}), bf16[4,384,512]{2,1,0:T(8,128)(2,1)S(1)}, u32[]{:S(2)}, u32[]{:S(2)}) async-start(bf16[4,384,512]{2,1,0:T(8,128)(2,1)} %get-tuple-element.17), calls=%async_computation.2 | async-start | bytes 3145728 | tf_op jit(solution)/shard_map/all_to_all | solution.py:239
  99.7 2.9 %collective-permute-start.3 = (bf16[384,512]{1,0:T(8,128)(2,1)S(1)}, bf16[384,512]{1,0:T(8,128)(2,1)S(1)}, u32[]{:S(2)}, u32[]{:S(2)}) collective-permute-start(bf16[384,512]{1,0:T(8,128)(2,1)S(1)} %get-tuple-element.21), channel_id=1, source_target_pairs={{0,1},{1,0},{2,3},{3,2},{4,5},{5,4},{6,7},{7,6},{8,9},{9,8},{10,11... | collective-permute-start | bytes 1179656 | tf_op jit(solution)/shard_map/ppermute | solution.py:248
  102.6 9.8 %collective-permute-done.3.in_ref = bf16[384,512]{1,0:T(8,128)(2,1)S(1)} collective-permute-done((bf16[384,512]{1,0:T(8,128)(2,1)S(1)}, bf16[384,512]{1,0:T(8,128)(2,1)S(1)}, u32[]{:S(2)}, u32[]{:S(2)}) %collective-permute-start.3) | collective-permute-done | bytes 393248 | tf_op jit(solution)/shard_map/ppermute | solution.py:248
  113.6 5.5 %all-to-all-done.2.enc_ref = bf16[4,384,512]{2,1,0:T(8,128)(2,1)S(1)} async-done(((bf16[4,384,512]{2,1,0:T(8,128)(2,1)}), bf16[4,384,512]{2,1,0:T(8,128)(2,1)S(1)}, u32[]{:S(2)}, u32[]{:S(2)}) %all-to-all-start.2) | async-done | bytes 1572896 | tf_op jit(solution)/shard_map/all_to_all | solution.py:239
  119.1 3.6 %all-to-all-start.3 = ((bf16[4,384,512]{2,1,0:T(8,128)(2,1)}), bf16[4,384,512]{2,1,0:T(8,128)(2,1)S(1)}, u32[]{:S(2)}, u32[]{:S(2)}) async-start(bf16[4,384,512]{2,1,0:T(8,128)(2,1)} %copy-done), calls=%async_computation.3 | async-start | bytes 3145728 | tf_op jit(solution)/shard_map/all_to_all | solution.py:239
  123.0 9.9 %all-gather.2.cloned.1.call-done.w_ref.q_w_ref = bf16[4096,768]{1,0:T(8,128)(2,1)} async-done(((bf16[128,768]{1,0:T(8,128)(2,1)}), bf16[4096,768]{1,0:T(8,128)(2,1)}) %all-gather.2.cloned.1.call-update) | async-done | bytes 6291472 | tf_op jit(solution)/shard_map/all_gather | solution.py:206
  132.9 1.4 copy-done.1
  134.3 4.7 %shard_map.98 = (f32[384,512]{1,0:T(8,128)S(1)}, bf16[192,256]{1,0:T(8,128)(2,1)S(1)}) custom-call(s32[4]{0:T(128)S(1)} %pad_add_fusion.scal_ref, bf16[4,384,512]{2,1,0:T(8,128)(2,1)S(1)} %all-to-all-done.2.enc_ref, bf16[4096,768]{1,0:T(8,128)(2,1)} %all-gather.2.cloned.1.call-done.w_ref.q_w_ref, bf16[3,64,4096]{2,1,0:T(8,128)(2,1)S(1)} %copy-done.1, ...), custom_call_target="tpu_custom_call" | custom-call | tf_op jit(solution)/shard_map/pallas_call | solution.py:261
  139.8 1.3 all-to-all-done.3.enc_ref
  142.3 4.5 %shard_map.100 = (bf16[3,64,256]{2,1,0:T(8,128)(2,1)S(1)}, bf16[3,64,256]{2,1,0:T(8,128)(2,1)S(1)}) custom-call(s32[4]{0:T(128)S(1)} %pad_add_fusion.scal_ref, f32[384,512]{1,0:T(8,128)S(1)} %copy-done.4, bf16[192,256]{1,0:T(8,128)(2,1)S(1)} %get-tuple-element.20.q_ref, bf16[4,384,512]{2,1,0:T(8,128)(2,1)S(1)} %all-to-all-done.3.enc_ref, ...), custom_call_target="tpu_custom_call" | custom-call | tf_op jit(solution)/shard_map/pallas_call | solution.py:285
  147.1 1.9 collective-permute-start.4
  149.0 1.3 collective-permute-done.4.last_ref
  150.3 2.4 %shard_map.101 = (bf16[3,64,256]{2,1,0:T(8,128)(2,1)}, bf16[8,192,512]{2,1,0:T(8,128)(2,1)S(1)}) custom-call(bf16[3,64,256]{2,1,0:T(8,128)(2,1)S(1)} %get-tuple-element.22.att_ref, bf16[3,64,256]{2,1,0:T(8,128)(2,1)S(1)} %get-tuple-element.23.dq_ref, bf16[3,512]{1,0:T(4,128)(2,1)S(1)} %collective-permute-done.4.last_ref, ...), custom_call_target="tpu_custom_call" | custom-call | tf_op jit(solution)/shard_map/pallas_call | solution.py:309
  152.7 26.1 %all_to_all.36.in_ref = bf16[8,192,512]{2,1,0:T(8,128)(2,1)S(1)} all-to-all(bf16[8,192,512]{2,1,0:T(8,128)(2,1)S(1)} %get-tuple-element.25), channel_id=1, replica_groups=mesh['group'=64,'mp'=8] {'mp'}, dimensions={0} | all-to-all | bytes 3145728 | tf_op jit(solution)/shard_map/all_to_all | solution.py:325
  179.0 26.8 %all_to_all.37.in_ref = bf16[8,192,512]{2,1,0:T(8,128)(2,1)S(1)} all-to-all(bf16[8,192,512]{2,1,0:T(8,128)(2,1)S(1)} %shard_map.102), channel_id=1, replica_groups=mesh['group'=64,'mp'=8] {'mp'}, dimensions={0} | all-to-all | bytes 3145728 | tf_op jit(solution)/shard_map/all_to_all | solution.py:331
  205.8 1.7 shard_map.103
  (41 shorter events, 11.7 us)
Async XLA Ops:
  7.2 36.3 %copy-start.2 = (bf16[1024,512]{1,0:T(8,128)(2,1)S(1)}, bf16[1024,512]{1,0:T(8,128)(2,1)}, u32[]{:S(2)}) copy-start(bf16[1024,512]{1,0:T(8,128)(2,1)} %table_ref.1) | copy-start | bytes 3145732
  9.5 21.5 %collective-permute-start.2 = (bf16[64,768]{1,0:T(8,128)(2,1)S(1)}, bf16[64,768]{1,0:T(8,128)(2,1)S(1)}, u32[]{:S(2)}, u32[]{:S(2)}) collective-permute-start(bf16[64,768]{1,0:T(8,128)(2,1)S(1)} %constant_dynamic-update-slice_fusion), channel_id=1, source_target_pairs={{0,16},{8,24},{16,0},{24,8},{32,48},{40,56},{48,32},{56,40},{64,80... | collective-permute-start | bytes 294920 | tf_op jit(solution)/shard_map/ppermute | solution.py:209
  13.9 29.5 %all-to-all-start = ((s32[64,1,128]{2,1,0:T(1,128)}), s32[64,1,128]{2,1,0:T(1,128)S(1)}, u32[]{:S(2)}, u32[]{:S(2)}) async-start(s32[64,1,128]{2,1,0:T(1,128)} %bitcast.2), calls=%async_computation | async-start | bytes 65536 | tf_op jit(solution)/shard_map/all_to_all | solution.py:224
  31.0 101.9 %all-gather.2.cloned.1.call-start = ((), (), s32[]{:S(2)}) async-start(), calls=%async_computation.6 | async-start | bytes 6488064 | tf_op jit(solution)/shard_map/all_gather | solution.py:206
  44.3 6.4 %copy-start.5 = (bf16[3,64,256]{2,1,0:T(8,128)(2,1)S(1)}, bf16[3,64,256]{2,1,0:T(8,128)(2,1)}, u32[]{:S(2)}) copy-start(bf16[3,64,256]{2,1,0:T(8,128)(2,1)} %grad_ref.1) | copy-start | bytes 294916
  45.2 48.3 %all-to-all-start.1 = ((bf16[64,2,2304]{2,1,0:T(2,128)(2,1)}), bf16[64,2,2304]{2,1,0:T(2,128)(2,1)S(1)}, u32[]{:S(2)}, u32[]{:S(2)}) async-start(bf16[64,2,2304]{2,1,0:T(2,128)(2,1)} %reshape.24), calls=%async_computation.1 | async-start | bytes 1179648 | tf_op jit(solution)/shard_map/all_to_all | solution.py:232
  51.8 41.8 %collective-permute-start.1 = (bf16[3,4352]{1,0:T(4,128)(2,1)S(1)}, bf16[3,4352]{1,0:T(4,128)(2,1)S(1)}, u32[]{:S(2)}, u32[]{:S(2)}) collective-permute-start(bf16[3,4352]{1,0:T(4,128)(2,1)S(1)} %pad_maximum_fusion.1), channel_id=1, source_target_pairs={{0,8},{8,16},{16,24},{24,32},{32,40},{40,48},{48,56},{56,64},{64,7... | collective-permute-start | bytes 78344 | tf_op jit(solution)/shard_map/ppermute | solution.py:211
  53.8 39.7 %collective-permute-start = (s32[3,128]{1,0:T(4,128)S(1)}, s32[3,128]{1,0:T(4,128)S(1)}, u32[]{:S(2)}, u32[]{:S(2)}) collective-permute-start(s32[3,128]{1,0:T(4,128)S(1)} %get-tuple-element.14), channel_id=1, source_target_pairs={{0,8},{8,16},{16,24},{24,32},{32,40},{40,48},{48,56},{56,64},{64,7... | collective-permute-start | bytes 4616 | tf_op jit(solution)/shard_map/ppermute | solution.py:223
  95.3 23.8 %all-to-all-start.2 = ((bf16[4,384,512]{2,1,0:T(8,128)(2,1)}), bf16[4,384,512]{2,1,0:T(8,128)(2,1)S(1)}, u32[]{:S(2)}, u32[]{:S(2)}) async-start(bf16[4,384,512]{2,1,0:T(8,128)(2,1)} %get-tuple-element.17), calls=%async_computation.2 | async-start | bytes 3145728 | tf_op jit(solution)/shard_map/all_to_all | solution.py:239
  99.7 12.7 %collective-permute-start.3 = (bf16[384,512]{1,0:T(8,128)(2,1)S(1)}, bf16[384,512]{1,0:T(8,128)(2,1)S(1)}, u32[]{:S(2)}, u32[]{:S(2)}) collective-permute-start(bf16[384,512]{1,0:T(8,128)(2,1)S(1)} %get-tuple-element.21), channel_id=1, source_target_pairs={{0,1},{1,0},{2,3},{3,2},{4,5},{5,4},{6,7},{7,6},{8,9},{9,8},{10,11... | collective-permute-start | bytes 1179656 | tf_op jit(solution)/shard_map/ppermute | solution.py:248
  112.5 1.1 copy-start
  113.6 9.1 %copy-start.6 = (s32[3,64]{1,0:T(4,128)S(1)}, s32[3,64]{1,0:T(4,128)}, u32[]{:S(2)}) copy-start(s32[3,64]{1,0:T(4,128)} %param.10) | copy-start | bytes 2308
  119.1 22.1 %all-to-all-start.3 = ((bf16[4,384,512]{2,1,0:T(8,128)(2,1)}), bf16[4,384,512]{2,1,0:T(8,128)(2,1)S(1)}, u32[]{:S(2)}, u32[]{:S(2)}) async-start(bf16[4,384,512]{2,1,0:T(8,128)(2,1)} %copy-done), calls=%async_computation.3 | async-start | bytes 3145728 | tf_op jit(solution)/shard_map/all_to_all | solution.py:239
  132.9 1.4 copy-start.1
  139.0 0.9 copy-start.3
  141.2 1.1 copy-start.4
  147.1 3.2 %collective-permute-start.4 = (bf16[3,512]{1,0:T(4,128)(2,1)S(1)}, bf16[3,512]{1,0:T(4,128)(2,1)S(1)}, u32[]{:S(2)}, u32[]{:S(2)}) collective-permute-start(bf16[3,512]{1,0:T(4,128)(2,1)S(1)} %pad_maximum_fusion.2), channel_id=1, source_target_pairs={{0,504},{8,0},{16,8},{24,16},{32,24},{40,32},{48,40},{56,48},{64,5... | collective-permute-start | bytes 9224 | tf_op jit(solution)/shard_map/ppermute | solution.py:305
Sparse Core Ops, SparseCore 0:
  43.5 89.2 all-gather.1

commit v4 on v3

--- a/solution.py
+++ b/solution.py
@@ -82,7 +82,8 @@
 
 
 def project_kernel(
-    run, scal_ref, enc_ref, w_ref, tok_ref, last_tok_ref, q_w_ref, kv_ref, q_ref, kv_acc, q_acc
+    run, scal_ref, enc_ref, w_ref, next_w_ref, tok_ref, last_tok_ref, q_w_ref, kv_ref, q_ref, kv_acc,
+    q_acc,
 ):
     step, steps = pl.program_id(0), pl.num_programs(0)
     seqs, length, deep = tok_ref.shape
@@ -96,7 +97,9 @@
     tok = jnp.concatenate(
         [jnp.where(is_last, last_tok_ref[s : s + 1, :], tok_ref[s]) for s in range(seqs)], axis=0
     )
-    kv_acc[...] += dot(enc_ref[0], in_order(w_ref[...], run))
+    enc = jnp.concatenate([enc_ref[0], enc_ref[1]], axis=1)
+    weights = jnp.concatenate([in_order(w_ref[...], run), in_order(next_w_ref[...], run)], axis=0)
+    kv_acc[...] += dot(enc, weights)
     q_acc[...] += dot(tok, in_order(q_w_ref[...], run))
 
     @pl.when(step == steps - 1)
@@ -106,7 +109,8 @@
 
 
 def attend_kernel(
-    run, scal_ref, kv_ref, q_ref, enc_ref, w_ref, grad_ref, last_grad_ref, att_ref, dq_ref, kv_acc
+    run, scal_ref, kv_ref, q_ref, enc_ref, w_ref, next_w_ref, grad_ref, last_grad_ref, att_ref, dq_ref,
+    kv_acc,
 ):
     step, steps = pl.program_id(0), pl.num_programs(0)
     seqs, length, cols = grad_ref.shape
@@ -116,7 +120,9 @@
     def _():
         kv_acc[...] = kv_ref[...]
 
-    kv_acc[...] += dot(enc_ref[0], in_order(w_ref[...], run))
+    enc = jnp.concatenate([enc_ref[0], enc_ref[1]], axis=1)
+    weights = jnp.concatenate([in_order(w_ref[...], run), in_order(next_w_ref[...], run)], axis=0)
+    kv_acc[...] += dot(enc, weights)
 
     @pl.when(step == steps - 1)
     def _():
@@ -205,7 +211,11 @@
         ]
         return lax.all_gather(value, "group", axis=0, tiled=True, axis_index_groups=groups)
 
-    own = jnp.concatenate([w_key, w_value, w_query], axis=1)
+    zero = jnp.zeros((), BF)
+    own = sum(
+        lax.pad(block, zero, ((0, 0, 0), (i * cols, (2 - i) * cols, 0)))
+        for i, block in enumerate((w_key, w_value, w_query))
+    )
     pair = paired(own, lax.ppermute(own, "group", [(g, g ^ 2) for g in range(nchunk)]))
 
     last_row = lax.ppermute(
@@ -262,13 +272,14 @@
         functools.partial(project_kernel, run),
         grid_spec=pltpu.PrefetchScalarGridSpec(
             num_scalar_prefetch=1,
-            grid=(across_x,),
+            grid=(across_x // 2,),
             in_specs=[
-                pl.BlockSpec((1, id_count, feats), lambda i, s: (i, 0, 0)),
-                pl.BlockSpec((feats, 2 * cols), lambda i, s: (2 * i + s[0], 0)),
-                pl.BlockSpec((seqs, length, 2 * feats), lambda i, s: (0, 0, i)),
-                pl.BlockSpec((seqs, 2 * feats), lambda i, s: (0, i)),
-                pl.BlockSpec((2 * feats, cols), lambda i, s: (i, 2)),
+                pl.BlockSpec((2, id_count, feats), lambda i, s: (i, 0, 0)),
+                pl.BlockSpec((feats, 2 * cols), lambda i, s: (4 * i + s[0], 0)),
+                pl.BlockSpec((feats, 2 * cols), lambda i, s: (4 * i + 2 + s[0], 0)),
+                pl.BlockSpec((seqs, length, 4 * feats), lambda i, s: (0, 0, i)),
+                pl.BlockSpec((seqs, 4 * feats), lambda i, s: (0, i)),
+                pl.BlockSpec((4 * feats, cols), lambda i, s: (i, 2)),
             ],
             out_specs=[whole(id_count, 2 * cols), whole(seqs * length, cols)],
             scratch_shapes=[
@@ -281,17 +292,18 @@
             jax.ShapeDtypeStruct((seqs * length, cols), BF),
         ],
         compiler_params=PARAMS,
-    )(scalars, encoded, weights, tokens, last_row, weights)
+    )(scalars, encoded, weights, weights, tokens, last_row, weights)
     att, dquery = pl.pallas_call(
         functools.partial(attend_kernel, run),
         grid_spec=pltpu.PrefetchScalarGridSpec(
             num_scalar_prefetch=1,
-            grid=(across_x,),
+            grid=(across_x // 2,),
             in_specs=[
                 whole(id_count, 2 * cols),
                 whole(seqs * length, cols),
-                pl.BlockSpec((1, id_count, feats), lambda i, s: (i, 0, 0)),
-                pl.BlockSpec((feats, 2 * cols), lambda i, s: (2 * i + 1 - s[0], 0)),
+                pl.BlockSpec((2, id_count, feats), lambda i, s: (i, 0, 0)),
+                pl.BlockSpec((feats, 2 * cols), lambda i, s: (4 * i + 1 - s[0], 0)),
+                pl.BlockSpec((feats, 2 * cols), lambda i, s: (4 * i + 3 - s[0], 0)),
                 whole(seqs, length, cols),
                 pl.BlockSpec((seqs, cols), lambda i, s: (0, width // cols)),
             ],
@@ -300,7 +312,7 @@
         ),
         out_shape=[jax.ShapeDtypeStruct((seqs, length, cols), BF)] * 2,
         compiler_params=PARAMS,
-    )(scalars, kv_part, query, encoded_other, weights, attended_grad, last_row)
+    )(scalars, kv_part, query, encoded_other, weights, weights, attended_grad, last_row)
 
     last = lax.ppermute(
         jnp.concatenate([att[:, -1], dquery[:, -1]], axis=-1), "group", backward

time: 216 us -> 213 us (0.986)
  local copies, waits for them, and re-layouts: 9.84 us -> 7.47 us
    unnamed x20 -> x18, local copies, waits for them, and re-layouts: 6.96 us -> 5.35 us
where the time goes in v4:
time: 213 us; the launch traced here: 211 us
  waiting for transfers between devices  75.7 us (36%)
  blocking collectives  52.3 us (25%)
  starting transfers between devices  43.3 us (20%)
  Pallas kernels  15.6 us (7%)
  between operations  14.3 us (7%)
  local copies, waits for them, and re-layouts  7.47 us (4%)
  other arithmetic  2.73 us (1%)
    all_to_all x2, blocking collectives, local(): part = lax.all_to_all(part, 'mp', split_axis=0, concat_axis=0, tiled=True)  52.3 us
    all_to_all x1, waiting for transfers between devices, local(): lax.all_to_all(found, 'group', split_axis=0, concat_axis=0, tiled=True)  36.3 us
    all_to_all x1, starting transfers between devices, local(): lax.all_to_all(requests, 'group', split_axis=0, concat_axis=0, tiled=True)  17.1 us
    all_to_all x1, waiting for transfers between devices, local(): lax.all_to_all(requests, 'group', split_axis=0, concat_axis=0, tiled=True)  10.7 us
    all_gather x1, waiting for transfers between devices, round_z(): lax.all_gather(value, 'group', axis=0, tiled=True, axis_index_groups=groups)  9.9 us
    ppermute x1, waiting for transfers between devices, local(): single = lax.ppermute(single, 'mp', [(m, m ^ 1) for m in range(mp_size)])  9.79 us
    all_to_all x2, starting transfers between devices, round_x(): lax.all_to_all(value, 'mp', split_axis=0, concat_axis=0, tiled=True, axis...  7.88 us
    all_to_all x2, waiting for transfers between devices, round_x(): lax.all_to_all(value, 'mp', split_axis=0, concat_axis=0, tiled=True, axis...  7.62 us
  transfers between devices with their start and end apart: 10, of which 7 were waited for; matrix products, arithmetic and copies ran while one was open for 2% of the time, Pallas kernels for 4%

profile of v4, /device:TPU:24, one launch (start us, length us, event | category | flops | bytes accessed | tf_op | source)
XLA Modules:
  0.0 211.4 jit_solution(17542440751794551846)
XLA Ops:
  8.1 2.6 %collective-permute-start.2 = (bf16[64,768]{1,0:T(8,128)(2,1)S(1)}, bf16[64,768]{1,0:T(8,128)(2,1)S(1)}, u32[]{:S(2)}, u32[]{:S(2)}) collective-permute-start(bf16[64,768]{1,0:T(8,128)(2,1)S(1)} %pad_add_fusion), channel_id=1, source_target_pairs={{0,16},{8,24},{16,0},{24,8},{32,48},{40,56},{48,32},{56,40},{64,80... | collective-permute-start | bytes 294920 | tf_op jit(solution)/shard_map/ppermute | solution.py:219
  12.4 17.1 %all-to-all-start = ((s32[64,1,128]{2,1,0:T(1,128)}), s32[64,1,128]{2,1,0:T(1,128)S(1)}, u32[]{:S(2)}, u32[]{:S(2)}) async-start(s32[64,1,128]{2,1,0:T(1,128)} %bitcast.2), calls=%async_computation | async-start | bytes 65536 | tf_op jit(solution)/shard_map/all_to_all | solution.py:234
  31.2 10.7 %all-to-all-done = s32[64,1,128]{2,1,0:T(1,128)S(1)} async-done(((s32[64,1,128]{2,1,0:T(1,128)}), s32[64,1,128]{2,1,0:T(1,128)S(1)}, u32[]{:S(2)}, u32[]{:S(2)}) %all-to-all-start) | async-done | bytes 32800 | tf_op jit(solution)/shard_map/all_to_all | solution.py:234
  43.7 5.5 %all-to-all-start.1 = ((bf16[64,2,2304]{2,1,0:T(2,128)(2,1)}), bf16[64,2,2304]{2,1,0:T(2,128)(2,1)S(1)}, u32[]{:S(2)}, u32[]{:S(2)}) async-start(bf16[64,2,2304]{2,1,0:T(2,128)(2,1)} %reshape.24), calls=%async_computation.1 | async-start | bytes 1179648 | tf_op jit(solution)/shard_map/all_to_all | solution.py:242
  50.3 2.1 collective-permute-start.1
  52.4 3.4 %collective-permute-start = (s32[3,128]{1,0:T(4,128)S(1)}, s32[3,128]{1,0:T(4,128)S(1)}, u32[]{:S(2)}, u32[]{:S(2)}) collective-permute-start(s32[3,128]{1,0:T(4,128)S(1)} %get-tuple-element.14), channel_id=1, source_target_pairs={{0,8},{8,16},{16,24},{24,32},{32,40},{40,48},{48,56},{56,64},{64,7... | collective-permute-start | bytes 4616 | tf_op jit(solution)/shard_map/ppermute | solution.py:233
  55.7 36.3 %all-to-all-done.1 = bf16[64,2,2304]{2,1,0:T(2,128)(2,1)S(1)} async-done(((bf16[64,2,2304]{2,1,0:T(2,128)(2,1)}), bf16[64,2,2304]{2,1,0:T(2,128)(2,1)S(1)}, u32[]{:S(2)}, u32[]{:S(2)}) %all-to-all-start.1) | async-done | bytes 589856 | tf_op jit(solution)/shard_map/all_to_all | solution.py:242
  92.1 1.8 shard_map.97
  93.9 4.3 %all-to-all-start.2 = ((bf16[4,384,512]{2,1,0:T(8,128)(2,1)}), bf16[4,384,512]{2,1,0:T(8,128)(2,1)S(1)}, u32[]{:S(2)}, u32[]{:S(2)}) async-start(bf16[4,384,512]{2,1,0:T(8,128)(2,1)} %get-tuple-element.17), calls=%async_computation.2 | async-start | bytes 3145728 | tf_op jit(solution)/shard_map/all_to_all | solution.py:249
  98.2 2.9 %collective-permute-start.3 = (bf16[384,512]{1,0:T(8,128)(2,1)S(1)}, bf16[384,512]{1,0:T(8,128)(2,1)S(1)}, u32[]{:S(2)}, u32[]{:S(2)}) collective-permute-start(bf16[384,512]{1,0:T(8,128)(2,1)S(1)} %get-tuple-element.21), channel_id=1, source_target_pairs={{0,1},{1,0},{2,3},{3,2},{4,5},{5,4},{6,7},{7,6},{8,9},{9,8},{10,11... | collective-permute-start | bytes 1179656 | tf_op jit(solution)/shard_map/ppermute | solution.py:258
  101.1 9.8 %collective-permute-done.3.in_ref = bf16[384,512]{1,0:T(8,128)(2,1)S(1)} collective-permute-done((bf16[384,512]{1,0:T(8,128)(2,1)S(1)}, bf16[384,512]{1,0:T(8,128)(2,1)S(1)}, u32[]{:S(2)}, u32[]{:S(2)}) %collective-permute-start.3) | collective-permute-done | bytes 393248 | tf_op jit(solution)/shard_map/ppermute | solution.py:258
  112.1 5.5 %all-to-all-done.2.enc_ref = bf16[4,384,512]{2,1,0:T(8,128)(2,1)S(1)} async-done(((bf16[4,384,512]{2,1,0:T(8,128)(2,1)}), bf16[4,384,512]{2,1,0:T(8,128)(2,1)S(1)}, u32[]{:S(2)}, u32[]{:S(2)}) %all-to-all-start.2) | async-done | bytes 1572896 | tf_op jit(solution)/shard_map/all_to_all | solution.py:249
  117.6 3.6 %all-to-all-start.3 = ((bf16[4,384,512]{2,1,0:T(8,128)(2,1)}), bf16[4,384,512]{2,1,0:T(8,128)(2,1)S(1)}, u32[]{:S(2)}, u32[]{:S(2)}) async-start(bf16[4,384,512]{2,1,0:T(8,128)(2,1)} %copy-done), calls=%async_computation.3 | async-start | bytes 3145728 | tf_op jit(solution)/shard_map/all_to_all | solution.py:249
  121.5 9.9 %all-gather.2.cloned.1.call-done.w_ref.next_w_ref.q_w_ref = bf16[4096,768]{1,0:T(8,128)(2,1)} async-done(((bf16[128,768]{1,0:T(8,128)(2,1)}), bf16[4096,768]{1,0:T(8,128)(2,1)}) %all-gather.2.cloned.1.call-update) | async-done | bytes 6291472 | tf_op jit(solution)/shard_map/all_gather | solution.py:212
  131.4 1.4 copy-done.1
  132.8 3.9 %shard_map.98 = (f32[384,512]{1,0:T(8,128)S(1)}, bf16[192,256]{1,0:T(8,128)(2,1)S(1)}) custom-call(s32[4]{0:T(128)S(1)} %pad_add_fusion.1.scal_ref, bf16[4,384,512]{2,1,0:T(8,128)(2,1)S(1)} %all-to-all-done.2.enc_ref, bf16[4096,768]{1,0:T(8,128)(2,1)} %all-gather.2.cloned.1.call-done.w_ref.next_w_ref.q_w_ref, ...), custom_call_target="tpu_custom_call" | custom-call | tf_op jit(solution)/shard_map/pallas_call | solution.py:271
  137.5 2.1 %all-to-all-done.3.enc_ref = bf16[4,384,512]{2,1,0:T(8,128)(2,1)S(1)} async-done(((bf16[4,384,512]{2,1,0:T(8,128)(2,1)}), bf16[4,384,512]{2,1,0:T(8,128)(2,1)S(1)}, u32[]{:S(2)}, u32[]{:S(2)}) %all-to-all-start.3) | async-done | bytes 1572896 | tf_op jit(solution)/shard_map/all_to_all | solution.py:249
  140.8 3.7 %shard_map.100 = (bf16[3,64,256]{2,1,0:T(8,128)(2,1)S(1)}, bf16[3,64,256]{2,1,0:T(8,128)(2,1)S(1)}) custom-call(s32[4]{0:T(128)S(1)} %pad_add_fusion.1.scal_ref, f32[384,512]{1,0:T(8,128)S(1)} %copy-done.4, bf16[192,256]{1,0:T(8,128)(2,1)S(1)} %get-tuple-element.20.q_ref, bf16[4,384,512]{2,1,0:T(8,128)(2,1)S(1)} %all-to-all-done.3.enc_ref, ...), custom_call_target="tpu_custom_call" | custom-call | tf_op jit(solution)/shard_map/pallas_call | solution.py:296
  144.7 1.9 collective-permute-start.4
  146.6 1.3 collective-permute-done.4.last_ref
  147.9 2.4 %shard_map.101 = (bf16[3,64,256]{2,1,0:T(8,128)(2,1)}, bf16[8,192,512]{2,1,0:T(8,128)(2,1)S(1)}) custom-call(bf16[3,64,256]{2,1,0:T(8,128)(2,1)S(1)} %get-tuple-element.22.att_ref, bf16[3,64,256]{2,1,0:T(8,128)(2,1)S(1)} %get-tuple-element.23.dq_ref, bf16[3,512]{1,0:T(4,128)(2,1)S(1)} %collective-permute-done.4.last_ref, ...), custom_call_target="tpu_custom_call" | custom-call | tf_op jit(solution)/shard_map/pallas_call | solution.py:321
  150.4 25.8 %all_to_all.36.in_ref = bf16[8,192,512]{2,1,0:T(8,128)(2,1)S(1)} all-to-all(bf16[8,192,512]{2,1,0:T(8,128)(2,1)S(1)} %get-tuple-element.25), channel_id=1, replica_groups=mesh['group'=64,'mp'=8] {'mp'}, dimensions={0} | all-to-all | bytes 3145728 | tf_op jit(solution)/shard_map/all_to_all | solution.py:337
  176.4 26.5 %all_to_all.37.in_ref = bf16[8,192,512]{2,1,0:T(8,128)(2,1)S(1)} all-to-all(bf16[8,192,512]{2,1,0:T(8,128)(2,1)S(1)} %shard_map.102), channel_id=1, replica_groups=mesh['group'=64,'mp'=8] {'mp'}, dimensions={0} | all-to-all | bytes 3145728 | tf_op jit(solution)/shard_map/all_to_all | solution.py:343
  202.9 1.7 shard_map.103
  (39 shorter events, 11.0 us)
Async XLA Ops:
  7.2 34.8 %copy-start.2 = (bf16[1024,512]{1,0:T(8,128)(2,1)S(1)}, bf16[1024,512]{1,0:T(8,128)(2,1)}, u32[]{:S(2)}) copy-start(bf16[1024,512]{1,0:T(8,128)(2,1)} %table_ref.1) | copy-start | bytes 3145732
  8.1 21.5 %collective-permute-start.2 = (bf16[64,768]{1,0:T(8,128)(2,1)S(1)}, bf16[64,768]{1,0:T(8,128)(2,1)S(1)}, u32[]{:S(2)}, u32[]{:S(2)}) collective-permute-start(bf16[64,768]{1,0:T(8,128)(2,1)S(1)} %pad_add_fusion), channel_id=1, source_target_pairs={{0,16},{8,24},{16,0},{24,8},{32,48},{40,56},{48,32},{56,40},{64,80... | collective-permute-start | bytes 294920 | tf_op jit(solution)/shard_map/ppermute | solution.py:219
  12.4 29.5 %all-to-all-start = ((s32[64,1,128]{2,1,0:T(1,128)}), s32[64,1,128]{2,1,0:T(1,128)S(1)}, u32[]{:S(2)}, u32[]{:S(2)}) async-start(s32[64,1,128]{2,1,0:T(1,128)} %bitcast.2), calls=%async_computation | async-start | bytes 65536 | tf_op jit(solution)/shard_map/all_to_all | solution.py:234
  29.5 101.9 %all-gather.2.cloned.1.call-start = ((), (), s32[]{:S(2)}) async-start(), calls=%async_computation.6 | async-start | bytes 6488064 | tf_op jit(solution)/shard_map/all_gather | solution.py:212
  42.8 6.4 %copy-start.5 = (bf16[3,64,256]{2,1,0:T(8,128)(2,1)S(1)}, bf16[3,64,256]{2,1,0:T(8,128)(2,1)}, u32[]{:S(2)}) copy-start(bf16[3,64,256]{2,1,0:T(8,128)(2,1)} %grad_ref.1) | copy-start | bytes 294916
  43.7 48.3 %all-to-all-start.1 = ((bf16[64,2,2304]{2,1,0:T(2,128)(2,1)}), bf16[64,2,2304]{2,1,0:T(2,128)(2,1)S(1)}, u32[]{:S(2)}, u32[]{:S(2)}) async-start(bf16[64,2,2304]{2,1,0:T(2,128)(2,1)} %reshape.24), calls=%async_computation.1 | async-start | bytes 1179648 | tf_op jit(solution)/shard_map/all_to_all | solution.py:242
  50.3 41.8 %collective-permute-start.1 = (bf16[3,4352]{1,0:T(4,128)(2,1)S(1)}, bf16[3,4352]{1,0:T(4,128)(2,1)S(1)}, u32[]{:S(2)}, u32[]{:S(2)}) collective-permute-start(bf16[3,4352]{1,0:T(4,128)(2,1)S(1)} %pad_maximum_fusion.1), channel_id=1, source_target_pairs={{0,8},{8,16},{16,24},{24,32},{32,40},{40,48},{48,56},{56,64},{64,7... | collective-permute-start | bytes 78344 | tf_op jit(solution)/shard_map/ppermute | solution.py:221
  52.4 39.7 %collective-permute-start = (s32[3,128]{1,0:T(4,128)S(1)}, s32[3,128]{1,0:T(4,128)S(1)}, u32[]{:S(2)}, u32[]{:S(2)}) collective-permute-start(s32[3,128]{1,0:T(4,128)S(1)} %get-tuple-element.14), channel_id=1, source_target_pairs={{0,8},{8,16},{16,24},{24,32},{32,40},{40,48},{48,56},{56,64},{64,7... | collective-permute-start | bytes 4616 | tf_op jit(solution)/shard_map/ppermute | solution.py:233
  93.9 23.8 %all-to-all-start.2 = ((bf16[4,384,512]{2,1,0:T(8,128)(2,1)}), bf16[4,384,512]{2,1,0:T(8,128)(2,1)S(1)}, u32[]{:S(2)}, u32[]{:S(2)}) async-start(bf16[4,384,512]{2,1,0:T(8,128)(2,1)} %get-tuple-element.17), calls=%async_computation.2 | async-start | bytes 3145728 | tf_op jit(solution)/shard_map/all_to_all | solution.py:249
  98.2 12.7 %collective-permute-start.3 = (bf16[384,512]{1,0:T(8,128)(2,1)S(1)}, bf16[384,512]{1,0:T(8,128)(2,1)S(1)}, u32[]{:S(2)}, u32[]{:S(2)}) collective-permute-start(bf16[384,512]{1,0:T(8,128)(2,1)S(1)} %get-tuple-element.21), channel_id=1, source_target_pairs={{0,1},{1,0},{2,3},{3,2},{4,5},{5,4},{6,7},{7,6},{8,9},{9,8},{10,11... | collective-permute-start | bytes 1179656 | tf_op jit(solution)/shard_map/ppermute | solution.py:258
  111.0 1.1 copy-start
  112.1 9.1 %copy-start.6 = (s32[3,64]{1,0:T(4,128)S(1)}, s32[3,64]{1,0:T(4,128)}, u32[]{:S(2)}) copy-start(s32[3,64]{1,0:T(4,128)} %param.10) | copy-start | bytes 2308
  117.6 22.1 %all-to-all-start.3 = ((bf16[4,384,512]{2,1,0:T(8,128)(2,1)}), bf16[4,384,512]{2,1,0:T(8,128)(2,1)S(1)}, u32[]{:S(2)}, u32[]{:S(2)}) async-start(bf16[4,384,512]{2,1,0:T(8,128)(2,1)} %copy-done), calls=%async_computation.3 | async-start | bytes 3145728 | tf_op jit(solution)/shard_map/all_to_all | solution.py:249
  131.4 1.4 copy-start.1
  136.7 0.9 copy-start.3
  139.7 1.1 copy-start.4
  144.7 3.2 %collective-permute-start.4 = (bf16[3,512]{1,0:T(4,128)(2,1)S(1)}, bf16[3,512]{1,0:T(4,128)(2,1)S(1)}, u32[]{:S(2)}, u32[]{:S(2)}) collective-permute-start(bf16[3,512]{1,0:T(4,128)(2,1)S(1)} %pad_maximum_fusion.2), channel_id=1, source_target_pairs={{0,504},{8,0},{16,8},{24,16},{32,24},{40,32},{48,40},{56,48},{64,5... | collective-permute-start | bytes 9224 | tf_op jit(solution)/shard_map/ppermute | solution.py:317
Sparse Core Ops, SparseCore 0:
  42.1 89.2 all-gather.1

commit v5 on v3

--- a/solution.py
+++ b/solution.py
@@ -81,32 +81,28 @@
         out_ref[c] = in_ref[...]
 
 
-def project_kernel(
-    run, scal_ref, enc_ref, w_ref, tok_ref, last_tok_ref, q_w_ref, kv_ref, q_ref, kv_acc, q_acc
-):
+def project_kernel(run, tok_ref, last_tok_ref, q_w_ref, q_ref, q_acc):
     step, steps = pl.program_id(0), pl.num_programs(0)
     seqs, length, deep = tok_ref.shape
 
     @pl.when(step == 0)
     def _():
-        kv_acc[...] = jnp.zeros_like(kv_acc)
         q_acc[...] = jnp.zeros_like(q_acc)
 
     is_last = iota((length, deep), 0) == length - 1
     tok = jnp.concatenate(
         [jnp.where(is_last, last_tok_ref[s : s + 1, :], tok_ref[s]) for s in range(seqs)], axis=0
     )
-    kv_acc[...] += dot(enc_ref[0], in_order(w_ref[...], run))
     q_acc[...] += dot(tok, in_order(q_w_ref[...], run))
 
     @pl.when(step == steps - 1)
     def _():
-        kv_ref[...] = kv_acc[...]
         q_ref[...] = q_acc[...].astype(BF)
 
 
 def attend_kernel(
-    run, scal_ref, kv_ref, q_ref, enc_ref, w_ref, grad_ref, last_grad_ref, att_ref, dq_ref, kv_acc
+    run, scal_ref, q_ref, enc_ref, other_ref, w_ref, next_w_ref, grad_ref, last_grad_ref, att_ref, dq_ref,
+    kv_acc,
 ):
     step, steps = pl.program_id(0), pl.num_programs(0)
     seqs, length, cols = grad_ref.shape
@@ -114,9 +110,20 @@
 
     @pl.when(step == 0)
     def _():
-        kv_acc[...] = kv_ref[...]
-
-    kv_acc[...] += dot(enc_ref[0], in_order(w_ref[...], run))
+        kv_acc[...] = jnp.zeros_like(kv_acc)
+
+    def add(ref):
+        enc = jnp.concatenate([ref[0], ref[1]], axis=1)
+        weights = jnp.concatenate([in_order(w_ref[...], run), in_order(next_w_ref[...], run)], axis=0)
+        kv_acc[...] += dot(enc, weights)
+
+    @pl.when(step < steps // 2)
+    def _():
+        add(enc_ref)
+
+    @pl.when(step >= steps // 2)
+    def _():
+        add(other_ref)
 
     @pl.when(step == steps - 1)
     def _():
@@ -205,7 +212,11 @@
         ]
         return lax.all_gather(value, "group", axis=0, tiled=True, axis_index_groups=groups)
 
-    own = jnp.concatenate([w_key, w_value, w_query], axis=1)
+    zero = jnp.zeros((), BF)
+    own = sum(
+        lax.pad(block, zero, ((0, 0, 0), (i * cols, (2 - i) * cols, 0)))
+        for i, block in enumerate((w_key, w_value, w_query))
+    )
     pair = paired(own, lax.ppermute(own, "group", [(g, g ^ 2) for g in range(nchunk)]))
 
     last_row = lax.ppermute(
@@ -258,40 +269,34 @@
     y_hi = lax.axis_index("mp") % 2
     scalars = jnp.concatenate([y_hi[None].astype(I32), same_doc.astype(I32)])
     whole = lambda *shape: pl.BlockSpec(shape, lambda i, s: (0,) * len(shape))
-    kv_part, query = pl.pallas_call(
+    query = pl.pallas_call(
         functools.partial(project_kernel, run),
-        grid_spec=pltpu.PrefetchScalarGridSpec(
-            num_scalar_prefetch=1,
-            grid=(across_x,),
-            in_specs=[
-                pl.BlockSpec((1, id_count, feats), lambda i, s: (i, 0, 0)),
-                pl.BlockSpec((feats, 2 * cols), lambda i, s: (2 * i + s[0], 0)),
-                pl.BlockSpec((seqs, length, 2 * feats), lambda i, s: (0, 0, i)),
-                pl.BlockSpec((seqs, 2 * feats), lambda i, s: (0, i)),
-                pl.BlockSpec((2 * feats, cols), lambda i, s: (i, 2)),
-            ],
-            out_specs=[whole(id_count, 2 * cols), whole(seqs * length, cols)],
-            scratch_shapes=[
-                pltpu.VMEM((id_count, 2 * cols), F32),
-                pltpu.VMEM((seqs * length, cols), F32),
-            ],
-        ),
-        out_shape=[
-            jax.ShapeDtypeStruct((id_count, 2 * cols), F32),
-            jax.ShapeDtypeStruct((seqs * length, cols), BF),
+        grid=(across_x // 2,),
+        in_specs=[
+            pl.BlockSpec((seqs, length, 4 * feats), lambda i: (0, 0, i)),
+            pl.BlockSpec((seqs, 4 * feats), lambda i: (0, i)),
+            pl.BlockSpec((4 * feats, cols), lambda i: (i, 2)),
         ],
-        compiler_params=PARAMS,
-    )(scalars, encoded, weights, tokens, last_row, weights)
+        out_specs=pl.BlockSpec((seqs * length, cols), lambda i: (0, 0)),
+        out_shape=jax.ShapeDtypeStruct((seqs * length, cols), BF),
+        scratch_shapes=[pltpu.VMEM((seqs * length, cols), F32)],
+        compiler_params=PARAMS,
+    )(tokens, last_row, weights)
+
+    def block(i, s):
+        return 4 * (i % 2) + s[0] + (i // 2) * (1 - 2 * s[0])
+
     att, dquery = pl.pallas_call(
         functools.partial(attend_kernel, run),
         grid_spec=pltpu.PrefetchScalarGridSpec(
             num_scalar_prefetch=1,
             grid=(across_x,),
             in_specs=[
-                whole(id_count, 2 * cols),
                 whole(seqs * length, cols),
-                pl.BlockSpec((1, id_count, feats), lambda i, s: (i, 0, 0)),
-                pl.BlockSpec((feats, 2 * cols), lambda i, s: (2 * i + 1 - s[0], 0)),
+                pl.BlockSpec((2, id_count, feats), lambda i, s: (jnp.minimum(i, 1), 0, 0)),
+                pl.BlockSpec((2, id_count, feats), lambda i, s: (jnp.maximum(i - 2, 0), 0, 0)),
+                pl.BlockSpec((feats, 2 * cols), lambda i, s: (block(i, s), 0)),
+                pl.BlockSpec((feats, 2 * cols), lambda i, s: (block(i, s) + 2, 0)),
                 whole(seqs, length, cols),
                 pl.BlockSpec((seqs, cols), lambda i, s: (0, width // cols)),
             ],
@@ -300,7 +305,7 @@
         ),
         out_shape=[jax.ShapeDtypeStruct((seqs, length, cols), BF)] * 2,
         compiler_params=PARAMS,
-    )(scalars, kv_part, query, encoded_other, weights, attended_grad, last_row)
+    )(scalars, query, encoded, encoded_other, weights, weights, attended_grad, last_row)
 
     last = lax.ppermute(
         jnp.concatenate([att[:, -1], dquery[:, -1]], axis=-1), "group", backward

time: 216 us -> 214 us (level)
  local copies, waits for them, and re-layouts: 9.84 us -> 5.46 us
  waiting for transfers between devices: 75.7 us -> 78.3 us
    unnamed x20 -> x14, local copies, waits for them, and re-layouts: 6.96 us -> 3.34 us
    all_to_all x2, waiting for transfers between devices: 6.8 us -> 10.3 us  [round_x(): lax.all_to_all(value, 'mp', split_axis=0, concat_axis=0, tiled=True, axis...]
    pallas_call x1, Pallas kernels: 4.69 us -> 2.09 us  [local(): pl.pallas_call(functools.partial(project_kernel, run), grid=(across_x //...]
  transfers between devices with their start and end apart: 10 -> 10, of which waited for: 7 -> 7; matrix products, arithmetic and copies ran while one was open for 2% -> 2% of each run, Pallas kernels for 4% -> 3%
where the time goes in v5:
time: 214 us; the launch traced here: 212 us
  waiting for transfers between devices  78.3 us (37%)
  blocking collectives  52.1 us (24%)
  starting transfers between devices  43.3 us (20%)
  Pallas kernels  15.7 us (7%)
  between operations  14.3 us (7%)
  local copies, waits for them, and re-layouts  5.46 us (3%)
  other arithmetic  2.75 us (1%)
    all_to_all x2, blocking collectives, local(): part = lax.all_to_all(part, 'mp', split_axis=0, concat_axis=0, tiled=True)  52.1 us
    all_to_all x1, waiting for transfers between devices, local(): lax.all_to_all(found, 'group', split_axis=0, concat_axis=0, tiled=True)  36.3 us
    all_to_all x1, starting transfers between devices, local(): lax.all_to_all(requests, 'group', split_axis=0, concat_axis=0, tiled=True)  17.1 us
    all_to_all x1, waiting for transfers between devices, local(): lax.all_to_all(requests, 'group', split_axis=0, concat_axis=0, tiled=True)  10.7 us
    all_to_all x2, waiting for transfers between devices, round_x(): lax.all_to_all(value, 'mp', split_axis=0, concat_axis=0, tiled=True, axis...  10.3 us
    all_gather x1, waiting for transfers between devices, round_z(): lax.all_gather(value, 'group', axis=0, tiled=True, axis_index_groups=groups)  9.9 us
    ppermute x1, waiting for transfers between devices, local(): single = lax.ppermute(single, 'mp', [(m, m ^ 1) for m in range(mp_size)])  9.79 us
    all_to_all x2, starting transfers between devices, round_x(): lax.all_to_all(value, 'mp', split_axis=0, concat_axis=0, tiled=True, axis...  7.88 us
  transfers between devices with their start and end apart: 10, of which 7 were waited for; matrix products, arithmetic and copies ran while one was open for 2% of the time, Pallas kernels for 3%

profile of v5, /device:TPU:24, one launch (start us, length us, event | category | flops | bytes accessed | tf_op | source)
XLA Modules:
  0.0 212.0 jit_solution(16185450820167337350)
XLA Ops:
  8.1 2.6 %collective-permute-start.1 = (bf16[64,768]{1,0:T(8,128)(2,1)S(1)}, bf16[64,768]{1,0:T(8,128)(2,1)S(1)}, u32[]{:S(2)}, u32[]{:S(2)}) collective-permute-start(bf16[64,768]{1,0:T(8,128)(2,1)S(1)} %pad_add_fusion), channel_id=1, source_target_pairs={{0,16},{8,24},{16,0},{24,8},{32,48},{40,56},{48,32},{56,40},{64,80... | collective-permute-start | bytes 294920 | tf_op jit(solution)/shard_map/ppermute | solution.py:220
  12.4 17.1 %all-to-all-start = ((s32[64,1,128]{2,1,0:T(1,128)}), s32[64,1,128]{2,1,0:T(1,128)S(1)}, u32[]{:S(2)}, u32[]{:S(2)}) async-start(s32[64,1,128]{2,1,0:T(1,128)} %bitcast.4), calls=%async_computation | async-start | bytes 65536 | tf_op jit(solution)/shard_map/all_to_all | solution.py:235
  31.2 10.7 %all-to-all-done = s32[64,1,128]{2,1,0:T(1,128)S(1)} async-done(((s32[64,1,128]{2,1,0:T(1,128)}), s32[64,1,128]{2,1,0:T(1,128)S(1)}, u32[]{:S(2)}, u32[]{:S(2)}) %all-to-all-start) | async-done | bytes 32800 | tf_op jit(solution)/shard_map/all_to_all | solution.py:235
  43.7 5.5 %all-to-all-start.1 = ((bf16[64,2,2304]{2,1,0:T(2,128)(2,1)}), bf16[64,2,2304]{2,1,0:T(2,128)(2,1)S(1)}, u32[]{:S(2)}, u32[]{:S(2)}) async-start(bf16[64,2,2304]{2,1,0:T(2,128)(2,1)} %reshape.24), calls=%async_computation.1 | async-start | bytes 1179648 | tf_op jit(solution)/shard_map/all_to_all | solution.py:243
  50.3 2.1 collective-permute-start
  52.4 3.4 %collective-permute-start.2 = (s32[3,128]{1,0:T(4,128)S(1)}, s32[3,128]{1,0:T(4,128)S(1)}, u32[]{:S(2)}, u32[]{:S(2)}) collective-permute-start(s32[3,128]{1,0:T(4,128)S(1)} %get-tuple-element.14), channel_id=1, source_target_pairs={{0,8},{8,16},{16,24},{24,32},{32,40},{40,48},{48,56},{56,64},{64,7... | collective-permute-start | bytes 4616 | tf_op jit(solution)/shard_map/ppermute | solution.py:234
  55.7 36.3 %all-to-all-done.1 = bf16[64,2,2304]{2,1,0:T(2,128)(2,1)S(1)} async-done(((bf16[64,2,2304]{2,1,0:T(2,128)(2,1)}), bf16[64,2,2304]{2,1,0:T(2,128)(2,1)S(1)}, u32[]{:S(2)}, u32[]{:S(2)}) %all-to-all-start.1) | async-done | bytes 589856 | tf_op jit(solution)/shard_map/all_to_all | solution.py:243
  92.1 1.8 shard_map.98
  93.9 4.3 %all-to-all-start.2 = ((bf16[4,384,512]{2,1,0:T(8,128)(2,1)}), bf16[4,384,512]{2,1,0:T(8,128)(2,1)S(1)}, u32[]{:S(2)}, u32[]{:S(2)}) async-start(bf16[4,384,512]{2,1,0:T(8,128)(2,1)} %get-tuple-element.16), calls=%async_computation.2 | async-start | bytes 3145728 | tf_op jit(solution)/shard_map/all_to_all | solution.py:250
  98.2 2.9 %collective-permute-start.3 = (bf16[384,512]{1,0:T(8,128)(2,1)S(1)}, bf16[384,512]{1,0:T(8,128)(2,1)S(1)}, u32[]{:S(2)}, u32[]{:S(2)}) collective-permute-start(bf16[384,512]{1,0:T(8,128)(2,1)S(1)} %get-tuple-element.17), channel_id=1, source_target_pairs={{0,1},{1,0},{2,3},{3,2},{4,5},{5,4},{6,7},{7,6},{8,9},{9,8},{10,11... | collective-permute-start | bytes 1179656 | tf_op jit(solution)/shard_map/ppermute | solution.py:259
  101.1 9.8 %collective-permute-done.3.in_ref = bf16[384,512]{1,0:T(8,128)(2,1)S(1)} collective-permute-done((bf16[384,512]{1,0:T(8,128)(2,1)S(1)}, bf16[384,512]{1,0:T(8,128)(2,1)S(1)}, u32[]{:S(2)}, u32[]{:S(2)}) %collective-permute-start.3) | collective-permute-done | bytes 393248 | tf_op jit(solution)/shard_map/ppermute | solution.py:259
  112.1 5.5 %all-to-all-done.2.enc_ref = bf16[4,384,512]{2,1,0:T(8,128)(2,1)S(1)} async-done(((bf16[4,384,512]{2,1,0:T(8,128)(2,1)}), bf16[4,384,512]{2,1,0:T(8,128)(2,1)S(1)}, u32[]{:S(2)}, u32[]{:S(2)}) %all-to-all-start.2) | async-done | bytes 1572896 | tf_op jit(solution)/shard_map/all_to_all | solution.py:250
  117.6 3.6 %all-to-all-start.3 = ((bf16[4,384,512]{2,1,0:T(8,128)(2,1)}), bf16[4,384,512]{2,1,0:T(8,128)(2,1)S(1)}, u32[]{:S(2)}, u32[]{:S(2)}) async-start(bf16[4,384,512]{2,1,0:T(8,128)(2,1)} %copy-done), calls=%async_computation.3 | async-start | bytes 3145728 | tf_op jit(solution)/shard_map/all_to_all | solution.py:250
  121.5 9.9 %all-gather.2.cloned.1.call-done.q_w_ref.w_ref.next_w_ref = bf16[4096,768]{1,0:T(8,128)(2,1)} async-done(((bf16[128,768]{1,0:T(8,128)(2,1)}), bf16[4096,768]{1,0:T(8,128)(2,1)}) %all-gather.2.cloned.1.call-update) | async-done | bytes 6291472 | tf_op jit(solution)/shard_map/all_gather | solution.py:213
  131.4 1.4 copy-done.1
  132.8 2.1 shard_map.96.q_ref
  134.9 4.8 %all-to-all-done.3.other_ref = bf16[4,384,512]{2,1,0:T(8,128)(2,1)S(1)} async-done(((bf16[4,384,512]{2,1,0:T(8,128)(2,1)}), bf16[4,384,512]{2,1,0:T(8,128)(2,1)S(1)}, u32[]{:S(2)}, u32[]{:S(2)}) %all-to-all-start.3) | async-done | bytes 1572896 | tf_op jit(solution)/shard_map/all_to_all | solution.py:250
  139.7 5.6 %shard_map.100 = (bf16[3,64,256]{2,1,0:T(8,128)(2,1)S(1)}, bf16[3,64,256]{2,1,0:T(8,128)(2,1)S(1)}) custom-call(s32[4]{0:T(128)S(1)} %pad_add_fusion.1.scal_ref, bf16[192,256]{1,0:T(8,128)(2,1)S(1)} %shard_map.96.q_ref, bf16[4,384,512]{2,1,0:T(8,128)(2,1)S(1)} %all-to-all-done.2.enc_ref, bf16[4,384,512]{2,1,0:T(8,128)(2,1)S(1)} %all-to-all-done.3.other_ref, ...), custom_call_target="tpu_custom_call" | custom-call | tf_op jit(solution)/shard_map/pallas_call | solution.py:289
  145.5 1.9 collective-permute-start.4
  147.4 1.3 collective-permute-done.4.last_ref
  148.7 2.4 %shard_map.101 = (bf16[3,64,256]{2,1,0:T(8,128)(2,1)}, bf16[8,192,512]{2,1,0:T(8,128)(2,1)S(1)}) custom-call(bf16[3,64,256]{2,1,0:T(8,128)(2,1)S(1)} %get-tuple-element.18.att_ref, bf16[3,64,256]{2,1,0:T(8,128)(2,1)S(1)} %get-tuple-element.19.dq_ref, bf16[3,512]{1,0:T(4,128)(2,1)S(1)} %collective-permute-done.4.last_ref, ...), custom_call_target="tpu_custom_call" | custom-call | tf_op jit(solution)/shard_map/pallas_call | solution.py:314
  151.2 26.0 %all_to_all.36.in_ref = bf16[8,192,512]{2,1,0:T(8,128)(2,1)S(1)} all-to-all(bf16[8,192,512]{2,1,0:T(8,128)(2,1)S(1)} %get-tuple-element.21), channel_id=1, replica_groups=mesh['group'=64,'mp'=8] {'mp'}, dimensions={0} | all-to-all | bytes 3145728 | tf_op jit(solution)/shard_map/all_to_all | solution.py:330
  177.4 26.1 %all_to_all.37.in_ref = bf16[8,192,512]{2,1,0:T(8,128)(2,1)S(1)} all-to-all(bf16[8,192,512]{2,1,0:T(8,128)(2,1)S(1)} %shard_map.102), channel_id=1, replica_groups=mesh['group'=64,'mp'=8] {'mp'}, dimensions={0} | all-to-all | bytes 3145728 | tf_op jit(solution)/shard_map/all_to_all | solution.py:336
  203.5 1.7 shard_map.103
  (35 shorter events, 9.0 us)
Async XLA Ops:
  7.2 34.8 %copy-start.2 = (bf16[1024,512]{1,0:T(8,128)(2,1)S(1)}, bf16[1024,512]{1,0:T(8,128)(2,1)}, u32[]{:S(2)}) copy-start(bf16[1024,512]{1,0:T(8,128)(2,1)} %table_ref.1) | copy-start | bytes 3145732
  8.1 21.5 %collective-permute-start.1 = (bf16[64,768]{1,0:T(8,128)(2,1)S(1)}, bf16[64,768]{1,0:T(8,128)(2,1)S(1)}, u32[]{:S(2)}, u32[]{:S(2)}) collective-permute-start(bf16[64,768]{1,0:T(8,128)(2,1)S(1)} %pad_add_fusion), channel_id=1, source_target_pairs={{0,16},{8,24},{16,0},{24,8},{32,48},{40,56},{48,32},{56,40},{64,80... | collective-permute-start | bytes 294920 | tf_op jit(solution)/shard_map/ppermute | solution.py:220
  12.4 29.5 %all-to-all-start = ((s32[64,1,128]{2,1,0:T(1,128)}), s32[64,1,128]{2,1,0:T(1,128)S(1)}, u32[]{:S(2)}, u32[]{:S(2)}) async-start(s32[64,1,128]{2,1,0:T(1,128)} %bitcast.4), calls=%async_computation | async-start | bytes 65536 | tf_op jit(solution)/shard_map/all_to_all | solution.py:235
  29.5 101.9 %all-gather.2.cloned.1.call-start = ((), (), s32[]{:S(2)}) async-start(), calls=%async_computation.6 | async-start | bytes 6488064 | tf_op jit(solution)/shard_map/all_gather | solution.py:213
  42.8 6.4 %copy-start.3 = (bf16[3,64,256]{2,1,0:T(8,128)(2,1)S(1)}, bf16[3,64,256]{2,1,0:T(8,128)(2,1)}, u32[]{:S(2)}) copy-start(bf16[3,64,256]{2,1,0:T(8,128)(2,1)} %grad_ref.1) | copy-start | bytes 294916
  43.7 48.3 %all-to-all-start.1 = ((bf16[64,2,2304]{2,1,0:T(2,128)(2,1)}), bf16[64,2,2304]{2,1,0:T(2,128)(2,1)S(1)}, u32[]{:S(2)}, u32[]{:S(2)}) async-start(bf16[64,2,2304]{2,1,0:T(2,128)(2,1)} %reshape.24), calls=%async_computation.1 | async-start | bytes 1179648 | tf_op jit(solution)/shard_map/all_to_all | solution.py:243
  50.3 41.8 %collective-permute-start = (bf16[3,4352]{1,0:T(4,128)(2,1)S(1)}, bf16[3,4352]{1,0:T(4,128)(2,1)S(1)}, u32[]{:S(2)}, u32[]{:S(2)}) collective-permute-start(bf16[3,4352]{1,0:T(4,128)(2,1)S(1)} %pad_maximum_fusion.1), channel_id=1, source_target_pairs={{0,8},{8,16},{16,24},{24,32},{32,40},{40,48},{48,56},{56,64},{64,7... | collective-permute-start | bytes 78344 | tf_op jit(solution)/shard_map/ppermute | solution.py:222
  52.4 39.7 %collective-permute-start.2 = (s32[3,128]{1,0:T(4,128)S(1)}, s32[3,128]{1,0:T(4,128)S(1)}, u32[]{:S(2)}, u32[]{:S(2)}) collective-permute-start(s32[3,128]{1,0:T(4,128)S(1)} %get-tuple-element.14), channel_id=1, source_target_pairs={{0,8},{8,16},{16,24},{24,32},{32,40},{40,48},{48,56},{56,64},{64,7... | collective-permute-start | bytes 4616 | tf_op jit(solution)/shard_map/ppermute | solution.py:234
  93.9 23.8 %all-to-all-start.2 = ((bf16[4,384,512]{2,1,0:T(8,128)(2,1)}), bf16[4,384,512]{2,1,0:T(8,128)(2,1)S(1)}, u32[]{:S(2)}, u32[]{:S(2)}) async-start(bf16[4,384,512]{2,1,0:T(8,128)(2,1)} %get-tuple-element.16), calls=%async_computation.2 | async-start | bytes 3145728 | tf_op jit(solution)/shard_map/all_to_all | solution.py:250
  98.2 12.7 %collective-permute-start.3 = (bf16[384,512]{1,0:T(8,128)(2,1)S(1)}, bf16[384,512]{1,0:T(8,128)(2,1)S(1)}, u32[]{:S(2)}, u32[]{:S(2)}) collective-permute-start(bf16[384,512]{1,0:T(8,128)(2,1)S(1)} %get-tuple-element.17), channel_id=1, source_target_pairs={{0,1},{1,0},{2,3},{3,2},{4,5},{5,4},{6,7},{7,6},{8,9},{9,8},{10,11... | collective-permute-start | bytes 1179656 | tf_op jit(solution)/shard_map/ppermute | solution.py:259
  111.0 1.1 copy-start
  112.1 9.1 %copy-start.4 = (s32[3,64]{1,0:T(4,128)S(1)}, s32[3,64]{1,0:T(4,128)}, u32[]{:S(2)}) copy-start(s32[3,64]{1,0:T(4,128)} %param.10) | copy-start | bytes 2308
  117.6 22.1 %all-to-all-start.3 = ((bf16[4,384,512]{2,1,0:T(8,128)(2,1)}), bf16[4,384,512]{2,1,0:T(8,128)(2,1)S(1)}, u32[]{:S(2)}, u32[]{:S(2)}) async-start(bf16[4,384,512]{2,1,0:T(8,128)(2,1)} %copy-done), calls=%async_computation.3 | async-start | bytes 3145728 | tf_op jit(solution)/shard_map/all_to_all | solution.py:250
  131.4 1.4 copy-start.1
  145.5 3.2 %collective-permute-start.4 = (bf16[3,512]{1,0:T(4,128)(2,1)S(1)}, bf16[3,512]{1,0:T(4,128)(2,1)S(1)}, u32[]{:S(2)}, u32[]{:S(2)}) collective-permute-start(bf16[3,512]{1,0:T(4,128)(2,1)S(1)} %pad_maximum_fusion.2), channel_id=1, source_target_pairs={{0,504},{8,0},{16,8},{24,16},{32,24},{40,32},{48,40},{56,48},{64,5... | collective-permute-start | bytes 9224 | tf_op jit(solution)/shard_map/ppermute | solution.py:310
Sparse Core Ops, SparseCore 0:
  42.1 89.2 all-gather.1

commit v6 on v5

--- a/solution.py
+++ b/solution.py
@@ -66,7 +66,8 @@
     for s in range(seqs):
         chosen = (slots[:, s : s + 1] == lanes).astype(F32).astype(BF)
         found = dot(chosen, rows).astype(BF)
-        one_ref[s * keys : (s + 1) * keys, :] = found
+        if s < seqs - 1:
+            one_ref[s * keys : (s + 1) * keys, :] = found
         for c in range(copies):
             out_ref[c, s * keys : (s + 1) * keys, :] = found
 
@@ -101,8 +102,8 @@
 
 
 def attend_kernel(
-    run, scal_ref, q_ref, enc_ref, other_ref, w_ref, next_w_ref, grad_ref, last_grad_ref, att_ref, dq_ref,
-    kv_acc,
+    run, scal_ref, q_ref, enc_ref, other_ref, other_last_ref, w_ref, next_w_ref, grad_ref, last_grad_ref,
+    att_ref, dq_ref, kv_acc,
 ):
     step, steps = pl.program_id(0), pl.num_programs(0)
     seqs, length, cols = grad_ref.shape
@@ -112,8 +113,9 @@
     def _():
         kv_acc[...] = jnp.zeros_like(kv_acc)
 
-    def add(ref):
-        enc = jnp.concatenate([ref[0], ref[1]], axis=1)
+    def add(*refs):
+        enc = [jnp.concatenate([ref[0], ref[1]], axis=1) for ref in refs]
+        enc = jnp.concatenate(enc, axis=0)
         weights = jnp.concatenate([in_order(w_ref[...], run), in_order(next_w_ref[...], run)], axis=0)
         kv_acc[...] += dot(enc, weights)
 
@@ -123,7 +125,7 @@
 
     @pl.when(step >= steps // 2)
     def _():
-        add(other_ref)
+        add(other_ref, other_last_ref)
 
     @pl.when(step == steps - 1)
     def _():
@@ -253,13 +255,20 @@
 
     single, encoded = pl.pallas_call(
         functools.partial(order_kernel, capacity),
-        out_shape=[jax.ShapeDtypeStruct((id_count, feats), BF), copies],
+        out_shape=[jax.ShapeDtypeStruct((id_count - keys, feats), BF), copies],
         compiler_params=PARAMS,
     )(slot, returned)
     single = lax.ppermute(single, "mp", [(m, m ^ 1) for m in range(mp_size)])
     encoded = round_x(encoded)
+    encoded_last = lax.ppermute(
+        encoded[:, id_count - keys :], "mp", [(m, m ^ 1) for m in range(mp_size)]
+    )
     encoded_other = round_x(
-        pl.pallas_call(copies_kernel, out_shape=copies, compiler_params=PARAMS)(single)
+        pl.pallas_call(
+            copies_kernel,
+            out_shape=jax.ShapeDtypeStruct((across_x, id_count - keys, feats), BF),
+            compiler_params=PARAMS,
+        )(single)
     )
 
     earlier = jnp.maximum(group_here - 1, 0)
@@ -294,7 +303,8 @@
             in_specs=[
                 whole(seqs * length, cols),
                 pl.BlockSpec((2, id_count, feats), lambda i, s: (jnp.minimum(i, 1), 0, 0)),
-                pl.BlockSpec((2, id_count, feats), lambda i, s: (jnp.maximum(i - 2, 0), 0, 0)),
+                pl.BlockSpec((2, id_count - keys, feats), lambda i, s: (jnp.maximum(i - 2, 0), 0, 0)),
+                pl.BlockSpec((2, keys, feats), lambda i, s: (jnp.maximum(i - 2, 0), 0, 0)),
                 pl.BlockSpec((feats, 2 * cols), lambda i, s: (block(i, s), 0)),
                 pl.BlockSpec((feats, 2 * cols), lambda i, s: (block(i, s) + 2, 0)),
                 whole(seqs, length, cols),
@@ -305,7 +315,7 @@
         ),
         out_shape=[jax.ShapeDtypeStruct((seqs, length, cols), BF)] * 2,
         compiler_params=PARAMS,
-    )(scalars, query, encoded, encoded_other, weights, weights, attended_grad, last_row)
+    )(scalars, query, encoded, encoded_other, encoded_last, weights, weights, attended_grad, last_row)
 
     last = lax.ppermute(
         jnp.concatenate([att[:, -1], dquery[:, -1]], axis=-1), "group", backward

time: 214 us -> 214 us (level)
  waiting for transfers between devices: 78.3 us -> 72.3 us
  starting transfers between devices: 43.3 us -> 45.9 us
    all_gather x1, waiting for transfers between devices: 9.9 us -> 6.57 us  [round_z(): lax.all_gather(value, 'group', axis=0, tiled=True, axis_index_groups=groups)]
    ppermute x1, waiting for transfers between devices: 9.79 us -> 6.98 us  [local(): single = lax.ppermute(single, 'mp', [(m, m ^ 1) for m in range(mp_size)])]
    ppermute x0 -> x1, starting transfers between devices: none -> 2.56 us  [local(): lax.ppermute(encoded[:, id_count - keys:], 'mp', [(m, m ^ 1) for m in ran...]
  transfers between devices with their start and end apart: 10 -> 11, of which waited for: 7 -> 7; matrix products, arithmetic and copies ran while one was open for 2% -> 3% of each run, Pallas kernels for 3% -> 3%
where the time goes in v6:
time: 214 us; the launch traced here: 211 us
  waiting for transfers between devices  72.3 us (34%)
  blocking collectives  54.2 us (25%)
  starting transfers between devices  45.9 us (21%)
  Pallas kernels  15.7 us (7%)
  between operations  14.3 us (7%)
  local copies, waits for them, and re-layouts  6.12 us (3%)
  other arithmetic  2.69 us (1%)
    all_to_all x2, blocking collectives, local(): part = lax.all_to_all(part, 'mp', split_axis=0, concat_axis=0, tiled=True)  54.2 us
    all_to_all x1, waiting for transfers between devices, local(): lax.all_to_all(found, 'group', split_axis=0, concat_axis=0, tiled=True)  36.3 us
    all_to_all x1, starting transfers between devices, local(): lax.all_to_all(requests, 'group', split_axis=0, concat_axis=0, tiled=True)  17.1 us
    all_to_all x1, waiting for transfers between devices, local(): lax.all_to_all(requests, 'group', split_axis=0, concat_axis=0, tiled=True)  10.8 us
    all_to_all x2, waiting for transfers between devices, round_x(): lax.all_to_all(value, 'mp', split_axis=0, concat_axis=0, tiled=True, axis...  8.52 us
    all_to_all x2, starting transfers between devices, round_x(): lax.all_to_all(value, 'mp', split_axis=0, concat_axis=0, tiled=True, axis...  7.83 us
    ppermute x1, waiting for transfers between devices, local(): single = lax.ppermute(single, 'mp', [(m, m ^ 1) for m in range(mp_size)])  6.98 us
    all_gather x1, waiting for transfers between devices, round_z(): lax.all_gather(value, 'group', axis=0, tiled=True, axis_index_groups=groups)  6.57 us
  transfers between devices with their start and end apart: 11, of which 7 were waited for; matrix products, arithmetic and copies ran while one was open for 3% of the time, Pallas kernels for 3%

profile of v6, /device:TPU:24, one launch (start us, length us, event | category | flops | bytes accessed | tf_op | source)
XLA Modules:
  0.0 211.1 jit_solution(6221692557499315639)
XLA Ops:
  8.1 2.6 %collective-permute-start.1 = (bf16[64,768]{1,0:T(8,128)(2,1)S(1)}, bf16[64,768]{1,0:T(8,128)(2,1)S(1)}, u32[]{:S(2)}, u32[]{:S(2)}) collective-permute-start(bf16[64,768]{1,0:T(8,128)(2,1)S(1)} %pad_add_fusion), channel_id=1, source_target_pairs={{0,16},{8,24},{16,0},{24,8},{32,48},{40,56},{48,32},{56,40},{64,80... | collective-permute-start | bytes 294920 | tf_op jit(solution)/shard_map/ppermute | solution.py:222
  12.4 17.1 %all-to-all-start = ((s32[64,1,128]{2,1,0:T(1,128)}), s32[64,1,128]{2,1,0:T(1,128)S(1)}, u32[]{:S(2)}, u32[]{:S(2)}) async-start(s32[64,1,128]{2,1,0:T(1,128)} %bitcast.4), calls=%async_computation | async-start | bytes 65536 | tf_op jit(solution)/shard_map/all_to_all | solution.py:237
  31.1 10.8 %all-to-all-done = s32[64,1,128]{2,1,0:T(1,128)S(1)} async-done(((s32[64,1,128]{2,1,0:T(1,128)}), s32[64,1,128]{2,1,0:T(1,128)S(1)}, u32[]{:S(2)}, u32[]{:S(2)}) %all-to-all-start) | async-done | bytes 32800 | tf_op jit(solution)/shard_map/all_to_all | solution.py:237
  43.7 5.5 %all-to-all-start.1 = ((bf16[64,2,2304]{2,1,0:T(2,128)(2,1)}), bf16[64,2,2304]{2,1,0:T(2,128)(2,1)S(1)}, u32[]{:S(2)}, u32[]{:S(2)}) async-start(bf16[64,2,2304]{2,1,0:T(2,128)(2,1)} %reshape.24), calls=%async_computation.1 | async-start | bytes 1179648 | tf_op jit(solution)/shard_map/all_to_all | solution.py:245
  50.3 2.1 collective-permute-start
  52.4 3.4 %collective-permute-start.2 = (s32[3,128]{1,0:T(4,128)S(1)}, s32[3,128]{1,0:T(4,128)S(1)}, u32[]{:S(2)}, u32[]{:S(2)}) collective-permute-start(s32[3,128]{1,0:T(4,128)S(1)} %get-tuple-element.14), channel_id=1, source_target_pairs={{0,8},{8,16},{16,24},{24,32},{32,40},{40,48},{48,56},{56,64},{64,7... | collective-permute-start | bytes 4616 | tf_op jit(solution)/shard_map/ppermute | solution.py:236
  55.7 36.3 %all-to-all-done.1 = bf16[64,2,2304]{2,1,0:T(2,128)(2,1)S(1)} async-done(((bf16[64,2,2304]{2,1,0:T(2,128)(2,1)}), bf16[64,2,2304]{2,1,0:T(2,128)(2,1)S(1)}, u32[]{:S(2)}, u32[]{:S(2)}) %all-to-all-start.1) | async-done | bytes 589856 | tf_op jit(solution)/shard_map/all_to_all | solution.py:245
  92.1 1.8 shard_map.98
  93.9 4.3 %all-to-all-start.2 = ((bf16[4,384,512]{2,1,0:T(8,128)(2,1)}), bf16[4,384,512]{2,1,0:T(8,128)(2,1)S(1)}, u32[]{:S(2)}, u32[]{:S(2)}) async-start(bf16[4,384,512]{2,1,0:T(8,128)(2,1)} %get-tuple-element.16), calls=%async_computation.2 | async-start | bytes 3145728 | tf_op jit(solution)/shard_map/all_to_all | solution.py:252
  98.2 2.9 %collective-permute-start.3 = (bf16[256,512]{1,0:T(8,128)(2,1)S(1)}, bf16[256,512]{1,0:T(8,128)(2,1)S(1)}, u32[]{:S(2)}, u32[]{:S(2)}) collective-permute-start(bf16[256,512]{1,0:T(8,128)(2,1)S(1)} %get-tuple-element.17), channel_id=1, source_target_pairs={{0,1},{1,0},{2,3},{3,2},{4,5},{5,4},{6,7},{7,6},{8,9},{9,8},{10,11... | collective-permute-start | bytes 786440 | tf_op jit(solution)/shard_map/ppermute | solution.py:261
  101.1 7.0 %collective-permute-done.3.in_ref = bf16[256,512]{1,0:T(8,128)(2,1)S(1)} collective-permute-done((bf16[256,512]{1,0:T(8,128)(2,1)S(1)}, bf16[256,512]{1,0:T(8,128)(2,1)S(1)}, u32[]{:S(2)}, u32[]{:S(2)}) %collective-permute-start.3) | collective-permute-done | bytes 262176 | tf_op jit(solution)/shard_map/ppermute | solution.py:261
  109.1 8.5 %all-to-all-done.2.enc_ref = bf16[4,384,512]{2,1,0:T(8,128)(2,1)S(1)} async-done(((bf16[4,384,512]{2,1,0:T(8,128)(2,1)}), bf16[4,384,512]{2,1,0:T(8,128)(2,1)S(1)}, u32[]{:S(2)}, u32[]{:S(2)}) %all-to-all-start.2) | async-done | bytes 1572896 | tf_op jit(solution)/shard_map/all_to_all | solution.py:252
  117.6 3.5 %all-to-all-start.3 = ((bf16[4,256,512]{2,1,0:T(8,128)(2,1)}), bf16[4,256,512]{2,1,0:T(8,128)(2,1)S(1)}, u32[]{:S(2)}, u32[]{:S(2)}) async-start(bf16[4,256,512]{2,1,0:T(8,128)(2,1)} %copy-done), calls=%async_computation.3 | async-start | bytes 2097152 | tf_op jit(solution)/shard_map/all_to_all | solution.py:252
  122.0 2.6 %collective-permute-start.4 = (bf16[4,128,512]{2,1,0:T(8,128)(2,1)}, bf16[4,128,512]{2,1,0:T(8,128)(2,1)S(1)}, u32[]{:S(2)}, u32[]{:S(2)}) collective-permute-start(bf16[4,128,512]{2,1,0:T(8,128)(2,1)} %slice.20), channel_id=1, source_target_pairs={{0,1},{1,0},{2,3},{3,2},{4,5},{5,4},{6,7},{7,6},{8,9},{9,8},{10,11... | collective-permute-start | bytes 1572872 | tf_op jit(solution)/shard_map/ppermute | solution.py:263
  124.8 6.6 %all-gather.2.cloned.1.call-done.q_w_ref.w_ref.next_w_ref = bf16[4096,768]{1,0:T(8,128)(2,1)} async-done(((bf16[128,768]{1,0:T(8,128)(2,1)}), bf16[4096,768]{1,0:T(8,128)(2,1)}) %all-gather.2.cloned.1.call-update) | async-done | bytes 6291472 | tf_op jit(solution)/shard_map/all_gather | solution.py:215
  131.4 1.4 copy-done.1
  132.8 2.1 shard_map.96.q_ref
  134.9 1.8 collective-permute-done.4.other_last_ref
  136.7 5.6 %shard_map.100 = (bf16[3,64,256]{2,1,0:T(8,128)(2,1)S(1)}, bf16[3,64,256]{2,1,0:T(8,128)(2,1)S(1)}) custom-call(s32[4]{0:T(128)S(1)} %pad_add_fusion.1.scal_ref, bf16[192,256]{1,0:T(8,128)(2,1)S(1)} %shard_map.96.q_ref, bf16[4,384,512]{2,1,0:T(8,128)(2,1)S(1)} %all-to-all-done.2.enc_ref, bf16[4,256,512]{2,1,0:T(8,128)(2,1)S(1)} %all-to-all-done.3.other_ref, ...), custom_call_target="tpu_custom_call" | custom-call | tf_op jit(solution)/shard_map/pallas_call | solution.py:298
  142.6 1.9 collective-permute-start.5
  145.8 2.4 %shard_map.101 = (bf16[3,64,256]{2,1,0:T(8,128)(2,1)}, bf16[8,192,512]{2,1,0:T(8,128)(2,1)S(1)}) custom-call(bf16[3,64,256]{2,1,0:T(8,128)(2,1)S(1)} %get-tuple-element.18.att_ref, bf16[3,64,256]{2,1,0:T(8,128)(2,1)S(1)} %get-tuple-element.19.dq_ref, bf16[3,512]{1,0:T(4,128)(2,1)S(1)} %collective-permute-done.5.last_ref, ...), custom_call_target="tpu_custom_call" | custom-call | tf_op jit(solution)/shard_map/pallas_call | solution.py:324
  148.3 28.1 %all_to_all.36.in_ref = bf16[8,192,512]{2,1,0:T(8,128)(2,1)S(1)} all-to-all(bf16[8,192,512]{2,1,0:T(8,128)(2,1)S(1)} %get-tuple-element.21), channel_id=1, replica_groups=mesh['group'=64,'mp'=8] {'mp'}, dimensions={0} | all-to-all | bytes 3145728 | tf_op jit(solution)/shard_map/all_to_all | solution.py:340
  176.5 26.1 %all_to_all.37.in_ref = bf16[8,192,512]{2,1,0:T(8,128)(2,1)S(1)} all-to-all(bf16[8,192,512]{2,1,0:T(8,128)(2,1)S(1)} %shard_map.102), channel_id=1, replica_groups=mesh['group'=64,'mp'=8] {'mp'}, dimensions={0} | all-to-all | bytes 3145728 | tf_op jit(solution)/shard_map/all_to_all | solution.py:346
  202.6 1.7 shard_map.103
  (38 shorter events, 10.9 us)
Async XLA Ops:
  7.2 34.8 %copy-start.2 = (bf16[1024,512]{1,0:T(8,128)(2,1)S(1)}, bf16[1024,512]{1,0:T(8,128)(2,1)}, u32[]{:S(2)}) copy-start(bf16[1024,512]{1,0:T(8,128)(2,1)} %table_ref.1) | copy-start | bytes 3145732
  8.1 21.5 %collective-permute-start.1 = (bf16[64,768]{1,0:T(8,128)(2,1)S(1)}, bf16[64,768]{1,0:T(8,128)(2,1)S(1)}, u32[]{:S(2)}, u32[]{:S(2)}) collective-permute-start(bf16[64,768]{1,0:T(8,128)(2,1)S(1)} %pad_add_fusion), channel_id=1, source_target_pairs={{0,16},{8,24},{16,0},{24,8},{32,48},{40,56},{48,32},{56,40},{64,80... | collective-permute-start | bytes 294920 | tf_op jit(solution)/shard_map/ppermute | solution.py:222
  12.4 29.5 %all-to-all-start = ((s32[64,1,128]{2,1,0:T(1,128)}), s32[64,1,128]{2,1,0:T(1,128)S(1)}, u32[]{:S(2)}, u32[]{:S(2)}) async-start(s32[64,1,128]{2,1,0:T(1,128)} %bitcast.4), calls=%async_computation | async-start | bytes 65536 | tf_op jit(solution)/shard_map/all_to_all | solution.py:237
  29.5 101.9 %all-gather.2.cloned.1.call-start = ((), (), s32[]{:S(2)}) async-start(), calls=%async_computation.6 | async-start | bytes 6488064 | tf_op jit(solution)/shard_map/all_gather | solution.py:215
  42.8 6.4 %copy-start.3 = (bf16[3,64,256]{2,1,0:T(8,128)(2,1)S(1)}, bf16[3,64,256]{2,1,0:T(8,128)(2,1)}, u32[]{:S(2)}) copy-start(bf16[3,64,256]{2,1,0:T(8,128)(2,1)} %grad_ref.1) | copy-start | bytes 294916
  43.7 48.3 %all-to-all-start.1 = ((bf16[64,2,2304]{2,1,0:T(2,128)(2,1)}), bf16[64,2,2304]{2,1,0:T(2,128)(2,1)S(1)}, u32[]{:S(2)}, u32[]{:S(2)}) async-start(bf16[64,2,2304]{2,1,0:T(2,128)(2,1)} %reshape.24), calls=%async_computation.1 | async-start | bytes 1179648 | tf_op jit(solution)/shard_map/all_to_all | solution.py:245
  50.3 41.8 %collective-permute-start = (bf16[3,4352]{1,0:T(4,128)(2,1)S(1)}, bf16[3,4352]{1,0:T(4,128)(2,1)S(1)}, u32[]{:S(2)}, u32[]{:S(2)}) collective-permute-start(bf16[3,4352]{1,0:T(4,128)(2,1)S(1)} %pad_maximum_fusion.1), channel_id=1, source_target_pairs={{0,8},{8,16},{16,24},{24,32},{32,40},{40,48},{48,56},{56,64},{64,7... | collective-permute-start | bytes 78344 | tf_op jit(solution)/shard_map/ppermute | solution.py:224
  52.4 39.7 %collective-permute-start.2 = (s32[3,128]{1,0:T(4,128)S(1)}, s32[3,128]{1,0:T(4,128)S(1)}, u32[]{:S(2)}, u32[]{:S(2)}) collective-permute-start(s32[3,128]{1,0:T(4,128)S(1)} %get-tuple-element.14), channel_id=1, source_target_pairs={{0,8},{8,16},{16,24},{24,32},{32,40},{40,48},{48,56},{56,64},{64,7... | collective-permute-start | bytes 4616 | tf_op jit(solution)/shard_map/ppermute | solution.py:236
  93.9 23.8 %all-to-all-start.2 = ((bf16[4,384,512]{2,1,0:T(8,128)(2,1)}), bf16[4,384,512]{2,1,0:T(8,128)(2,1)S(1)}, u32[]{:S(2)}, u32[]{:S(2)}) async-start(bf16[4,384,512]{2,1,0:T(8,128)(2,1)} %get-tuple-element.16), calls=%async_computation.2 | async-start | bytes 3145728 | tf_op jit(solution)/shard_map/all_to_all | solution.py:252
  98.2 9.9 %collective-permute-start.3 = (bf16[256,512]{1,0:T(8,128)(2,1)S(1)}, bf16[256,512]{1,0:T(8,128)(2,1)S(1)}, u32[]{:S(2)}, u32[]{:S(2)}) collective-permute-start(bf16[256,512]{1,0:T(8,128)(2,1)S(1)} %get-tuple-element.17), channel_id=1, source_target_pairs={{0,1},{1,0},{2,3},{3,2},{4,5},{5,4},{6,7},{7,6},{8,9},{9,8},{10,11... | collective-permute-start | bytes 786440 | tf_op jit(solution)/shard_map/ppermute | solution.py:261
  108.1 1.0 copy-start
  109.1 15.5 %copy-start.4 = (s32[3,64]{1,0:T(4,128)S(1)}, s32[3,64]{1,0:T(4,128)}, u32[]{:S(2)}) copy-start(s32[3,64]{1,0:T(4,128)} %param.10) | copy-start | bytes 2308
  117.6 17.3 %all-to-all-start.3 = ((bf16[4,256,512]{2,1,0:T(8,128)(2,1)}), bf16[4,256,512]{2,1,0:T(8,128)(2,1)S(1)}, u32[]{:S(2)}, u32[]{:S(2)}) async-start(bf16[4,256,512]{2,1,0:T(8,128)(2,1)} %copy-done), calls=%async_computation.3 | async-start | bytes 2097152 | tf_op jit(solution)/shard_map/all_to_all | solution.py:252
  122.0 14.8 %collective-permute-start.4 = (bf16[4,128,512]{2,1,0:T(8,128)(2,1)}, bf16[4,128,512]{2,1,0:T(8,128)(2,1)S(1)}, u32[]{:S(2)}, u32[]{:S(2)}) collective-permute-start(bf16[4,128,512]{2,1,0:T(8,128)(2,1)} %slice.20), channel_id=1, source_target_pairs={{0,1},{1,0},{2,3},{3,2},{4,5},{5,4},{6,7},{7,6},{8,9},{9,8},{10,11... | collective-permute-start | bytes 1572872 | tf_op jit(solution)/shard_map/ppermute | solution.py:263
  131.4 1.4 copy-start.1
  142.6 3.2 %collective-permute-start.5 = (bf16[3,512]{1,0:T(4,128)(2,1)S(1)}, bf16[3,512]{1,0:T(4,128)(2,1)S(1)}, u32[]{:S(2)}, u32[]{:S(2)}) collective-permute-start(bf16[3,512]{1,0:T(4,128)(2,1)S(1)} %pad_maximum_fusion.2), channel_id=1, source_target_pairs={{0,504},{8,0},{16,8},{24,16},{32,24},{40,32},{48,40},{56,48},{64,5... | collective-permute-start | bytes 9224 | tf_op jit(solution)/shard_map/ppermute | solution.py:320
Sparse Core Ops, SparseCore 0:
  42.1 89.2 all-gather.1

commit v7 on v6

--- a/solution.py
+++ b/solution.py
@@ -10,6 +10,7 @@
 HEAD_DIM = 128
 BF, F32, I32 = jnp.bfloat16, jnp.float32, jnp.int32
 PARAMS = pltpu.CompilerParams(vmem_limit_bytes=48 * 1024 * 1024)
+ROOMY = pltpu.CompilerParams(vmem_limit_bytes=60 * 1024 * 1024)
 NT = (((1,), (1,)), ((), ()))
 
 
@@ -280,16 +281,16 @@
     whole = lambda *shape: pl.BlockSpec(shape, lambda i, s: (0,) * len(shape))
     query = pl.pallas_call(
         functools.partial(project_kernel, run),
-        grid=(across_x // 2,),
+        grid=(across_x,),
         in_specs=[
-            pl.BlockSpec((seqs, length, 4 * feats), lambda i: (0, 0, i)),
-            pl.BlockSpec((seqs, 4 * feats), lambda i: (0, i)),
-            pl.BlockSpec((4 * feats, cols), lambda i: (i, 2)),
+            pl.BlockSpec((seqs, length, 2 * feats), lambda i: (0, 0, i)),
+            pl.BlockSpec((seqs, 2 * feats), lambda i: (0, i)),
+            pl.BlockSpec((2 * feats, cols), lambda i: (i, 2)),
         ],
         out_specs=pl.BlockSpec((seqs * length, cols), lambda i: (0, 0)),
         out_shape=jax.ShapeDtypeStruct((seqs * length, cols), BF),
         scratch_shapes=[pltpu.VMEM((seqs * length, cols), F32)],
-        compiler_params=PARAMS,
+        compiler_params=ROOMY,
     )(tokens, last_row, weights)
 
     def block(i, s):

time: 214 us -> 215 us (level)
  transfers between devices with their start and end apart: 11 -> 11, of which waited for: 7 -> 7; matrix products, arithmetic and copies ran while one was open for 3% -> 3% of each run, Pallas kernels for 3% -> 4%
where the time goes in v7:
time: 215 us; the launch traced here: 212 us
  waiting for transfers between devices  71.9 us (33%)
  blocking collectives  54.2 us (25%)
  starting transfers between devices  45.8 us (21%)
  Pallas kernels  17.5 us (8%)
  between operations  14.3 us (7%)
  local copies, waits for them, and re-layouts  5.61 us (3%)
  other arithmetic  2.69 us (1%)
    all_to_all x2, blocking collectives, local(): part = lax.all_to_all(part, 'mp', split_axis=0, concat_axis=0, tiled=True)  54.2 us
    all_to_all x1, waiting for transfers between devices, local(): lax.all_to_all(found, 'group', split_axis=0, concat_axis=0, tiled=True)  36.3 us
    all_to_all x1, starting transfers between devices, local(): lax.all_to_all(requests, 'group', split_axis=0, concat_axis=0, tiled=True)  17.1 us
    all_to_all x1, waiting for transfers between devices, local(): lax.all_to_all(requests, 'group', split_axis=0, concat_axis=0, tiled=True)  10.8 us
    all_to_all x2, waiting for transfers between devices, round_x(): lax.all_to_all(value, 'mp', split_axis=0, concat_axis=0, tiled=True, axis...  8.52 us
    all_to_all x2, starting transfers between devices, round_x(): lax.all_to_all(value, 'mp', split_axis=0, concat_axis=0, tiled=True, axis...  7.83 us
    ppermute x1, waiting for transfers between devices, local(): single = lax.ppermute(single, 'mp', [(m, m ^ 1) for m in range(mp_size)])  7 us
    all_gather x1, waiting for transfers between devices, round_z(): lax.all_gather(value, 'group', axis=0, tiled=True, axis_index_groups=groups)  6.56 us
  transfers between devices with their start and end apart: 11, of which 7 were waited for; matrix products, arithmetic and copies ran while one was open for 3% of the time, Pallas kernels for 4%

profile of v7, /device:TPU:24, one launch (start us, length us, event | category | flops | bytes accessed | tf_op | source)
XLA Modules:
  0.0 212.0 jit_solution(10942077394370232040)
XLA Ops:
  8.1 2.6 %collective-permute-start.1 = (bf16[64,768]{1,0:T(8,128)(2,1)S(1)}, bf16[64,768]{1,0:T(8,128)(2,1)S(1)}, u32[]{:S(2)}, u32[]{:S(2)}) collective-permute-start(bf16[64,768]{1,0:T(8,128)(2,1)S(1)} %pad_add_fusion), channel_id=1, source_target_pairs={{0,16},{8,24},{16,0},{24,8},{32,48},{40,56},{48,32},{56,40},{64,80... | collective-permute-start | bytes 294920 | tf_op jit(solution)/shard_map/ppermute | solution.py:223
  12.4 17.1 %all-to-all-start = ((s32[64,1,128]{2,1,0:T(1,128)}), s32[64,1,128]{2,1,0:T(1,128)S(1)}, u32[]{:S(2)}, u32[]{:S(2)}) async-start(s32[64,1,128]{2,1,0:T(1,128)} %bitcast.4), calls=%async_computation | async-start | bytes 65536 | tf_op jit(solution)/shard_map/all_to_all | solution.py:238
  31.1 10.8 %all-to-all-done = s32[64,1,128]{2,1,0:T(1,128)S(1)} async-done(((s32[64,1,128]{2,1,0:T(1,128)}), s32[64,1,128]{2,1,0:T(1,128)S(1)}, u32[]{:S(2)}, u32[]{:S(2)}) %all-to-all-start) | async-done | bytes 32800 | tf_op jit(solution)/shard_map/all_to_all | solution.py:238
  43.7 5.5 %all-to-all-start.1 = ((bf16[64,2,2304]{2,1,0:T(2,128)(2,1)}), bf16[64,2,2304]{2,1,0:T(2,128)(2,1)S(1)}, u32[]{:S(2)}, u32[]{:S(2)}) async-start(bf16[64,2,2304]{2,1,0:T(2,128)(2,1)} %reshape.24), calls=%async_computation.1 | async-start | bytes 1179648 | tf_op jit(solution)/shard_map/all_to_all | solution.py:246
  50.3 2.1 collective-permute-start
  52.4 3.4 %collective-permute-start.2 = (s32[3,128]{1,0:T(4,128)S(1)}, s32[3,128]{1,0:T(4,128)S(1)}, u32[]{:S(2)}, u32[]{:S(2)}) collective-permute-start(s32[3,128]{1,0:T(4,128)S(1)} %get-tuple-element.14), channel_id=1, source_target_pairs={{0,8},{8,16},{16,24},{24,32},{32,40},{40,48},{48,56},{56,64},{64,7... | collective-permute-start | bytes 4616 | tf_op jit(solution)/shard_map/ppermute | solution.py:237
  55.7 36.3 %all-to-all-done.1 = bf16[64,2,2304]{2,1,0:T(2,128)(2,1)S(1)} async-done(((bf16[64,2,2304]{2,1,0:T(2,128)(2,1)}), bf16[64,2,2304]{2,1,0:T(2,128)(2,1)S(1)}, u32[]{:S(2)}, u32[]{:S(2)}) %all-to-all-start.1) | async-done | bytes 589856 | tf_op jit(solution)/shard_map/all_to_all | solution.py:246
  92.1 1.8 shard_map.98
  93.9 4.3 %all-to-all-start.2 = ((bf16[4,384,512]{2,1,0:T(8,128)(2,1)}), bf16[4,384,512]{2,1,0:T(8,128)(2,1)S(1)}, u32[]{:S(2)}, u32[]{:S(2)}) async-start(bf16[4,384,512]{2,1,0:T(8,128)(2,1)} %get-tuple-element.16), calls=%async_computation.2 | async-start | bytes 3145728 | tf_op jit(solution)/shard_map/all_to_all | solution.py:253
  98.2 2.9 %collective-permute-start.3 = (bf16[256,512]{1,0:T(8,128)(2,1)S(1)}, bf16[256,512]{1,0:T(8,128)(2,1)S(1)}, u32[]{:S(2)}, u32[]{:S(2)}) collective-permute-start(bf16[256,512]{1,0:T(8,128)(2,1)S(1)} %get-tuple-element.17), channel_id=1, source_target_pairs={{0,1},{1,0},{2,3},{3,2},{4,5},{5,4},{6,7},{7,6},{8,9},{9,8},{10,11... | collective-permute-start | bytes 786440 | tf_op jit(solution)/shard_map/ppermute | solution.py:262
  101.1 7.0 %collective-permute-done.3.in_ref = bf16[256,512]{1,0:T(8,128)(2,1)S(1)} collective-permute-done((bf16[256,512]{1,0:T(8,128)(2,1)S(1)}, bf16[256,512]{1,0:T(8,128)(2,1)S(1)}, u32[]{:S(2)}, u32[]{:S(2)}) %collective-permute-start.3) | collective-permute-done | bytes 262176 | tf_op jit(solution)/shard_map/ppermute | solution.py:262
  109.1 8.5 %all-to-all-done.2.enc_ref = bf16[4,384,512]{2,1,0:T(8,128)(2,1)S(1)} async-done(((bf16[4,384,512]{2,1,0:T(8,128)(2,1)}), bf16[4,384,512]{2,1,0:T(8,128)(2,1)S(1)}, u32[]{:S(2)}, u32[]{:S(2)}) %all-to-all-start.2) | async-done | bytes 1572896 | tf_op jit(solution)/shard_map/all_to_all | solution.py:253
  117.6 3.5 %all-to-all-start.3 = ((bf16[4,256,512]{2,1,0:T(8,128)(2,1)}), bf16[4,256,512]{2,1,0:T(8,128)(2,1)S(1)}, u32[]{:S(2)}, u32[]{:S(2)}) async-start(bf16[4,256,512]{2,1,0:T(8,128)(2,1)} %copy-done), calls=%async_computation.3 | async-start | bytes 2097152 | tf_op jit(solution)/shard_map/all_to_all | solution.py:253
  122.0 2.5 %collective-permute-start.4 = (bf16[4,128,512]{2,1,0:T(8,128)(2,1)}, bf16[4,128,512]{2,1,0:T(8,128)(2,1)S(1)}, u32[]{:S(2)}, u32[]{:S(2)}) collective-permute-start(bf16[4,128,512]{2,1,0:T(8,128)(2,1)} %slice.20), channel_id=1, source_target_pairs={{0,1},{1,0},{2,3},{3,2},{4,5},{5,4},{6,7},{7,6},{8,9},{9,8},{10,11... | collective-permute-start | bytes 1572872 | tf_op jit(solution)/shard_map/ppermute | solution.py:264
  124.8 6.6 %all-gather.2.cloned.1.call-done.q_w_ref.w_ref.next_w_ref = bf16[4096,768]{1,0:T(8,128)(2,1)} async-done(((bf16[128,768]{1,0:T(8,128)(2,1)}), bf16[4096,768]{1,0:T(8,128)(2,1)}) %all-gather.2.cloned.1.call-update) | async-done | bytes 6291472 | tf_op jit(solution)/shard_map/all_gather | solution.py:216
  131.4 3.9 %shard_map.96.q_ref = bf16[192,256]{1,0:T(8,128)(2,1)} custom-call(bf16[3,64,4096]{2,1,0:T(8,128)(2,1)} %tok_ref.1, bf16[3,4352]{1,0:T(4,128)(2,1)} %copy-done.3, bf16[4096,768]{1,0:T(8,128)(2,1)} %all-gather.2.cloned.1.call-done.q_w_ref.w_ref.next_w_ref), custom_call_target="tpu_custom_call" | custom-call | tf_op jit(solution)/shard_map/pallas_call | solution.py:282
  135.3 1.4 collective-permute-done.4.other_last_ref
  137.7 5.6 %shard_map.100 = (bf16[3,64,256]{2,1,0:T(8,128)(2,1)S(1)}, bf16[3,64,256]{2,1,0:T(8,128)(2,1)S(1)}) custom-call(s32[4]{0:T(128)S(1)} %pad_add_fusion.1.scal_ref, bf16[192,256]{1,0:T(8,128)(2,1)S(1)} %copy-done.2, bf16[4,384,512]{2,1,0:T(8,128)(2,1)S(1)} %all-to-all-done.2.enc_ref, bf16[4,256,512]{2,1,0:T(8,128)(2,1)S(1)} %all-to-all-done.3.other_ref, ...), custom_call_target="tpu_custom_call" | custom-call | tf_op jit(solution)/shard_map/pallas_call | solution.py:299
  143.5 1.9 collective-permute-start.5
  145.4 1.3 collective-permute-done.5.last_ref
  146.7 2.4 %shard_map.101 = (bf16[3,64,256]{2,1,0:T(8,128)(2,1)}, bf16[8,192,512]{2,1,0:T(8,128)(2,1)S(1)}) custom-call(bf16[3,64,256]{2,1,0:T(8,128)(2,1)S(1)} %get-tuple-element.18.att_ref, bf16[3,64,256]{2,1,0:T(8,128)(2,1)S(1)} %get-tuple-element.19.dq_ref, bf16[3,512]{1,0:T(4,128)(2,1)S(1)} %collective-permute-done.5.last_ref, ...), custom_call_target="tpu_custom_call" | custom-call | tf_op jit(solution)/shard_map/pallas_call | solution.py:325
  149.2 28.1 %all_to_all.36.in_ref = bf16[8,192,512]{2,1,0:T(8,128)(2,1)S(1)} all-to-all(bf16[8,192,512]{2,1,0:T(8,128)(2,1)S(1)} %get-tuple-element.21), channel_id=1, replica_groups=mesh['group'=64,'mp'=8] {'mp'}, dimensions={0} | all-to-all | bytes 3145728 | tf_op jit(solution)/shard_map/all_to_all | solution.py:341
  177.4 26.1 %all_to_all.37.in_ref = bf16[8,192,512]{2,1,0:T(8,128)(2,1)S(1)} all-to-all(bf16[8,192,512]{2,1,0:T(8,128)(2,1)S(1)} %shard_map.102), channel_id=1, replica_groups=mesh['group'=64,'mp'=8] {'mp'}, dimensions={0} | all-to-all | bytes 3145728 | tf_op jit(solution)/shard_map/all_to_all | solution.py:347
  203.5 1.7 shard_map.103
  (42 shorter events, 10.5 us)
Async XLA Ops:
  7.2 34.8 %copy-start.1 = (bf16[1024,512]{1,0:T(8,128)(2,1)S(1)}, bf16[1024,512]{1,0:T(8,128)(2,1)}, u32[]{:S(2)}) copy-start(bf16[1024,512]{1,0:T(8,128)(2,1)} %table_ref.1) | copy-start | bytes 3145732
  8.1 21.5 %collective-permute-start.1 = (bf16[64,768]{1,0:T(8,128)(2,1)S(1)}, bf16[64,768]{1,0:T(8,128)(2,1)S(1)}, u32[]{:S(2)}, u32[]{:S(2)}) collective-permute-start(bf16[64,768]{1,0:T(8,128)(2,1)S(1)} %pad_add_fusion), channel_id=1, source_target_pairs={{0,16},{8,24},{16,0},{24,8},{32,48},{40,56},{48,32},{56,40},{64,80... | collective-permute-start | bytes 294920 | tf_op jit(solution)/shard_map/ppermute | solution.py:223
  12.4 29.5 %all-to-all-start = ((s32[64,1,128]{2,1,0:T(1,128)}), s32[64,1,128]{2,1,0:T(1,128)S(1)}, u32[]{:S(2)}, u32[]{:S(2)}) async-start(s32[64,1,128]{2,1,0:T(1,128)} %bitcast.4), calls=%async_computation | async-start | bytes 65536 | tf_op jit(solution)/shard_map/all_to_all | solution.py:238
  29.5 101.9 %all-gather.2.cloned.1.call-start = ((), (), s32[]{:S(2)}) async-start(), calls=%async_computation.6 | async-start | bytes 6488064 | tf_op jit(solution)/shard_map/all_gather | solution.py:216
  42.8 6.4 %copy-start.5 = (bf16[3,64,256]{2,1,0:T(8,128)(2,1)S(1)}, bf16[3,64,256]{2,1,0:T(8,128)(2,1)}, u32[]{:S(2)}) copy-start(bf16[3,64,256]{2,1,0:T(8,128)(2,1)} %grad_ref.1) | copy-start | bytes 294916
  43.7 48.3 %all-to-all-start.1 = ((bf16[64,2,2304]{2,1,0:T(2,128)(2,1)}), bf16[64,2,2304]{2,1,0:T(2,128)(2,1)S(1)}, u32[]{:S(2)}, u32[]{:S(2)}) async-start(bf16[64,2,2304]{2,1,0:T(2,128)(2,1)} %reshape.24), calls=%async_computation.1 | async-start | bytes 1179648 | tf_op jit(solution)/shard_map/all_to_all | solution.py:246
  50.3 41.8 %collective-permute-start = (bf16[3,4352]{1,0:T(4,128)(2,1)S(1)}, bf16[3,4352]{1,0:T(4,128)(2,1)S(1)}, u32[]{:S(2)}, u32[]{:S(2)}) collective-permute-start(bf16[3,4352]{1,0:T(4,128)(2,1)S(1)} %pad_maximum_fusion.1), channel_id=1, source_target_pairs={{0,8},{8,16},{16,24},{24,32},{32,40},{40,48},{48,56},{56,64},{64,7... | collective-permute-start | bytes 78344 | tf_op jit(solution)/shard_map/ppermute | solution.py:225
  52.4 39.7 %collective-permute-start.2 = (s32[3,128]{1,0:T(4,128)S(1)}, s32[3,128]{1,0:T(4,128)S(1)}, u32[]{:S(2)}, u32[]{:S(2)}) collective-permute-start(s32[3,128]{1,0:T(4,128)S(1)} %get-tuple-element.14), channel_id=1, source_target_pairs={{0,8},{8,16},{16,24},{24,32},{32,40},{40,48},{48,56},{56,64},{64,7... | collective-permute-start | bytes 4616 | tf_op jit(solution)/shard_map/ppermute | solution.py:237
  92.1 1.8 copy-start.3
  93.9 23.8 %all-to-all-start.2 = ((bf16[4,384,512]{2,1,0:T(8,128)(2,1)}), bf16[4,384,512]{2,1,0:T(8,128)(2,1)S(1)}, u32[]{:S(2)}, u32[]{:S(2)}) async-start(bf16[4,384,512]{2,1,0:T(8,128)(2,1)} %get-tuple-element.16), calls=%async_computation.2 | async-start | bytes 3145728 | tf_op jit(solution)/shard_map/all_to_all | solution.py:253
  98.2 9.9 %collective-permute-start.3 = (bf16[256,512]{1,0:T(8,128)(2,1)S(1)}, bf16[256,512]{1,0:T(8,128)(2,1)S(1)}, u32[]{:S(2)}, u32[]{:S(2)}) collective-permute-start(bf16[256,512]{1,0:T(8,128)(2,1)S(1)} %get-tuple-element.17), channel_id=1, source_target_pairs={{0,1},{1,0},{2,3},{3,2},{4,5},{5,4},{6,7},{7,6},{8,9},{9,8},{10,11... | collective-permute-start | bytes 786440 | tf_op jit(solution)/shard_map/ppermute | solution.py:262
  108.1 1.0 copy-start
  109.1 15.4 %copy-start.6 = (s32[3,64]{1,0:T(4,128)S(1)}, s32[3,64]{1,0:T(4,128)}, u32[]{:S(2)}) copy-start(s32[3,64]{1,0:T(4,128)} %param.10) | copy-start | bytes 2308
  117.6 17.7 %all-to-all-start.3 = ((bf16[4,256,512]{2,1,0:T(8,128)(2,1)}), bf16[4,256,512]{2,1,0:T(8,128)(2,1)S(1)}, u32[]{:S(2)}, u32[]{:S(2)}) async-start(bf16[4,256,512]{2,1,0:T(8,128)(2,1)} %copy-done), calls=%async_computation.3 | async-start | bytes 2097152 | tf_op jit(solution)/shard_map/all_to_all | solution.py:253
  122.0 14.8 %collective-permute-start.4 = (bf16[4,128,512]{2,1,0:T(8,128)(2,1)}, bf16[4,128,512]{2,1,0:T(8,128)(2,1)S(1)}, u32[]{:S(2)}, u32[]{:S(2)}) collective-permute-start(bf16[4,128,512]{2,1,0:T(8,128)(2,1)} %slice.20), channel_id=1, source_target_pairs={{0,1},{1,0},{2,3},{3,2},{4,5},{5,4},{6,7},{7,6},{8,9},{9,8},{10,11... | collective-permute-start | bytes 1572872 | tf_op jit(solution)/shard_map/ppermute | solution.py:264
  124.8 11.9 %copy-start.4 = (bf16[3,4352]{1,0:T(4,128)(2,1)S(1)}, bf16[3,4352]{1,0:T(4,128)(2,1)}, u32[]{:S(2)}) copy-start(bf16[3,4352]{1,0:T(4,128)(2,1)} %copy-done.3) | copy-start | bytes 78340
  136.8 0.9 copy-start.2
  143.5 3.2 %collective-permute-start.5 = (bf16[3,512]{1,0:T(4,128)(2,1)S(1)}, bf16[3,512]{1,0:T(4,128)(2,1)S(1)}, u32[]{:S(2)}, u32[]{:S(2)}) collective-permute-start(bf16[3,512]{1,0:T(4,128)(2,1)S(1)} %pad_maximum_fusion.2), channel_id=1, source_target_pairs={{0,504},{8,0},{16,8},{24,16},{32,24},{40,32},{48,40},{56,48},{64,5... | collective-permute-start | bytes 9224 | tf_op jit(solution)/shard_map/ppermute | solution.py:321
Sparse Core Ops, SparseCore 0:
  42.1 89.2 all-gather.1

commit v8 on v4

--- a/solution.py
+++ b/solution.py
@@ -343,9 +343,9 @@
     part = lax.all_to_all(part, "mp", split_axis=0, concat_axis=0, tiled=True)
     token_grad = pl.pallas_call(
         join_kernel,
-        grid=(mp_size // 2,),
-        in_specs=[pl.BlockSpec((2, seqs * length, feats), lambda i: (i, 0, 0))],
-        out_specs=pl.BlockSpec((seqs * length, 2 * feats), lambda i: (0, i)),
+        grid=(2,),
+        in_specs=[pl.BlockSpec((mp_size // 2, seqs * length, feats), lambda i: (i, 0, 0))],
+        out_specs=pl.BlockSpec((seqs * length, width // 2), lambda i: (0, i)),
         out_shape=jax.ShapeDtypeStruct((seqs * length, width), BF),
         compiler_params=PARAMS,
     )(part)

time: 213 us -> 213 us (level)
  no operation moved by 1% of the time
where the time goes in v8:
time: 213 us; the launch traced here: 211 us
  waiting for transfers between devices  75.7 us (36%)
  blocking collectives  52.3 us (25%)
  starting transfers between devices  43.3 us (20%)
  Pallas kernels  15.1 us (7%)
  between operations  14.3 us (7%)
  local copies, waits for them, and re-layouts  7.47 us (4%)
  other arithmetic  2.73 us (1%)
    all_to_all x2, blocking collectives, local(): part = lax.all_to_all(part, 'mp', split_axis=0, concat_axis=0, tiled=True)  52.3 us
    all_to_all x1, waiting for transfers between devices, local(): lax.all_to_all(found, 'group', split_axis=0, concat_axis=0, tiled=True)  36.3 us
    all_to_all x1, starting transfers between devices, local(): lax.all_to_all(requests, 'group', split_axis=0, concat_axis=0, tiled=True)  17.1 us
    all_to_all x1, waiting for transfers between devices, local(): lax.all_to_all(requests, 'group', split_axis=0, concat_axis=0, tiled=True)  10.7 us
    all_gather x1, waiting for transfers between devices, round_z(): lax.all_gather(value, 'group', axis=0, tiled=True, axis_index_groups=groups)  9.9 us
    ppermute x1, waiting for transfers between devices, local(): single = lax.ppermute(single, 'mp', [(m, m ^ 1) for m in range(mp_size)])  9.79 us
    all_to_all x2, starting transfers between devices, round_x(): lax.all_to_all(value, 'mp', split_axis=0, concat_axis=0, tiled=True, axis...  7.88 us
    all_to_all x2, waiting for transfers between devices, round_x(): lax.all_to_all(value, 'mp', split_axis=0, concat_axis=0, tiled=True, axis...  7.62 us
  transfers between devices with their start and end apart: 10, of which 7 were waited for; matrix products, arithmetic and copies ran while one was open for 2% of the time, Pallas kernels for 4%

profile of v8, /device:TPU:24, one launch (start us, length us, event | category | flops | bytes accessed | tf_op | source)
XLA Modules:
  0.0 210.9 jit_solution(17587791191052713185)
XLA Ops:
  8.1 2.6 %collective-permute-start.2 = (bf16[64,768]{1,0:T(8,128)(2,1)S(1)}, bf16[64,768]{1,0:T(8,128)(2,1)S(1)}, u32[]{:S(2)}, u32[]{:S(2)}) collective-permute-start(bf16[64,768]{1,0:T(8,128)(2,1)S(1)} %pad_add_fusion), channel_id=1, source_target_pairs={{0,16},{8,24},{16,0},{24,8},{32,48},{40,56},{48,32},{56,40},{64,80... | collective-permute-start | bytes 294920 | tf_op jit(solution)/shard_map/ppermute | solution.py:219
  12.4 17.1 %all-to-all-start = ((s32[64,1,128]{2,1,0:T(1,128)}), s32[64,1,128]{2,1,0:T(1,128)S(1)}, u32[]{:S(2)}, u32[]{:S(2)}) async-start(s32[64,1,128]{2,1,0:T(1,128)} %bitcast.2), calls=%async_computation | async-start | bytes 65536 | tf_op jit(solution)/shard_map/all_to_all | solution.py:234
  31.2 10.7 %all-to-all-done = s32[64,1,128]{2,1,0:T(1,128)S(1)} async-done(((s32[64,1,128]{2,1,0:T(1,128)}), s32[64,1,128]{2,1,0:T(1,128)S(1)}, u32[]{:S(2)}, u32[]{:S(2)}) %all-to-all-start) | async-done | bytes 32800 | tf_op jit(solution)/shard_map/all_to_all | solution.py:234
  43.7 5.5 %all-to-all-start.1 = ((bf16[64,2,2304]{2,1,0:T(2,128)(2,1)}), bf16[64,2,2304]{2,1,0:T(2,128)(2,1)S(1)}, u32[]{:S(2)}, u32[]{:S(2)}) async-start(bf16[64,2,2304]{2,1,0:T(2,128)(2,1)} %reshape.24), calls=%async_computation.1 | async-start | bytes 1179648 | tf_op jit(solution)/shard_map/all_to_all | solution.py:242
  50.3 2.1 collective-permute-start.1
  52.4 3.4 %collective-permute-start = (s32[3,128]{1,0:T(4,128)S(1)}, s32[3,128]{1,0:T(4,128)S(1)}, u32[]{:S(2)}, u32[]{:S(2)}) collective-permute-start(s32[3,128]{1,0:T(4,128)S(1)} %get-tuple-element.14), channel_id=1, source_target_pairs={{0,8},{8,16},{16,24},{24,32},{32,40},{40,48},{48,56},{56,64},{64,7... | collective-permute-start | bytes 4616 | tf_op jit(solution)/shard_map/ppermute | solution.py:233
  55.7 36.3 %all-to-all-done.1 = bf16[64,2,2304]{2,1,0:T(2,128)(2,1)S(1)} async-done(((bf16[64,2,2304]{2,1,0:T(2,128)(2,1)}), bf16[64,2,2304]{2,1,0:T(2,128)(2,1)S(1)}, u32[]{:S(2)}, u32[]{:S(2)}) %all-to-all-start.1) | async-done | bytes 589856 | tf_op jit(solution)/shard_map/all_to_all | solution.py:242
  92.1 1.8 shard_map.97
  93.9 4.3 %all-to-all-start.2 = ((bf16[4,384,512]{2,1,0:T(8,128)(2,1)}), bf16[4,384,512]{2,1,0:T(8,128)(2,1)S(1)}, u32[]{:S(2)}, u32[]{:S(2)}) async-start(bf16[4,384,512]{2,1,0:T(8,128)(2,1)} %get-tuple-element.17), calls=%async_computation.2 | async-start | bytes 3145728 | tf_op jit(solution)/shard_map/all_to_all | solution.py:249
  98.2 2.9 %collective-permute-start.3 = (bf16[384,512]{1,0:T(8,128)(2,1)S(1)}, bf16[384,512]{1,0:T(8,128)(2,1)S(1)}, u32[]{:S(2)}, u32[]{:S(2)}) collective-permute-start(bf16[384,512]{1,0:T(8,128)(2,1)S(1)} %get-tuple-element.21), channel_id=1, source_target_pairs={{0,1},{1,0},{2,3},{3,2},{4,5},{5,4},{6,7},{7,6},{8,9},{9,8},{10,11... | collective-permute-start | bytes 1179656 | tf_op jit(solution)/shard_map/ppermute | solution.py:258
  101.1 9.8 %collective-permute-done.3.in_ref = bf16[384,512]{1,0:T(8,128)(2,1)S(1)} collective-permute-done((bf16[384,512]{1,0:T(8,128)(2,1)S(1)}, bf16[384,512]{1,0:T(8,128)(2,1)S(1)}, u32[]{:S(2)}, u32[]{:S(2)}) %collective-permute-start.3) | collective-permute-done | bytes 393248 | tf_op jit(solution)/shard_map/ppermute | solution.py:258
  112.1 5.5 %all-to-all-done.2.enc_ref = bf16[4,384,512]{2,1,0:T(8,128)(2,1)S(1)} async-done(((bf16[4,384,512]{2,1,0:T(8,128)(2,1)}), bf16[4,384,512]{2,1,0:T(8,128)(2,1)S(1)}, u32[]{:S(2)}, u32[]{:S(2)}) %all-to-all-start.2) | async-done | bytes 1572896 | tf_op jit(solution)/shard_map/all_to_all | solution.py:249
  117.6 3.6 %all-to-all-start.3 = ((bf16[4,384,512]{2,1,0:T(8,128)(2,1)}), bf16[4,384,512]{2,1,0:T(8,128)(2,1)S(1)}, u32[]{:S(2)}, u32[]{:S(2)}) async-start(bf16[4,384,512]{2,1,0:T(8,128)(2,1)} %copy-done), calls=%async_computation.3 | async-start | bytes 3145728 | tf_op jit(solution)/shard_map/all_to_all | solution.py:249
  121.5 9.9 %all-gather.2.cloned.1.call-done.w_ref.next_w_ref.q_w_ref = bf16[4096,768]{1,0:T(8,128)(2,1)} async-done(((bf16[128,768]{1,0:T(8,128)(2,1)}), bf16[4096,768]{1,0:T(8,128)(2,1)}) %all-gather.2.cloned.1.call-update) | async-done | bytes 6291472 | tf_op jit(solution)/shard_map/all_gather | solution.py:212
  131.4 1.4 copy-done.1
  132.8 3.9 %shard_map.98 = (f32[384,512]{1,0:T(8,128)S(1)}, bf16[192,256]{1,0:T(8,128)(2,1)S(1)}) custom-call(s32[4]{0:T(128)S(1)} %pad_add_fusion.1.scal_ref, bf16[4,384,512]{2,1,0:T(8,128)(2,1)S(1)} %all-to-all-done.2.enc_ref, bf16[4096,768]{1,0:T(8,128)(2,1)} %all-gather.2.cloned.1.call-done.w_ref.next_w_ref.q_w_ref, ...), custom_call_target="tpu_custom_call" | custom-call | tf_op jit(solution)/shard_map/pallas_call | solution.py:271
  137.5 2.1 %all-to-all-done.3.enc_ref = bf16[4,384,512]{2,1,0:T(8,128)(2,1)S(1)} async-done(((bf16[4,384,512]{2,1,0:T(8,128)(2,1)}), bf16[4,384,512]{2,1,0:T(8,128)(2,1)S(1)}, u32[]{:S(2)}, u32[]{:S(2)}) %all-to-all-start.3) | async-done | bytes 1572896 | tf_op jit(solution)/shard_map/all_to_all | solution.py:249
  140.8 3.7 %shard_map.100 = (bf16[3,64,256]{2,1,0:T(8,128)(2,1)S(1)}, bf16[3,64,256]{2,1,0:T(8,128)(2,1)S(1)}) custom-call(s32[4]{0:T(128)S(1)} %pad_add_fusion.1.scal_ref, f32[384,512]{1,0:T(8,128)S(1)} %copy-done.4, bf16[192,256]{1,0:T(8,128)(2,1)S(1)} %get-tuple-element.20.q_ref, bf16[4,384,512]{2,1,0:T(8,128)(2,1)S(1)} %all-to-all-done.3.enc_ref, ...), custom_call_target="tpu_custom_call" | custom-call | tf_op jit(solution)/shard_map/pallas_call | solution.py:296
  144.7 1.9 collective-permute-start.4
  146.6 1.3 collective-permute-done.4.last_ref
  147.9 2.4 %shard_map.101 = (bf16[3,64,256]{2,1,0:T(8,128)(2,1)}, bf16[8,192,512]{2,1,0:T(8,128)(2,1)S(1)}) custom-call(bf16[3,64,256]{2,1,0:T(8,128)(2,1)S(1)} %get-tuple-element.22.att_ref, bf16[3,64,256]{2,1,0:T(8,128)(2,1)S(1)} %get-tuple-element.23.dq_ref, bf16[3,512]{1,0:T(4,128)(2,1)S(1)} %collective-permute-done.4.last_ref, ...), custom_call_target="tpu_custom_call" | custom-call | tf_op jit(solution)/shard_map/pallas_call | solution.py:321
  150.4 25.8 %all_to_all.36.in_ref = bf16[8,192,512]{2,1,0:T(8,128)(2,1)S(1)} all-to-all(bf16[8,192,512]{2,1,0:T(8,128)(2,1)S(1)} %get-tuple-element.25), channel_id=1, replica_groups=mesh['group'=64,'mp'=8] {'mp'}, dimensions={0} | all-to-all | bytes 3145728 | tf_op jit(solution)/shard_map/all_to_all | solution.py:337
  176.4 26.5 %all_to_all.37.in_ref = bf16[8,192,512]{2,1,0:T(8,128)(2,1)S(1)} all-to-all(bf16[8,192,512]{2,1,0:T(8,128)(2,1)S(1)} %shard_map.102), channel_id=1, replica_groups=mesh['group'=64,'mp'=8] {'mp'}, dimensions={0} | all-to-all | bytes 3145728 | tf_op jit(solution)/shard_map/all_to_all | solution.py:343
  202.9 1.2 shard_map.103
  (39 shorter events, 11.0 us)
Async XLA Ops:
  7.2 34.8 %copy-start.2 = (bf16[1024,512]{1,0:T(8,128)(2,1)S(1)}, bf16[1024,512]{1,0:T(8,128)(2,1)}, u32[]{:S(2)}) copy-start(bf16[1024,512]{1,0:T(8,128)(2,1)} %table_ref.1) | copy-start | bytes 3145732
  8.1 21.5 %collective-permute-start.2 = (bf16[64,768]{1,0:T(8,128)(2,1)S(1)}, bf16[64,768]{1,0:T(8,128)(2,1)S(1)}, u32[]{:S(2)}, u32[]{:S(2)}) collective-permute-start(bf16[64,768]{1,0:T(8,128)(2,1)S(1)} %pad_add_fusion), channel_id=1, source_target_pairs={{0,16},{8,24},{16,0},{24,8},{32,48},{40,56},{48,32},{56,40},{64,80... | collective-permute-start | bytes 294920 | tf_op jit(solution)/shard_map/ppermute | solution.py:219
  12.4 29.5 %all-to-all-start = ((s32[64,1,128]{2,1,0:T(1,128)}), s32[64,1,128]{2,1,0:T(1,128)S(1)}, u32[]{:S(2)}, u32[]{:S(2)}) async-start(s32[64,1,128]{2,1,0:T(1,128)} %bitcast.2), calls=%async_computation | async-start | bytes 65536 | tf_op jit(solution)/shard_map/all_to_all | solution.py:234
  29.5 101.9 %all-gather.2.cloned.1.call-start = ((), (), s32[]{:S(2)}) async-start(), calls=%async_computation.6 | async-start | bytes 6488064 | tf_op jit(solution)/shard_map/all_gather | solution.py:212
  42.8 6.4 %copy-start.5 = (bf16[3,64,256]{2,1,0:T(8,128)(2,1)S(1)}, bf16[3,64,256]{2,1,0:T(8,128)(2,1)}, u32[]{:S(2)}) copy-start(bf16[3,64,256]{2,1,0:T(8,128)(2,1)} %grad_ref.1) | copy-start | bytes 294916
  43.7 48.3 %all-to-all-start.1 = ((bf16[64,2,2304]{2,1,0:T(2,128)(2,1)}), bf16[64,2,2304]{2,1,0:T(2,128)(2,1)S(1)}, u32[]{:S(2)}, u32[]{:S(2)}) async-start(bf16[64,2,2304]{2,1,0:T(2,128)(2,1)} %reshape.24), calls=%async_computation.1 | async-start | bytes 1179648 | tf_op jit(solution)/shard_map/all_to_all | solution.py:242
  50.3 41.8 %collective-permute-start.1 = (bf16[3,4352]{1,0:T(4,128)(2,1)S(1)}, bf16[3,4352]{1,0:T(4,128)(2,1)S(1)}, u32[]{:S(2)}, u32[]{:S(2)}) collective-permute-start(bf16[3,4352]{1,0:T(4,128)(2,1)S(1)} %pad_maximum_fusion.1), channel_id=1, source_target_pairs={{0,8},{8,16},{16,24},{24,32},{32,40},{40,48},{48,56},{56,64},{64,7... | collective-permute-start | bytes 78344 | tf_op jit(solution)/shard_map/ppermute | solution.py:221
  52.4 39.7 %collective-permute-start = (s32[3,128]{1,0:T(4,128)S(1)}, s32[3,128]{1,0:T(4,128)S(1)}, u32[]{:S(2)}, u32[]{:S(2)}) collective-permute-start(s32[3,128]{1,0:T(4,128)S(1)} %get-tuple-element.14), channel_id=1, source_target_pairs={{0,8},{8,16},{16,24},{24,32},{32,40},{40,48},{48,56},{56,64},{64,7... | collective-permute-start | bytes 4616 | tf_op jit(solution)/shard_map/ppermute | solution.py:233
  93.9 23.8 %all-to-all-start.2 = ((bf16[4,384,512]{2,1,0:T(8,128)(2,1)}), bf16[4,384,512]{2,1,0:T(8,128)(2,1)S(1)}, u32[]{:S(2)}, u32[]{:S(2)}) async-start(bf16[4,384,512]{2,1,0:T(8,128)(2,1)} %get-tuple-element.17), calls=%async_computation.2 | async-start | bytes 3145728 | tf_op jit(solution)/shard_map/all_to_all | solution.py:249
  98.2 12.7 %collective-permute-start.3 = (bf16[384,512]{1,0:T(8,128)(2,1)S(1)}, bf16[384,512]{1,0:T(8,128)(2,1)S(1)}, u32[]{:S(2)}, u32[]{:S(2)}) collective-permute-start(bf16[384,512]{1,0:T(8,128)(2,1)S(1)} %get-tuple-element.21), channel_id=1, source_target_pairs={{0,1},{1,0},{2,3},{3,2},{4,5},{5,4},{6,7},{7,6},{8,9},{9,8},{10,11... | collective-permute-start | bytes 1179656 | tf_op jit(solution)/shard_map/ppermute | solution.py:258
  111.0 1.1 copy-start
  112.1 9.1 %copy-start.6 = (s32[3,64]{1,0:T(4,128)S(1)}, s32[3,64]{1,0:T(4,128)}, u32[]{:S(2)}) copy-start(s32[3,64]{1,0:T(4,128)} %param.10) | copy-start | bytes 2308
  117.6 22.1 %all-to-all-start.3 = ((bf16[4,384,512]{2,1,0:T(8,128)(2,1)}), bf16[4,384,512]{2,1,0:T(8,128)(2,1)S(1)}, u32[]{:S(2)}, u32[]{:S(2)}) async-start(bf16[4,384,512]{2,1,0:T(8,128)(2,1)} %copy-done), calls=%async_computation.3 | async-start | bytes 3145728 | tf_op jit(solution)/shard_map/all_to_all | solution.py:249
  131.4 1.4 copy-start.1
  136.7 0.9 copy-start.3
  139.7 1.1 copy-start.4
  144.7 3.2 %collective-permute-start.4 = (bf16[3,512]{1,0:T(4,128)(2,1)S(1)}, bf16[3,512]{1,0:T(4,128)(2,1)S(1)}, u32[]{:S(2)}, u32[]{:S(2)}) collective-permute-start(bf16[3,512]{1,0:T(4,128)(2,1)S(1)} %pad_maximum_fusion.2), channel_id=1, source_target_pairs={{0,504},{8,0},{16,8},{24,16},{32,24},{40,32},{48,40},{56,48},{64,5... | collective-permute-start | bytes 9224 | tf_op jit(solution)/shard_map/ppermute | solution.py:317
Sparse Core Ops, SparseCore 0:
  42.1 89.2 all-gather.1
